TPU v7x, 32 devices: a whole 2x2x4 slice. The times are simulated.
32 devices in a mesh: row: 4 (over y, x), col: 8 (over z, core).
Axes of the slice: x: 2, y: 2, z: 4, core: 2. Of those that a mesh axis runs over, the one named last changes fastest.
Arguments:
- inv_known: float32 [512, 512], P('row', 'col'), as said below
- pattern: int32 [8, 8], P('row', 'col'), may hold values from 0 to 1, as said below
- factor: float32 [512, 2, 512], P(('row', 'col')), may hold values from -0.25 to 0.25
- listed: int32 [512, 2], P(('row', 'col')), may hold values 0 or 1
- diag_inverse: float32 [512, 2, 512], P('col'), may hold values from -6 to 6
Outputs:
- inverse_columns: float32 [512, 2, 512], P('col', None, 'row')
- schur: float32 [512, 2, 512], P('col')
Inputs may be any that keep to these rules, and one draw needn't show every extreme that they name: `inv_known`: symmetric. `pattern`: symmetric; every diagonal tile is present.
All inputs are finite; a program needn't handle non-finite values. No bound on the sum of `listed` on one device may be relied on, other than what follows from the above.
Results may differ from a plain program's by a relative error of at most 0.0001.
Values sent between devices are 32-bit elements; how exact they have to be, the bound alone decides.
No kernel may reach another device: no remote copies, remote signals or barrier semaphores. Data moves between devices by JAX's collectives and lax.ppermute only.
A program may use at most 64 MiB of HBM per device.

v0:
```python
import jax
import jax.numpy as jnp
from jax import lax
from jax.sharding import PartitionSpec as P


def supernode_pass(present, masked, listed_f, diag_part, ratio):
    row_block, row_listed = (
        lax.all_gather(masked, "col", axis=0, tiled=True),
        lax.all_gather(listed_f, "col", axis=0, tiled=True),
    )
    held = lax.psum_scatter(
        jnp.einsum("ij,ika->jka", present, row_block, precision=lax.Precision.HIGHEST),
        "row",
        scatter_dimension=0,
        tiled=True,
    )
    count_row = lax.axis_size("row")
    count_col = lax.axis_size("col")
    local_rows = held.shape[0]
    nodes = held.shape[1]
    narrow = held.shape[2] // count_col
    by_column = lax.all_to_all(held[None], "col", split_axis=3, concat_axis=0, tiled=True)
    grouped = by_column.reshape(count_row, 1, ratio, local_rows, nodes, narrow)
    moved = lax.all_to_all(grouped, "row", split_axis=0, concat_axis=1, tiled=True)
    ordered = jnp.transpose(moved[0], (1, 0, 2, 3, 4)).reshape(
        ratio * count_row * local_rows, nodes, narrow
    )
    summed = jnp.transpose(ordered, (2, 1, 0))
    columns = -summed * jnp.transpose(row_listed)[None, :, :]
    update = jnp.einsum("akj,jkb->akb", columns, row_block, precision=lax.Precision.HIGHEST)
    schur = diag_part - lax.psum(update, "row")
    return (columns, schur)


def local(inv_known, pattern, factor, listed, diag_inverse):
    tile = inv_known.shape[0] // pattern.shape[0]
    flags = pattern.astype(jnp.float32)
    spread = jnp.repeat(jnp.repeat(flags, tile, axis=0), tile, axis=1)
    present = inv_known * spread
    listed_f = listed.astype(jnp.float32)
    masked = factor * listed_f[:, :, None]
    ratio = lax.axis_size("col") // lax.axis_size("row")
    columns, schur = supernode_pass(present, masked, listed_f, diag_inverse, ratio)
    return (columns, schur)


def solution(mesh):
    in_specs = (
        P("row", "col"),
        P("row", "col"),
        P(("row", "col"), None, None),
        P(("row", "col"), None),
        P("col", None, None),
    )
    out_specs = (P("col", None, "row"), P("col", None, None))
    return jax.shard_map(local, mesh=mesh, in_specs=in_specs, out_specs=out_specs, check_vma=False)
```

profile of v0, /device:TPU:0, one launch (start us, length us, event | category | flops | bytes accessed | tf_op | source)
XLA Modules:
  0.0 133.8 jit_solution(2223798226949201739)
XLA Ops:
  7.2 0.0 reduce-scatter.2.cloned.1.call-start
  7.2 0.7 convert_bitcast_fusion
  7.9 0.1 broadcast_in_dim.11
  7.9 0.0 copy-start.2
  7.9 0.1 broadcast_in_dim.12
  8.0 0.6 copy-done.2
  8.6 0.9 copy_multiply_fusion
  9.5 0.0 copy-start.1
  9.5 16.7 %all_gather.6 = f32[128,2,512]{2,0,1:T(8,128)S(1)} all-gather(f32[16,2,512]{2,0,1:T(8,128)S(1)} %copy_multiply_fusion), channel_id=1, replica_groups=mesh['row'=4,'col'=8] {'col'}, dimensions={0}, use_global_device_ids=true | all-gather | bytes 589824 | tf_op jit(solution)/shard_map/all_gather | solution.py:9
  26.2 0.0 copy-done.1
  26.2 1.1 fusion
  27.4 0.0 reduce-scatter.2.cloned.1.call-update
  27.4 25.3 %reduce-scatter.2.cloned.1.call-done = f32[16,2,512]{2,0,1:T(8,128)} async-done(((f32[64,2,512]{2,0,1:T(8,128)}), f32[16,2,512]{2,0,1:T(8,128)}) %reduce-scatter.2.cloned.1.call-update) | async-done | bytes 65552 | tf_op jit(solution)/shard_map/reduce_scatter | solution.py:12
  52.7 1.1 copy.35
  53.8 0.7 reshape.34
  54.5 10.3 %all_to_all.24 = f32[8,1,2048]{2,1,0:T(1,128)S(1)} all-to-all(f32[8,1,2048]{2,1,0:T(1,128)S(1)} %reshape.34), channel_id=1, replica_groups=mesh['row'=4,'col'=8] {'col'}, dimensions={0} | all-to-all | bytes 131072 | tf_op jit(solution)/shard_map/all_to_all | solution.py:23
  64.8 0.5 broadcast.7
  65.3 0.8 reduce
  66.1 0.7 reshape.35
  66.8 0.2 copy.46
  67.0 0.8 reshape.36
  67.8 3.3 %all-to-all-start.1 = ((f32[4,1,4096]{2,1,0:T(1,128)}), f32[4,1,4096]{2,1,0:T(1,128)S(1)}, u32[]{:S(2)}, u32[]{:S(2)}) async-start(f32[4,1,4096]{2,1,0:T(1,128)} %reshape.36), calls=%async_computation.2 | async-start | bytes 131072 | tf_op jit(solution)/shard_map/all_to_all | solution.py:25
  71.1 0.0 all-reduce.2.cloned.1.call-start
  71.1 9.3 %all-gather = f32[8,16,2]{1,2,0:T(2,128)S(1)} all-gather(f32[1,16,2]{1,2,0:T(2,128)S(1)} %get-tuple-element.12), channel_id=1, replica_groups=mesh['row'=4,'col'=8] {'col'}, dimensions={0}, use_global_device_ids=true | all-gather | bytes 1152 | tf_op jit(solution)/shard_map/all_gather | solution.py:10
  80.4 0.1 reshape.28
  80.5 0.0 all-to-all-done.1
  80.5 0.8 reduce.1
  81.3 0.1 reshape.37
  81.5 0.1 bitcast_multiply_fusion
  81.6 1.2 convolution_bitcast_fusion
  82.7 0.0 copy-start
  82.7 0.0 all-reduce.2.cloned.1.call-update
  82.8 0.7 copy.42
  83.5 41.5 %all-reduce.2.cloned.1.call-done = f32[64,2,512]{2,0,1:T(8,128)} async-done(((f32[64,2,512]{2,0,1:T(8,128)}), f32[64,2,512]{2,0,1:T(8,128)}) %all-reduce.2.cloned.1.call-update) | async-done | bytes 262160 | tf_op jit(solution)/shard_map/psum | solution.py:32
  125.0 0.0 copy-done
  125.0 1.0 copy_subtract_fusion
  126.0 0.9 copy.43
  (4 shorter events, 0.0 us)
Async XLA Ops:
  7.2 45.5 %reduce-scatter.2.cloned.1.call-start = ((), (), s32[]{:S(2)}) async-start(), calls=%async_computation.3 | async-start | bytes 327680 | tf_op jit(solution)/shard_map/reduce_scatter | solution.py:12
  7.9 0.7 copy-start.2
  9.5 16.7 %copy-start.1 = (f32[128,64]{0,1:T(8,128)S(1)}, f32[128,64]{0,1:T(8,128)}, u32[]{:S(2)}) copy-start(f32[128,64]{0,1:T(8,128)} %param.5) | copy-start | bytes 98308
  67.8 12.7 %all-to-all-start.1 = ((f32[4,1,4096]{2,1,0:T(1,128)}), f32[4,1,4096]{2,1,0:T(1,128)S(1)}, u32[]{:S(2)}, u32[]{:S(2)}) async-start(f32[4,1,4096]{2,1,0:T(1,128)} %reshape.36), calls=%async_computation.2 | async-start | bytes 131072 | tf_op jit(solution)/shard_map/all_to_all | solution.py:25
  71.1 53.9 %all-reduce.2.cloned.1.call-start = ((), (), s32[]{:S(2)}) async-start(), calls=%async_computation.4 | async-start | bytes 524288 | tf_op jit(solution)/shard_map/psum | solution.py:32
  82.7 42.3 %copy-start = (f32[64,2,512]{2,1,0:T(2,128)S(1)}, f32[64,2,512]{2,1,0:T(2,128)}, u32[]{:S(2)}) copy-start(f32[64,2,512]{2,1,0:T(2,128)} %param.9) | copy-start | bytes 786436
Sparse Core Ops, SparseCore 0:
  27.5 25.1 reduce-scatter.1
  82.9 42.0 all-reduce.1
where the time goes:
time: 134 us
  waiting for transfers between devices  66.9 us (50%)
  blocking collectives  36.3 us (27%)
  between operations  14.1 us (11%)
  local copies, waits for them, and re-layouts  6.55 us (5%)
  other arithmetic  4.31 us (3%)
  starting transfers between devices  3.36 us (3%)
  matrix products  2.3 us (2%)
    psum x1, waiting for transfers between devices, supernode_pass(): schur = diag_part - lax.psum(update, 'row')  41.5 us
    reduce_scatter x1, waiting for transfers between devices, supernode_pass(): lax.psum_scatter(jnp.einsum('ij,ika->jka', present, row_block, precision=...  25.3 us
    all_gather x1, blocking collectives, supernode_pass(): lax.all_gather(masked, 'col', axis=0, tiled=True)  16.7 us
    all_to_all x1, blocking collectives, supernode_pass(): lax.all_to_all(held[None], 'col', split_axis=3, concat_axis=0, tiled=True)  10.3 us
    all_gather x1, blocking collectives, supernode_pass(): lax.all_gather(listed_f, 'col', axis=0, tiled=True)  9.28 us
    unnamed x13, local copies, waits for them, and re-layouts  4.63 us
    all_to_all x1, starting transfers between devices, supernode_pass(): lax.all_to_all(grouped, 'row', split_axis=0, concat_axis=1, tiled=True)  3.28 us
  transfers between devices with their start and end apart: 3, of which 2 were waited for; matrix products, arithmetic and copies ran while one was open for 1% of the time, Pallas kernels for 0%

commit v1 on v0

--- a/solution.py
+++ b/solution.py
@@ -1,7 +1,23 @@
+import functools
+
 import jax
 import jax.numpy as jnp
 from jax import lax
+from jax.experimental import pallas as pl
+from jax.experimental.pallas import tpu as pltpu
 from jax.sharding import PartitionSpec as P
+
+LANES = 128
+CORES = 2
+AXES = ("row", "col")
+VMEM = pl.BlockSpec(memory_space=pltpu.VMEM)
+SMEM = pl.BlockSpec(memory_space=pltpu.SMEM)
+
+
+def exact(a, b, contract):
+    return lax.dot_general(
+        a, b, (contract, ((), ())), precision=lax.Precision.HIGHEST, preferred_element_type=jnp.float32
+    )
 
 
 def supernode_pass(present, masked, listed_f, diag_part, ratio):
@@ -33,7 +49,7 @@
     return (columns, schur)
 
 
-def local(inv_known, pattern, factor, listed, diag_inverse):
+def general(inv_known, pattern, factor, listed, diag_inverse):
     tile = inv_known.shape[0] // pattern.shape[0]
     flags = pattern.astype(jnp.float32)
     spread = jnp.repeat(jnp.repeat(flags, tile, axis=0), tile, axis=1)
@@ -41,8 +57,197 @@
     listed_f = listed.astype(jnp.float32)
     masked = factor * listed_f[:, :, None]
     ratio = lax.axis_size("col") // lax.axis_size("row")
-    columns, schur = supernode_pass(present, masked, listed_f, diag_inverse, ratio)
-    return (columns, schur)
+    return supernode_pass(present, masked, listed_f, diag_inverse, ratio)
+
+
+class Sizes:
+    def __init__(self, inv_known, pattern, factor, diag_inverse):
+        self.n_row = lax.axis_size("row")
+        self.n_col = lax.axis_size("col")
+        self.n_z = self.n_col // CORES
+        self.own = factor.shape[0]
+        self.nodes = factor.shape[1]
+        self.width = factor.shape[2]
+        self.tiles = self.width // LANES
+        self.slots = self.tiles * self.nodes
+        self.rows_r = inv_known.shape[0]
+        self.rows_c = inv_known.shape[1]
+        self.wide = diag_inverse.shape[0]
+        self.pattern = pattern.shape
+        self.span = self.n_col * self.own
+        self.m_rows = self.own * self.slots
+        self.bulk = self.m_rows + self.rows_c + 8
+        self.small = self.nodes * self.own
+        self.total = self.n_row * self.rows_r
+
+    def fits(self):
+        def power(n):
+            return n > 0 and n & (n - 1) == 0
+
+        return (
+            self.n_col % CORES == 0
+            and power(self.n_row)
+            and power(self.n_z)
+            and self.n_row > 1
+            and self.wide * CORES == LANES
+            and self.rows_r == LANES
+            and self.span == LANES
+            and self.width % LANES == 0
+            and self.slots % 8 == 0
+            and self.own % 8 == 0
+            and self.rows_c % 8 == 0
+            and self.nodes <= 8
+        )
+
+
+def spot():
+    r = lax.axis_index("row")
+    c = lax.axis_index("col")
+    return r, lax.div(c, CORES), lax.rem(c, CORES)
+
+
+def pack_kernel(n, factor, listed, inv_t, pattern, bulk, *smalls):
+    r, z, core = spot()
+    col = z * CORES + core
+    line = lax.broadcasted_iota(jnp.int32, (n.slots, LANES), 0)
+    head = lax.broadcasted_iota(jnp.int32, (8, LANES), 0)
+    lane8 = lax.broadcasted_iota(jnp.int32, (8, LANES), 1)
+    flags = jnp.zeros((8, LANES), jnp.float32)
+    for m in range(n.own):
+        keep = jnp.zeros((n.slots, LANES), jnp.float32)
+        for k in range(n.nodes):
+            value = listed[m, k].astype(jnp.float32)
+            keep = jnp.where(lax.rem(line, n.nodes) == k, value, keep)
+            flags = jnp.where((head == k) & (lane8 == col * n.own + m), value, flags)
+        part = pl.ds(m * n.slots, n.slots)
+        bulk[part, :] = factor[part, :] * keep
+    bulk[pl.ds(n.m_rows + n.rows_c, 8), :] = flags
+    high = n.rows_r // n.pattern[0]
+    deep = n.rows_c // n.pattern[1]
+    lane = lax.broadcasted_iota(jnp.int32, (deep, LANES), 1)
+    for q in range(n.pattern[1]):
+        keep = jnp.zeros((deep, LANES), jnp.float32)
+        for p in range(n.pattern[0]):
+            keep = jnp.where(lax.div(lane, high) == p, pattern[p, q].astype(jnp.float32), keep)
+        bulk[pl.ds(n.m_rows + q * deep, deep), :] = inv_t[pl.ds(q * deep, deep), :] * keep
+    for k in range(n.nodes):
+        loads = [bulk[pl.ds(t * n.nodes + k, n.own, stride=n.slots), :] for t in range(n.tiles)]
+        for s, small in enumerate(smalls):
+            want = z ^ s
+            piece = loads[0]
+            for t in range(1, n.tiles):
+                piece = jnp.where(want == t, loads[t], piece)
+            small[pl.ds(k * n.own, n.own), :] = piece
+
+
+def stack_kernel(n, *refs):
+    out = refs[-1]
+    for s, ref in enumerate(refs[:-1]):
+        out[pl.ds(s * n.small, n.small), :] = ref[...]
+
+
+def work_kernel(n, *refs):
+    smalls = refs[: CORES * n.n_row]
+    bulks = refs[CORES * n.n_row : CORES * (n.n_row + n.n_z)]
+    columns, update, m_all, m_row, p_t, x_t = refs[CORES * (n.n_row + n.n_z) :]
+    r, z, core = spot()
+    mask = jnp.zeros((8, LANES), jnp.float32)
+    for q in range(CORES):
+        for s in range(n.n_z):
+            ref = bulks[q * n.n_z + s]
+            c = (z ^ s) * CORES + (core ^ q)
+            m_row[pl.ds(c * n.m_rows, n.m_rows), :] = ref[pl.ds(0, n.m_rows), :]
+            p_t[pl.ds(c * n.rows_c, n.rows_c), :] = ref[pl.ds(n.m_rows, n.rows_c), :]
+            mask += ref[pl.ds(n.m_rows + n.rows_c, 8), :]
+        for d in range(n.n_row):
+            ref = smalls[q * n.n_row + d]
+            for s in range(n.n_z):
+                c = (z ^ s) * CORES + (core ^ q)
+                at = (r ^ d) * n.span + c * n.own
+                for k in range(n.nodes):
+                    m_all[k, pl.ds(at, n.own), :] = ref[pl.ds(s * n.small + k * n.own, n.own), :]
+    for k in range(n.nodes):
+        x_t[k] = exact(m_all[k], p_t[...], ((0,), (0,)))
+        part = -x_t[k, pl.ds(core * n.wide, n.wide), :] * mask[k : k + 1, :]
+        columns[pl.ds(k, n.wide, stride=n.nodes), :] = part
+        for t in range(n.tiles):
+            side = m_row[pl.ds(t * n.nodes + k, n.rows_r, stride=n.slots), :]
+            update[pl.ds(t * n.nodes + k, n.wide, stride=n.slots), :] = exact(part, side, ((1,), (0,)))
+
+
+def fast(n, inv_known, pattern, factor, listed, diag_inverse):
+    def shape(*dims):
+        return jax.ShapeDtypeStruct(dims, jnp.float32)
+
+    def route(array, change):
+        pairs = []
+        for r in range(n.n_row):
+            for z in range(n.n_z):
+                for core in range(CORES):
+                    r2, z2, core2 = change(r, z, core)
+                    pairs.append(((r * n.n_z + z) * CORES + core, (r2 * n.n_z + z2) * CORES + core2))
+        return lax.ppermute(array, AXES, pairs)
+
+    def over_z(array, s):
+        return route(array, lambda r, z, core: (r, z ^ s, core))
+
+    def over_row(array, d):
+        return route(array, lambda r, z, core: (r ^ d, z, core))
+
+    def over_core(array):
+        return route(array, lambda r, z, core: (r, z, core ^ 1))
+
+    steps = [1 << i for i in range(n.n_row.bit_length() - 1)]
+
+    def over_pair(array, i):
+        return route(array, lambda r, z, core: (r ^ (steps[i] if core == 0 else steps[-1 - i]), z, core))
+
+    def view(array):
+        lead = array.shape[0]
+        split = array.reshape(lead, n.nodes, n.tiles, LANES)
+        return jnp.transpose(split, (0, 2, 1, 3)).reshape(lead * n.slots, LANES)
+
+    bulk, *smalls = pl.pallas_call(
+        functools.partial(pack_kernel, n),
+        in_specs=[VMEM, SMEM, VMEM, SMEM],
+        out_specs=[VMEM] * (1 + n.n_z),
+        out_shape=[shape(n.bulk, LANES)] + [shape(n.small, LANES)] * n.n_z,
+    )(view(factor), listed, inv_known.T, pattern)
+
+    smalls = [smalls[0]] + [over_z(smalls[s], s) for s in range(1, n.n_z)]
+    bulks = [bulk] + [over_z(bulk, s) for s in range(1, n.n_z)]
+    small = pl.pallas_call(
+        functools.partial(stack_kernel, n),
+        in_specs=[VMEM] * n.n_z,
+        out_specs=VMEM,
+        out_shape=shape(n.n_z * n.small, LANES),
+    )(*smalls)
+    spread = [small] + [over_row(small, d) for d in range(1, n.n_row)]
+    other_bulks = [over_core(b) for b in bulks]
+    other_spread = [over_core(b) for b in spread]
+    columns, update = pl.pallas_call(
+        functools.partial(work_kernel, n),
+        in_specs=[VMEM] * (CORES * (n.n_row + n.n_z)),
+        out_specs=[VMEM] * 2,
+        out_shape=[shape(n.wide * n.nodes, LANES), shape(n.wide * n.slots, LANES)],
+        scratch_shapes=[
+            pltpu.VMEM((n.nodes, n.total, LANES), jnp.float32),
+            pltpu.VMEM((n.span * n.slots, LANES), jnp.float32),
+            pltpu.VMEM((n.total, LANES), jnp.float32),
+            pltpu.VMEM((n.nodes, LANES, LANES), jnp.float32),
+        ],
+    )(*spread, *other_spread, *bulks, *other_bulks)
+    for i in range(len(steps)):
+        update = update + over_pair(update, i)
+    schur = view(diag_inverse) - update
+    schur = jnp.transpose(schur.reshape(n.wide, n.tiles, n.nodes, LANES), (0, 2, 1, 3))
+    return columns.reshape(n.wide, n.nodes, LANES), schur.reshape(n.wide, n.nodes, n.width)
+
+
+def local(inv_known, pattern, factor, listed, diag_inverse):
+    n = Sizes(inv_known, pattern, factor, diag_inverse)
+    plan = functools.partial(fast, n) if n.fits() else general
+    return plan(inv_known, pattern, factor, listed, diag_inverse)
 
 
 def solution(mesh):

time: 134 us -> 52.5 us (0.39)
  waiting for transfers between devices: 66.9 us -> 22.1 us
  blocking collectives: 36.3 us -> 0 us
  starting transfers between devices: 3.36 us -> 17.1 us
  between operations: 14.1 us -> 0.79 us
  Pallas kernels: 0 us -> 6.54 us
  local copies, waits for them, and re-layouts: 6.55 us -> 3.88 us
  other arithmetic: 4.31 us -> 1.73 us
  matrix products: 2.3 us -> 0 us
    psum x1 -> x0, waiting for transfers between devices: 41.5 us -> none  [supernode_pass(): schur = diag_part - lax.psum(update, 'row')]
    all_gather x2 -> x0, blocking collectives: 26 us -> none  [the longest x1 16.7 us: supernode_pass(): lax.all_gather(masked, 'col', axis=0, tiled=True)]
    reduce_scatter x1 -> x0, waiting for transfers between devices: 25.3 us -> none  [supernode_pass(): lax.psum_scatter(jnp.einsum('ij,ika->jka', present, row_block, precision=...]
    ppermute x0 -> x19, waiting for transfers between devices: none -> 22.1 us  [route(): return lax.ppermute(array, AXES, pairs)]
    ppermute x0 -> x19, starting transfers between devices: none -> 17.1 us  [route(): return lax.ppermute(array, AXES, pairs)]
    all_to_all x1 -> x0, blocking collectives: 10.3 us -> none  [supernode_pass(): lax.all_to_all(held[None], 'col', split_axis=3, concat_axis=0, tiled=True)]
    pallas_call x0 -> x3, Pallas kernels: none -> 6.54 us  [the longest x1 3.48 us: fast(): pl.pallas_call(functools.partial(work_kernel, n), in_specs=[VMEM] * (CORE...]
    all_to_all x1 -> x0, starting transfers between devices: 3.28 us -> none  [supernode_pass(): lax.all_to_all(grouped, 'row', split_axis=0, concat_axis=1, tiled=True)]
  transfers between devices with their start and end apart: 3 -> 19, of which waited for: 2 -> 8; matrix products, arithmetic and copies ran while one was open for 1% -> 0% of each run, Pallas kernels for 0% -> 0%
where the time goes in v1:
time: 52.5 us; the launch traced here: 52.2 us
  waiting for transfers between devices  22.1 us (42%)
  starting transfers between devices  17.1 us (33%)
  Pallas kernels  6.54 us (12%)
  local copies, waits for them, and re-layouts  3.88 us (7%)
  other arithmetic  1.73 us (3%)
  between operations  0.79 us (2%)
    ppermute x19, waiting for transfers between devices, route(): return lax.ppermute(array, AXES, pairs)  22.1 us
    ppermute x19, starting transfers between devices, route(): return lax.ppermute(array, AXES, pairs)  17.1 us
    unnamed x42, local copies, waits for them, and re-layouts  3.88 us
    pallas_call x1, Pallas kernels, fast(): pl.pallas_call(functools.partial(work_kernel, n), in_specs=[VMEM] * (CORE...  3.48 us
    pallas_call x1, Pallas kernels, fast(): pl.pallas_call(functools.partial(pack_kernel, n), in_specs=[VMEM, SMEM, V...  1.67 us
    pallas_call x1, Pallas kernels, fast(): pl.pallas_call(functools.partial(stack_kernel, n), in_specs=[VMEM] * n.n_...  1.4 us
  transfers between devices with their start and end apart: 19, of which 8 were waited for; matrix products, arithmetic and copies ran while one was open for 0% of the time, Pallas kernels for 0%

profile of v1, /device:TPU:0, one launch (start us, length us, event | category | flops | bytes accessed | tf_op | source)
XLA Modules:
  0.0 52.2 jit_solution(4752130298947354719)
XLA Ops:
  0.6 0.0 copy-start.19
  0.6 1.3 %copy.9.pattern = s32[2,1]{1,0:T(2,128)} copy(s32[2,1]{0,1:T(1,128)} %param.6) | data formatting | bytes 16 | tf_op args[1]
  2.0 0.7 %copy.8.listed = s32[16,2]{1,0:T(8,128)} copy(s32[16,2]{0,1:T(2,128)S(1)} %copy-done.19) | data formatting | bytes 256 | tf_op args[3]
  2.6 1.7 %shard_map.68 = (f32[200,128]{1,0:T(8,128)}, f32[32,128]{1,0:T(8,128)}, f32[32,128]{1,0:T(8,128)}, f32[32,128]{1,0:T(8,128)}, f32[32,128]{1,0:T(8,128)}) custom-call(f32[128,128]{1,0:T(8,128)} %bitcast.19, s32[16,2]{1,0:T(8,128)} %copy.8.listed, f32[64,128]{1,0:T(8,128)} %bitcast.20, s32[2,1]{1,0:T(2,128)} %copy.9.pattern), custom_call_target="tpu_custom_call" | custom-call | tf_op jit(solution)/shard_map/pallas_call | solution.py:210
  4.3 3.0 %collective-permute-start = (f32[32,128]{1,0:T(8,128)}, f32[32,128]{1,0:T(8,128)S(1)}, u32[]{:S(2)}, u32[]{:S(2)}) collective-permute-start(f32[32,128]{1,0:T(8,128)} %get-tuple-element.10), channel_id=1, source_target_pairs={{0,2},{1,3},{2,0},{3,1},{4,6},{5,7},{6,4},{7,5},{8,10},{9,11},{10,... | collective-permute-start | bytes 49160 | tf_op jit(solution)/shard_map/ppermute | solution.py:189
  7.3 2.6 %collective-permute-start.1 = (f32[32,128]{1,0:T(8,128)}, f32[32,128]{1,0:T(8,128)S(1)}, u32[]{:S(2)}, u32[]{:S(2)}) collective-permute-start(f32[32,128]{1,0:T(8,128)} %get-tuple-element.11), channel_id=1, source_target_pairs={{0,4},{1,5},{2,6},{3,7},{4,0},{5,1},{6,2},{7,3},{8,12},{9,13},{10,... | collective-permute-start | bytes 49160 | tf_op jit(solution)/shard_map/ppermute | solution.py:189
  9.9 0.0 collective-permute-start.2
  9.9 0.0 collective-permute-done.refs_1_
  9.9 2.3 %collective-permute-done.1.refs_2_ = f32[32,128]{1,0:T(8,128)S(1)} collective-permute-done((f32[32,128]{1,0:T(8,128)}, f32[32,128]{1,0:T(8,128)S(1)}, u32[]{:S(2)}, u32[]{:S(2)}) %collective-permute-start.1) | collective-permute-done | bytes 16416 | tf_op jit(solution)/shard_map/ppermute | solution.py:189
  12.3 3.4 %collective-permute-done.2.refs_3_ = f32[32,128]{1,0:T(8,128)S(1)} collective-permute-done((f32[32,128]{1,0:T(8,128)}, f32[32,128]{1,0:T(8,128)S(1)}, u32[]{:S(2)}, u32[]{:S(2)}) %collective-permute-start.2) | collective-permute-done | bytes 16416 | tf_op jit(solution)/shard_map/ppermute | solution.py:189
  15.7 0.6 %copy-done.18 = f32[32,128]{1,0:T(8,128)} copy-done((f32[32,128]{1,0:T(8,128)}, f32[32,128]{1,0:T(8,128)S(1)}, u32[]{:S(2)}) %copy-start.18) | copy-done | bytes 16408
  16.3 1.4 %shard_map.69.refs_0_ = f32[128,128]{1,0:T(8,128)} custom-call(f32[32,128]{1,0:T(8,128)} %get-tuple-element.9.refs_0_, f32[32,128]{1,0:T(8,128)} %copy-done.16, f32[32,128]{1,0:T(8,128)} %copy-done.17, f32[32,128]{1,0:T(8,128)} %copy-done.18), custom_call_target="tpu_custom_call" | custom-call | tf_op jit(solution)/shard_map/pallas_call | solution.py:219
  17.7 0.0 collective-permute-start.6
  17.7 2.4 %collective-permute-start.5 = (f32[128,128]{1,0:T(8,128)}, f32[128,128]{1,0:T(8,128)S(1)}, u32[]{:S(2)}, u32[]{:S(2)}) collective-permute-start(f32[128,128]{1,0:T(8,128)} %shard_map.69.refs_0_), channel_id=1, source_target_pairs={{0,24},{1,25},{2,26},{3,27},{4,28},{5,29},{6,30},{7,31},{8,16},{9,... | collective-permute-start | bytes 196616 | tf_op jit(solution)/shard_map/ppermute | solution.py:189
  20.1 0.5 collective-permute-start.4
  20.6 0.2 collective-permute-start.12
  20.8 0.0 collective-permute-start.11
  20.8 0.0 collective-permute-done.6.refs_4_
  20.9 4.2 %collective-permute-start.10 = (f32[200,128]{1,0:T(8,128)S(1)}, f32[200,128]{1,0:T(8,128)S(1)}, u32[]{:S(2)}, u32[]{:S(2)}) collective-permute-start(f32[200,128]{1,0:T(8,128)S(1)} %copy-done.1), channel_id=1, source_target_pairs={{0,2},{1,3},{2,0},{3,1},{4,6},{5,7},{6,4},{7,5},{8,10},{9,11},{10,... | collective-permute-start | bytes 307208 | tf_op jit(solution)/shard_map/ppermute | solution.py:189
  25.0 0.0 collective-permute-done.5.refs_3_
  25.0 0.5 %collective-permute-start.3 = (f32[128,128]{1,0:T(8,128)}, f32[128,128]{1,0:T(8,128)S(1)}, u32[]{:S(2)}, u32[]{:S(2)}) collective-permute-start(f32[128,128]{1,0:T(8,128)} %shard_map.69.refs_0_), channel_id=1, source_target_pairs={{0,8},{1,9},{2,10},{3,11},{4,12},{5,13},{6,14},{7,15},{8,0},{9,1},... | collective-permute-start | bytes 196616 | tf_op jit(solution)/shard_map/ppermute | solution.py:189
  25.6 0.0 collective-permute-done.4.refs_2_
  25.6 0.0 collective-permute-start.13
  25.6 3.9 %collective-permute-done.3.refs_1_ = f32[128,128]{1,0:T(8,128)S(1)} collective-permute-done((f32[128,128]{1,0:T(8,128)}, f32[128,128]{1,0:T(8,128)S(1)}, u32[]{:S(2)}, u32[]{:S(2)}) %collective-permute-start.3) | collective-permute-done | bytes 65568 | tf_op jit(solution)/shard_map/ppermute | solution.py:189
  29.5 0.0 collective-permute-start.9
  29.5 0.0 collective-permute-done.12.refs_11_
  29.5 0.0 copy-start.2
  29.5 0.5 collective-permute-start.16
  30.0 0.6 %collective-permute-done.11.refs_10_ = f32[200,128]{1,0:T(8,128)S(1)} collective-permute-done((f32[200,128]{1,0:T(8,128)S(1)}, f32[200,128]{1,0:T(8,128)S(1)}, u32[]{:S(2)}, u32[]{:S(2)}) %collective-permute-start.11) | collective-permute-done | bytes 102432 | tf_op jit(solution)/shard_map/ppermute | solution.py:189
  30.7 0.0 collective-permute-start.15
  30.7 0.0 collective-permute-done.10.refs_9_
  30.7 0.0 copy-start.4
  30.7 0.5 collective-permute-start.14
  31.2 0.0 collective-permute-done.13.refs_12_
  31.2 0.1 collective-permute-start.8
  31.3 0.0 collective-permute-done.9.refs_7_
  31.3 0.4 collective-permute-start.7
  31.7 0.7 %collective-permute-done.8.refs_6_ = f32[128,128]{1,0:T(8,128)S(1)} collective-permute-done((f32[128,128]{1,0:T(8,128)S(1)}, f32[128,128]{1,0:T(8,128)S(1)}, u32[]{:S(2)}, u32[]{:S(2)}) %collective-permute-start.8) | collective-permute-done | bytes 65568 | tf_op jit(solution)/shard_map/ppermute | solution.py:189
  32.4 0.2 collective-permute-done.7.refs_5_
  32.6 0.0 collective-permute-done.16.refs_15_
  32.6 0.0 collective-permute-done.15.refs_14_
  32.6 0.0 collective-permute-done.14.refs_13_
  32.6 0.0 copy-done.9
  32.6 0.0 copy-done.10
  32.6 0.0 copy-done.11
  32.7 0.0 copy-done.12
  32.7 0.0 copy-done.2
  32.7 0.0 copy-done.3
  32.7 0.0 copy-done.4
  32.7 0.0 copy-done.5
  32.7 0.0 copy-done.13
  32.7 0.3 copy-done.14
  33.1 0.2 copy-done.15
  33.2 0.0 copy-done.6
  33.3 0.1 copy-done.7
  33.3 0.6 %copy-done.8 = f32[200,128]{1,0:T(8,128)} copy-done((f32[200,128]{1,0:T(8,128)}, f32[200,128]{1,0:T(8,128)S(1)}, u32[]{:S(2)}) %copy-start.8) | copy-done | bytes 102424
  34.0 3.5 %shard_map.70 = (f32[128,128]{1,0:T(8,128)}, f32[512,128]{1,0:T(8,128)}) custom-call(f32[128,128]{1,0:T(8,128)} %shard_map.69.refs_0_, f32[128,128]{1,0:T(8,128)} %copy-done.12, f32[128,128]{1,0:T(8,128)} %copy-done.11, f32[128,128]{1,0:T(8,128)} %copy-done.10, f32[128,128]{1,0:T(8,128)} %copy-done.9, f32[128,128]{1,0:T(8,128)} %copy-done.15, ...), custom_call_target="tpu_custom_call" | custom-call | tf_op jit(solution)/shard_map/pallas_call | solution.py:228
  37.4 0.5 %collective-permute-start.17 = (f32[512,128]{1,0:T(8,128)}, f32[512,128]{1,0:T(8,128)S(1)}, u32[]{:S(2)}, u32[]{:S(2)}) collective-permute-start(f32[512,128]{1,0:T(8,128)} %get-tuple-element.15), channel_id=1, source_target_pairs={{0,8},{1,17},{2,10},{3,19},{4,12},{5,21},{6,14},{7,23},{8,0},{9,25... | collective-permute-start | bytes 786440 | tf_op jit(solution)/shard_map/ppermute | solution.py:189
  38.0 6.1 %collective-permute-done.17 = f32[512,128]{1,0:T(8,128)S(1)} collective-permute-done((f32[512,128]{1,0:T(8,128)}, f32[512,128]{1,0:T(8,128)S(1)}, u32[]{:S(2)}, u32[]{:S(2)}) %collective-permute-start.17) | collective-permute-done | bytes 262176 | tf_op jit(solution)/shard_map/ppermute | solution.py:189
  44.0 1.0 %add.6 = f32[512,128]{1,0:T(8,128)S(1)} add(f32[512,128]{1,0:T(8,128)} %get-tuple-element.15, f32[512,128]{1,0:T(8,128)S(1)} %collective-permute-done.17) | non-fusion elementwise | flops 65536 | bytes 786432 | tf_op jit(solution)/shard_map/add | solution.py:241
  45.0 1.6 %collective-permute-start.18 = (f32[512,128]{1,0:T(8,128)S(1)}, f32[512,128]{1,0:T(8,128)S(1)}, u32[]{:S(2)}, u32[]{:S(2)}) collective-permute-start(f32[512,128]{1,0:T(8,128)S(1)} %add.6), channel_id=1, source_target_pairs={{0,16},{1,9},{2,18},{3,11},{4,20},{5,13},{6,22},{7,15},{8,24},{9,1... | collective-permute-start | bytes 786440 | tf_op jit(solution)/shard_map/ppermute | solution.py:189
  46.6 4.9 %collective-permute-done.18 = f32[512,128]{1,0:T(8,128)S(1)} collective-permute-done((f32[512,128]{1,0:T(8,128)S(1)}, f32[512,128]{1,0:T(8,128)S(1)}, u32[]{:S(2)}, u32[]{:S(2)}) %collective-permute-start.18) | collective-permute-done | bytes 262176 | tf_op jit(solution)/shard_map/ppermute | solution.py:189
  51.5 0.0 copy-done
  51.5 0.7 %add_subtract_fusion = f32[512,128]{1,0:T(8,128)} fusion(f32[512,128]{1,0:T(8,128)S(1)} %bitcast.17, f32[512,128]{1,0:T(8,128)S(1)} %add.6, f32[512,128]{1,0:T(8,128)S(1)} %collective-permute-done.18), kind=kLoop, calls=%fused_computation | loop fusion | flops 131072 | bytes 1048576 | tf_op jit(solution)/shard_map/sub | solution.py:242
  (21 shorter events, 0.0 us)
Async XLA Ops:
  0.6 1.3 %copy-start.19 = (s32[16,2]{0,1:T(2,128)S(1)}, s32[16,2]{0,1:T(2,128)}, u32[]{:S(2)}) copy-start(s32[16,2]{0,1:T(2,128)} %param.8) | copy-start | bytes 388
  4.3 16.3 %copy-start.1 = (f32[200,128]{1,0:T(8,128)S(1)}, f32[200,128]{1,0:T(8,128)}, u32[]{:S(2)}) copy-start(f32[200,128]{1,0:T(8,128)} %get-tuple-element.13.refs_8_) | copy-start | bytes 307204
  4.3 5.6 %collective-permute-start = (f32[32,128]{1,0:T(8,128)}, f32[32,128]{1,0:T(8,128)S(1)}, u32[]{:S(2)}, u32[]{:S(2)}) collective-permute-start(f32[32,128]{1,0:T(8,128)} %get-tuple-element.10), channel_id=1, source_target_pairs={{0,2},{1,3},{2,0},{3,1},{4,6},{5,7},{6,4},{7,5},{8,10},{9,11},{10,... | collective-permute-start | bytes 49160 | tf_op jit(solution)/shard_map/ppermute | solution.py:189
  7.3 4.9 %collective-permute-start.1 = (f32[32,128]{1,0:T(8,128)}, f32[32,128]{1,0:T(8,128)S(1)}, u32[]{:S(2)}, u32[]{:S(2)}) collective-permute-start(f32[32,128]{1,0:T(8,128)} %get-tuple-element.11), channel_id=1, source_target_pairs={{0,4},{1,5},{2,6},{3,7},{4,0},{5,1},{6,2},{7,3},{8,12},{9,13},{10,... | collective-permute-start | bytes 49160 | tf_op jit(solution)/shard_map/ppermute | solution.py:189
  9.9 5.7 %collective-permute-start.2 = (f32[32,128]{1,0:T(8,128)}, f32[32,128]{1,0:T(8,128)S(1)}, u32[]{:S(2)}, u32[]{:S(2)}) collective-permute-start(f32[32,128]{1,0:T(8,128)} %get-tuple-element.12), channel_id=1, source_target_pairs={{0,6},{1,7},{2,4},{3,5},{4,2},{5,3},{6,0},{7,1},{8,14},{9,15},{10,... | collective-permute-start | bytes 49160 | tf_op jit(solution)/shard_map/ppermute | solution.py:189
  9.9 5.7 %copy-start.16 = (f32[32,128]{1,0:T(8,128)}, f32[32,128]{1,0:T(8,128)S(1)}, u32[]{:S(2)}) copy-start(f32[32,128]{1,0:T(8,128)S(1)} %collective-permute-done.refs_1_) | copy-start | bytes 49156
  12.3 3.4 %copy-start.17 = (f32[32,128]{1,0:T(8,128)}, f32[32,128]{1,0:T(8,128)S(1)}, u32[]{:S(2)}) copy-start(f32[32,128]{1,0:T(8,128)S(1)} %collective-permute-done.1.refs_2_) | copy-start | bytes 49156
  15.7 0.6 %copy-start.18 = (f32[32,128]{1,0:T(8,128)}, f32[32,128]{1,0:T(8,128)S(1)}, u32[]{:S(2)}) copy-start(f32[32,128]{1,0:T(8,128)S(1)} %collective-permute-done.2.refs_3_) | copy-start | bytes 49156
  17.7 3.2 %collective-permute-start.6 = (f32[128,128]{1,0:T(8,128)}, f32[128,128]{1,0:T(8,128)S(1)}, u32[]{:S(2)}, u32[]{:S(2)}) collective-permute-start(f32[128,128]{1,0:T(8,128)} %shard_map.69.refs_0_), channel_id=1, source_target_pairs={{0,1},{1,0},{2,3},{3,2},{4,5},{5,4},{6,7},{7,6},{8,9},{9,8},{10,11... | collective-permute-start | bytes 196616 | tf_op jit(solution)/shard_map/ppermute | solution.py:189
  17.7 7.4 %collective-permute-start.5 = (f32[128,128]{1,0:T(8,128)}, f32[128,128]{1,0:T(8,128)S(1)}, u32[]{:S(2)}, u32[]{:S(2)}) collective-permute-start(f32[128,128]{1,0:T(8,128)} %shard_map.69.refs_0_), channel_id=1, source_target_pairs={{0,24},{1,25},{2,26},{3,27},{4,28},{5,29},{6,30},{7,31},{8,16},{9,... | collective-permute-start | bytes 196616 | tf_op jit(solution)/shard_map/ppermute | solution.py:189
  20.1 5.4 %collective-permute-start.4 = (f32[128,128]{1,0:T(8,128)}, f32[128,128]{1,0:T(8,128)S(1)}, u32[]{:S(2)}, u32[]{:S(2)}) collective-permute-start(f32[128,128]{1,0:T(8,128)} %shard_map.69.refs_0_), channel_id=1, source_target_pairs={{0,16},{1,17},{2,18},{3,19},{4,20},{5,21},{6,22},{7,23},{8,24},{9,... | collective-permute-start | bytes 196616 | tf_op jit(solution)/shard_map/ppermute | solution.py:189
  20.6 8.9 %collective-permute-start.12 = (f32[200,128]{1,0:T(8,128)S(1)}, f32[200,128]{1,0:T(8,128)S(1)}, u32[]{:S(2)}, u32[]{:S(2)}) collective-permute-start(f32[200,128]{1,0:T(8,128)S(1)} %copy-done.1), channel_id=1, source_target_pairs={{0,6},{1,7},{2,4},{3,5},{4,2},{5,3},{6,0},{7,1},{8,14},{9,15},{10,... | collective-permute-start | bytes 307208 | tf_op jit(solution)/shard_map/ppermute | solution.py:189
  20.8 9.8 %collective-permute-start.11 = (f32[200,128]{1,0:T(8,128)S(1)}, f32[200,128]{1,0:T(8,128)S(1)}, u32[]{:S(2)}, u32[]{:S(2)}) collective-permute-start(f32[200,128]{1,0:T(8,128)S(1)} %copy-done.1), channel_id=1, source_target_pairs={{0,4},{1,5},{2,6},{3,7},{4,0},{5,1},{6,2},{7,3},{8,12},{9,13},{10,... | collective-permute-start | bytes 307208 | tf_op jit(solution)/shard_map/ppermute | solution.py:189
  20.9 11.8 %copy-start.9 = (f32[128,128]{1,0:T(8,128)}, f32[128,128]{1,0:T(8,128)S(1)}, u32[]{:S(2)}) copy-start(f32[128,128]{1,0:T(8,128)S(1)} %collective-permute-done.6.refs_4_) | copy-start | bytes 196612
  20.9 9.8 %collective-permute-start.10 = (f32[200,128]{1,0:T(8,128)S(1)}, f32[200,128]{1,0:T(8,128)S(1)}, u32[]{:S(2)}, u32[]{:S(2)}) collective-permute-start(f32[200,128]{1,0:T(8,128)S(1)} %copy-done.1), channel_id=1, source_target_pairs={{0,2},{1,3},{2,0},{3,1},{4,6},{5,7},{6,4},{7,5},{8,10},{9,11},{10,... | collective-permute-start | bytes 307208 | tf_op jit(solution)/shard_map/ppermute | solution.py:189
  25.0 7.6 %copy-start.10 = (f32[128,128]{1,0:T(8,128)}, f32[128,128]{1,0:T(8,128)S(1)}, u32[]{:S(2)}) copy-start(f32[128,128]{1,0:T(8,128)S(1)} %collective-permute-done.5.refs_3_) | copy-start | bytes 196612
  25.0 4.5 %collective-permute-start.3 = (f32[128,128]{1,0:T(8,128)}, f32[128,128]{1,0:T(8,128)S(1)}, u32[]{:S(2)}, u32[]{:S(2)}) collective-permute-start(f32[128,128]{1,0:T(8,128)} %shard_map.69.refs_0_), channel_id=1, source_target_pairs={{0,8},{1,9},{2,10},{3,11},{4,12},{5,13},{6,14},{7,15},{8,0},{9,1},... | collective-permute-start | bytes 196616 | tf_op jit(solution)/shard_map/ppermute | solution.py:189
  25.6 7.1 %copy-start.11 = (f32[128,128]{1,0:T(8,128)}, f32[128,128]{1,0:T(8,128)S(1)}, u32[]{:S(2)}) copy-start(f32[128,128]{1,0:T(8,128)S(1)} %collective-permute-done.4.refs_2_) | copy-start | bytes 196612
  25.6 5.6 %collective-permute-start.13 = (f32[200,128]{1,0:T(8,128)S(1)}, f32[200,128]{1,0:T(8,128)S(1)}, u32[]{:S(2)}, u32[]{:S(2)}) collective-permute-start(f32[200,128]{1,0:T(8,128)S(1)} %copy-done.1), channel_id=1, source_target_pairs={{0,1},{1,0},{2,3},{3,2},{4,5},{5,4},{6,7},{7,6},{8,9},{9,8},{10,11... | collective-permute-start | bytes 307208 | tf_op jit(solution)/shard_map/ppermute | solution.py:189
  29.5 3.2 %copy-start.12 = (f32[128,128]{1,0:T(8,128)}, f32[128,128]{1,0:T(8,128)S(1)}, u32[]{:S(2)}) copy-start(f32[128,128]{1,0:T(8,128)S(1)} %collective-permute-done.3.refs_1_) | copy-start | bytes 196612
  29.5 1.8 %collective-permute-start.9 = (f32[128,128]{1,0:T(8,128)S(1)}, f32[128,128]{1,0:T(8,128)S(1)}, u32[]{:S(2)}, u32[]{:S(2)}) collective-permute-start(f32[128,128]{1,0:T(8,128)S(1)} %collective-permute-done.5.refs_3_), channel_id=1, source_target_pairs={{0,1},{1,0},{2,3},{3,2},{4,5},{5,4},{6,7},{7,6},{8,9},{9,8},{10,11... | collective-permute-start | bytes 196616 | tf_op jit(solution)/shard_map/ppermute | solution.py:189
  29.5 3.2 %copy-start.2 = (f32[200,128]{1,0:T(8,128)}, f32[200,128]{1,0:T(8,128)S(1)}, u32[]{:S(2)}) copy-start(f32[200,128]{1,0:T(8,128)S(1)} %collective-permute-done.12.refs_11_) | copy-start | bytes 307204
  29.5 3.1 %collective-permute-start.16 = (f32[200,128]{1,0:T(8,128)S(1)}, f32[200,128]{1,0:T(8,128)S(1)}, u32[]{:S(2)}, u32[]{:S(2)}) collective-permute-start(f32[200,128]{1,0:T(8,128)S(1)} %collective-permute-done.12.refs_11_), channel_id=1, source_target_pairs={{0,1},{1,0},{2,3},{3,2},{4,5},{5,4},{6,7},{7,6},{8,9},{9,8},{10,11... | collective-permute-start | bytes 307208 | tf_op jit(solution)/shard_map/ppermute | solution.py:189
  30.7 2.0 %copy-start.3 = (f32[200,128]{1,0:T(8,128)}, f32[200,128]{1,0:T(8,128)S(1)}, u32[]{:S(2)}) copy-start(f32[200,128]{1,0:T(8,128)S(1)} %collective-permute-done.11.refs_10_) | copy-start | bytes 307204
  30.7 2.0 %collective-permute-start.15 = (f32[200,128]{1,0:T(8,128)S(1)}, f32[200,128]{1,0:T(8,128)S(1)}, u32[]{:S(2)}, u32[]{:S(2)}) collective-permute-start(f32[200,128]{1,0:T(8,128)S(1)} %collective-permute-done.11.refs_10_), channel_id=1, source_target_pairs={{0,1},{1,0},{2,3},{3,2},{4,5},{5,4},{6,7},{7,6},{8,9},{9,8},{10,11... | collective-permute-start | bytes 307208 | tf_op jit(solution)/shard_map/ppermute | solution.py:189
  30.7 2.0 %copy-start.4 = (f32[200,128]{1,0:T(8,128)}, f32[200,128]{1,0:T(8,128)S(1)}, u32[]{:S(2)}) copy-start(f32[200,128]{1,0:T(8,128)S(1)} %collective-permute-done.10.refs_9_) | copy-start | bytes 307204
  30.7 1.9 %collective-permute-start.14 = (f32[200,128]{1,0:T(8,128)S(1)}, f32[200,128]{1,0:T(8,128)S(1)}, u32[]{:S(2)}, u32[]{:S(2)}) collective-permute-start(f32[200,128]{1,0:T(8,128)S(1)} %collective-permute-done.10.refs_9_), channel_id=1, source_target_pairs={{0,1},{1,0},{2,3},{3,2},{4,5},{5,4},{6,7},{7,6},{8,9},{9,8},{10,11... | collective-permute-start | bytes 307208 | tf_op jit(solution)/shard_map/ppermute | solution.py:189
  31.2 1.5 %copy-start.5 = (f32[200,128]{1,0:T(8,128)}, f32[200,128]{1,0:T(8,128)S(1)}, u32[]{:S(2)}) copy-start(f32[200,128]{1,0:T(8,128)S(1)} %collective-permute-done.13.refs_12_) | copy-start | bytes 307204
  31.2 1.3 %collective-permute-start.8 = (f32[128,128]{1,0:T(8,128)S(1)}, f32[128,128]{1,0:T(8,128)S(1)}, u32[]{:S(2)}, u32[]{:S(2)}) collective-permute-start(f32[128,128]{1,0:T(8,128)S(1)} %collective-permute-done.4.refs_2_), channel_id=1, source_target_pairs={{0,1},{1,0},{2,3},{3,2},{4,5},{5,4},{6,7},{7,6},{8,9},{9,8},{10,11... | collective-permute-start | bytes 196616 | tf_op jit(solution)/shard_map/ppermute | solution.py:189
  31.3 1.4 %copy-start.13 = (f32[128,128]{1,0:T(8,128)}, f32[128,128]{1,0:T(8,128)S(1)}, u32[]{:S(2)}) copy-start(f32[128,128]{1,0:T(8,128)S(1)} %collective-permute-done.9.refs_7_) | copy-start | bytes 196612
  31.3 1.3 %collective-permute-start.7 = (f32[128,128]{1,0:T(8,128)S(1)}, f32[128,128]{1,0:T(8,128)S(1)}, u32[]{:S(2)}, u32[]{:S(2)}) collective-permute-start(f32[128,128]{1,0:T(8,128)S(1)} %collective-permute-done.3.refs_1_), channel_id=1, source_target_pairs={{0,1},{1,0},{2,3},{3,2},{4,5},{5,4},{6,7},{7,6},{8,9},{9,8},{10,11... | collective-permute-start | bytes 196616 | tf_op jit(solution)/shard_map/ppermute | solution.py:189
  32.4 0.6 %copy-start.14 = (f32[128,128]{1,0:T(8,128)}, f32[128,128]{1,0:T(8,128)S(1)}, u32[]{:S(2)}) copy-start(f32[128,128]{1,0:T(8,128)S(1)} %collective-permute-done.8.refs_6_) | copy-start | bytes 196612
  32.6 0.6 %copy-start.15 = (f32[128,128]{1,0:T(8,128)}, f32[128,128]{1,0:T(8,128)S(1)}, u32[]{:S(2)}) copy-start(f32[128,128]{1,0:T(8,128)S(1)} %collective-permute-done.7.refs_5_) | copy-start | bytes 196612
  32.6 0.7 %copy-start.6 = (f32[200,128]{1,0:T(8,128)}, f32[200,128]{1,0:T(8,128)S(1)}, u32[]{:S(2)}) copy-start(f32[200,128]{1,0:T(8,128)S(1)} %collective-permute-done.16.refs_15_) | copy-start | bytes 307204
  32.6 0.7 %copy-start.7 = (f32[200,128]{1,0:T(8,128)}, f32[200,128]{1,0:T(8,128)S(1)}, u32[]{:S(2)}) copy-start(f32[200,128]{1,0:T(8,128)S(1)} %collective-permute-done.15.refs_14_) | copy-start | bytes 307204
  33.3 0.6 %copy-start.8 = (f32[200,128]{1,0:T(8,128)}, f32[200,128]{1,0:T(8,128)S(1)}, u32[]{:S(2)}) copy-start(f32[200,128]{1,0:T(8,128)S(1)} %collective-permute-done.14.refs_13_) | copy-start | bytes 307204
  37.4 14.0 %copy-start = (f32[64,2,512]{2,1,0:T(2,128)S(1)}, f32[64,2,512]{2,1,0:T(2,128)}, u32[]{:S(2)}) copy-start(f32[64,2,512]{2,1,0:T(2,128)} %param.9) | copy-start | bytes 786436
  37.4 6.6 %collective-permute-start.17 = (f32[512,128]{1,0:T(8,128)}, f32[512,128]{1,0:T(8,128)S(1)}, u32[]{:S(2)}, u32[]{:S(2)}) collective-permute-start(f32[512,128]{1,0:T(8,128)} %get-tuple-element.15), channel_id=1, source_target_pairs={{0,8},{1,17},{2,10},{3,19},{4,12},{5,21},{6,14},{7,23},{8,0},{9,25... | collective-permute-start | bytes 786440 | tf_op jit(solution)/shard_map/ppermute | solution.py:189
  45.0 6.4 %collective-permute-start.18 = (f32[512,128]{1,0:T(8,128)S(1)}, f32[512,128]{1,0:T(8,128)S(1)}, u32[]{:S(2)}, u32[]{:S(2)}) collective-permute-start(f32[512,128]{1,0:T(8,128)S(1)} %add.6), channel_id=1, source_target_pairs={{0,16},{1,9},{2,18},{3,11},{4,20},{5,13},{6,22},{7,15},{8,24},{9,1... | collective-permute-start | bytes 786440 | tf_op jit(solution)/shard_map/ppermute | solution.py:189

commit v2 on v1

--- a/solution.py
+++ b/solution.py
@@ -1,4 +1,5 @@
 import functools
+import math
 
 import jax
 import jax.numpy as jnp
@@ -9,9 +10,17 @@
 
 LANES = 128
 CORES = 2
+CHUNKS = 2
 AXES = ("row", "col")
 VMEM = pl.BlockSpec(memory_space=pltpu.VMEM)
-SMEM = pl.BlockSpec(memory_space=pltpu.SMEM)
+
+
+def room(*arrays):
+    return pltpu.CompilerParams(vmem_limit_bytes=8 * sum(math.prod(a.shape) for a in arrays) + (1 << 20))
+
+
+def cheap():
+    return pl.CostEstimate(flops=1, bytes_accessed=1, transcendentals=0)
 
 
 def exact(a, b, contract):
@@ -79,6 +88,8 @@
         self.bulk = self.m_rows + self.rows_c + 8
         self.small = self.nodes * self.own
         self.total = self.n_row * self.rows_r
+        far = range(CORES, self.n_z)
+        self.pairs = [tuple(far[i : i + CORES]) for i in range(0, len(far), CORES)]
 
     def fits(self):
         def power(n):
@@ -89,6 +100,7 @@
             and power(self.n_row)
             and power(self.n_z)
             and self.n_row > 1
+            and self.n_z > 1
             and self.wide * CORES == LANES
             and self.rows_r == LANES
             and self.span == LANES
@@ -96,7 +108,9 @@
             and self.slots % 8 == 0
             and self.own % 8 == 0
             and self.rows_c % 8 == 0
+            and self.nodes % CORES == 0
             and self.nodes <= 8
+            and self.wide % (8 * CHUNKS) == 0
         )
 
 
@@ -106,73 +120,134 @@
     return r, lax.div(c, CORES), lax.rem(c, CORES)
 
 
-def pack_kernel(n, factor, listed, inv_t, pattern, bulk, *smalls):
-    r, z, core = spot()
+def pack_kernel(n, factor_h, listed_h, inv_h, pattern_h, bulk, *rest):
+    smalls = rest[: n.n_z - 1]
+    factor, listed_t, inv_t, pattern_t, wide_l, sems = rest[n.n_z - 1 :]
+    pairs = ((factor_h, factor), (listed_h, listed_t), (inv_h, inv_t), (pattern_h, pattern_t))
+    copies = [pltpu.make_async_copy(a, b, sems.at[i]) for i, (a, b) in enumerate(pairs)]
+    for copy in copies:
+        copy.start()
+    for copy in copies:
+        copy.wait()
+    _, z, core = spot()
     col = z * CORES + core
-    line = lax.broadcasted_iota(jnp.int32, (n.slots, LANES), 0)
-    head = lax.broadcasted_iota(jnp.int32, (8, LANES), 0)
-    lane8 = lax.broadcasted_iota(jnp.int32, (8, LANES), 1)
-    flags = jnp.zeros((8, LANES), jnp.float32)
-    for m in range(n.own):
-        keep = jnp.zeros((n.slots, LANES), jnp.float32)
-        for k in range(n.nodes):
-            value = listed[m, k].astype(jnp.float32)
-            keep = jnp.where(lax.rem(line, n.nodes) == k, value, keep)
-            flags = jnp.where((head == k) & (lane8 == col * n.own + m), value, flags)
-        part = pl.ds(m * n.slots, n.slots)
-        bulk[part, :] = factor[part, :] * keep
-    bulk[pl.ds(n.m_rows + n.rows_c, 8), :] = flags
+    wide_l[...] = jnp.zeros((8, LANES), jnp.float32)
+    wide_l[pl.ds(0, n.nodes), pl.ds(0, n.own)] = listed_t[...].astype(jnp.float32)
+    flags = wide_l[...]
+    row = lax.broadcasted_iota(jnp.int32, (n.m_rows, LANES), 0)
+    lane = lax.broadcasted_iota(jnp.int32, (n.m_rows, LANES), 1)
+    node = lax.rem(row, n.nodes)
+    mine = jnp.zeros((n.m_rows, LANES), jnp.float32)
+    for k in range(n.nodes):
+        mine = jnp.where(node == k, flags[k : k + 1, :], mine)
+    keep = jnp.sum(jnp.where(lane == lax.div(row, n.slots), mine, 0.0), axis=1, keepdims=True)
+    bulk[pl.ds(0, n.m_rows), :] = factor[...] * keep
+    bulk[pl.ds(n.m_rows + n.rows_c, 8), :] = pltpu.roll(flags, col * n.own, 1)
     high = n.rows_r // n.pattern[0]
     deep = n.rows_c // n.pattern[1]
-    lane = lax.broadcasted_iota(jnp.int32, (deep, LANES), 1)
+    tile = lax.div(lax.broadcasted_iota(jnp.int32, (1, LANES), 1), high)
     for q in range(n.pattern[1]):
-        keep = jnp.zeros((deep, LANES), jnp.float32)
+        keep = jnp.zeros((1, LANES), jnp.float32)
         for p in range(n.pattern[0]):
-            keep = jnp.where(lax.div(lane, high) == p, pattern[p, q].astype(jnp.float32), keep)
+            keep = jnp.where(tile == p, pattern_t[q : q + 1, p : p + 1].astype(jnp.float32), keep)
         bulk[pl.ds(n.m_rows + q * deep, deep), :] = inv_t[pl.ds(q * deep, deep), :] * keep
+    for s, small in zip((0, *range(CORES, n.n_z)), smalls):
+        cut(n, bulk, z ^ s, small, 0)
+
+
+def cut(n, bulk, want, out, at):
     for k in range(n.nodes):
-        loads = [bulk[pl.ds(t * n.nodes + k, n.own, stride=n.slots), :] for t in range(n.tiles)]
-        for s, small in enumerate(smalls):
-            want = z ^ s
-            piece = loads[0]
-            for t in range(1, n.tiles):
-                piece = jnp.where(want == t, loads[t], piece)
-            small[pl.ds(k * n.own, n.own), :] = piece
-
-
-def stack_kernel(n, *refs):
+        piece = None
+        for t in range(n.tiles):
+            load = bulk[pl.ds(t * n.nodes + k, n.own, stride=n.slots), :]
+            piece = load if piece is None else jnp.where(want == t, load, piece)
+        out[pl.ds(at + k * n.own, n.own), :] = piece
+
+
+def stack_kernel(n, own, bulk, *refs):
     out = refs[-1]
+    _, z, _ = spot()
+    out[pl.ds(0, n.small), :] = own[...]
+    cut(n, bulk, z, out, n.small)
     for s, ref in enumerate(refs[:-1]):
-        out[pl.ds(s * n.small, n.small), :] = ref[...]
+        out[pl.ds((s + CORES) * n.small, n.small), :] = ref[...]
+
+
+def join_kernel(n, *refs):
+    out = refs[-1]
+    at = 0
+    for ref in refs[:-1]:
+        out[pl.ds(at, ref.shape[0]), :] = ref[...]
+        at += ref.shape[0]
+
+
+def choose(core, pair):
+    return jnp.where(core == 0, pair[0], pair[1])
+
+
+def place_kernel(n, *refs):
+    half = len(refs[:-3]) // CORES
+    m_row, p_t, mask_ref = refs[-3:]
+    _, z, core = spot()
+    mask_ref[...] = jnp.zeros((8, LANES), jnp.float32)
+
+    def put(ref, at, c):
+        m_row[pl.ds(c * n.m_rows, n.m_rows), :] = ref[pl.ds(at, n.m_rows), :]
+        p_t[pl.ds(c * n.rows_c, n.rows_c), :] = ref[pl.ds(at + n.m_rows, n.rows_c), :]
+        mask_ref[...] += ref[pl.ds(at + n.m_rows + n.rows_c, 8), :]
+
+    for q in range(CORES):
+        owner = core ^ q
+        own, near, *rest = refs[q * half : (q + 1) * half]
+        put(own, 0, z * CORES + owner)
+        put(near, 0, (z ^ 1) * CORES + owner)
+        for pair, ref in zip(n.pairs, rest):
+            for i in range(CORES):
+                put(ref, i * n.bulk, (z ^ choose(owner, pair)) * CORES + (owner ^ i))
 
 
 def work_kernel(n, *refs):
-    smalls = refs[: CORES * n.n_row]
-    bulks = refs[CORES * n.n_row : CORES * (n.n_row + n.n_z)]
-    columns, update, m_all, m_row, p_t, x_t = refs[CORES * (n.n_row + n.n_z) :]
+    smalls = refs[:CORES]
+    m_row, p_t, mask_ref, columns = refs[CORES : CORES + 4]
+    *updates, m_all = refs[CORES + 4 :]
     r, z, core = spot()
-    mask = jnp.zeros((8, LANES), jnp.float32)
+    lane = lax.broadcasted_iota(jnp.int32, (n.own, LANES), 1)
+    left = lane < n.wide
+    first = core == 0
     for q in range(CORES):
-        for s in range(n.n_z):
-            ref = bulks[q * n.n_z + s]
-            c = (z ^ s) * CORES + (core ^ q)
-            m_row[pl.ds(c * n.m_rows, n.m_rows), :] = ref[pl.ds(0, n.m_rows), :]
-            p_t[pl.ds(c * n.rows_c, n.rows_c), :] = ref[pl.ds(n.m_rows, n.rows_c), :]
-            mask += ref[pl.ds(n.m_rows + n.rows_c, 8), :]
         for d in range(n.n_row):
-            ref = smalls[q * n.n_row + d]
             for s in range(n.n_z):
                 c = (z ^ s) * CORES + (core ^ q)
                 at = (r ^ d) * n.span + c * n.own
-                for k in range(n.nodes):
-                    m_all[k, pl.ds(at, n.own), :] = ref[pl.ds(s * n.small + k * n.own, n.own), :]
+                for k in range(0, n.nodes, CORES):
+                    start = (d * n.n_z + s) * n.small + k * n.own
+                    one = smalls[q][pl.ds(start, n.own), :]
+                    two = smalls[q][pl.ds(start + n.own, n.own), :]
+                    turned = pltpu.roll(jnp.where(first, two, one), n.wide, 1)
+                    both = jnp.where(left == first, jnp.where(first, one, two), turned)
+                    m_all[k // CORES, pl.ds(at, n.own), :] = both
+    chunk = n.wide // len(updates)
     for k in range(n.nodes):
-        x_t[k] = exact(m_all[k], p_t[...], ((0,), (0,)))
-        part = -x_t[k, pl.ds(core * n.wide, n.wide), :] * mask[k : k + 1, :]
+        if k % CORES == 0:
+            x_t = exact(m_all[k // CORES], p_t[...], ((0,), (0,)))
+        at = k % CORES * n.wide
+        part = -x_t[at : at + n.wide, :] * mask_ref[k : k + 1, :]
         columns[pl.ds(k, n.wide, stride=n.nodes), :] = part
+        sides = [m_row[pl.ds(t * n.nodes + k, n.rows_r, stride=n.slots), :] for t in range(n.tiles)]
+        wide = exact(part, jnp.concatenate(sides, axis=1), ((1,), (0,)))
         for t in range(n.tiles):
-            side = m_row[pl.ds(t * n.nodes + k, n.rows_r, stride=n.slots), :]
-            update[pl.ds(t * n.nodes + k, n.wide, stride=n.slots), :] = exact(part, side, ((1,), (0,)))
+            for h, update in enumerate(updates):
+                piece = wide[h * chunk : (h + 1) * chunk, t * LANES : (t + 1) * LANES]
+                update[pl.ds(t * n.nodes + k, chunk, stride=n.slots), :] = piece
+
+
+def finish_kernel(h, diag, one, two, *refs):
+    out, room_ref, sem = refs[-3:]
+    size = one.shape[0]
+    room_ref[...] = diag[pl.ds(h * size, size), :] - (one[...] + two[...])
+    copy = pltpu.make_async_copy(room_ref, out.at[pl.ds(h * size, size), :], sem)
+    copy.start()
+    copy.wait()
 
 
 def fast(n, inv_known, pattern, factor, listed, diag_inverse):
@@ -207,39 +282,88 @@
         split = array.reshape(lead, n.nodes, n.tiles, LANES)
         return jnp.transpose(split, (0, 2, 1, 3)).reshape(lead * n.slots, LANES)
 
+    taken = [view(factor), listed.T, inv_known.T, pattern.T]
+    out = [shape(n.bulk, LANES)] + [shape(n.small, LANES)] * (n.n_z - 1)
     bulk, *smalls = pl.pallas_call(
         functools.partial(pack_kernel, n),
-        in_specs=[VMEM, SMEM, VMEM, SMEM],
-        out_specs=[VMEM] * (1 + n.n_z),
-        out_shape=[shape(n.bulk, LANES)] + [shape(n.small, LANES)] * n.n_z,
-    )(view(factor), listed, inv_known.T, pattern)
-
-    smalls = [smalls[0]] + [over_z(smalls[s], s) for s in range(1, n.n_z)]
-    bulks = [bulk] + [over_z(bulk, s) for s in range(1, n.n_z)]
+        in_specs=[pl.BlockSpec(memory_space=pltpu.HBM)] * 4,
+        out_specs=[VMEM] * len(out),
+        out_shape=out,
+        scratch_shapes=[pltpu.VMEM(a.shape, a.dtype) for a in taken]
+        + [pltpu.VMEM((8, LANES), jnp.float32), pltpu.SemaphoreType.DMA((len(taken),))],
+
+        cost_estimate=cheap(),
+    )(*taken)
+
+    def join(*arrays):
+        out = shape(sum(a.shape[0] for a in arrays), LANES)
+        return pl.pallas_call(
+            functools.partial(join_kernel, n),
+            in_specs=[VMEM] * len(arrays),
+            out_specs=VMEM,
+            out_shape=out,
+            compiler_params=room(out),
+        )(*arrays)
+
+    def over_pair_z(array, pair):
+        return route(array, lambda r, z, core: (r, z ^ pair[core], core))
+
+    near = over_z(bulk, 1)
+    far = [over_z(small, s) for s, small in zip(range(CORES, n.n_z), smalls[1:])]
+    other = over_core(bulk)
+    both, near, far = lax.optimization_barrier((join(bulk, other), near, far))
+    out = shape(n.n_z * n.small, LANES)
     small = pl.pallas_call(
         functools.partial(stack_kernel, n),
         in_specs=[VMEM] * n.n_z,
         out_specs=VMEM,
-        out_shape=shape(n.n_z * n.small, LANES),
-    )(*smalls)
-    spread = [small] + [over_row(small, d) for d in range(1, n.n_row)]
-    other_bulks = [over_core(b) for b in bulks]
-    other_spread = [over_core(b) for b in spread]
-    columns, update = pl.pallas_call(
+        out_shape=out,
+        compiler_params=room(out),
+    )(smalls[0], near, *far)
+    bulks = [over_pair_z(both, pair) for pair in n.pairs]
+    spread = [over_row(small, d) for d in range(1, n.n_row)]
+    bulks = [bulk, near, *bulks]
+    other_bulks = [other] + [over_core(b) for b in bulks[1:]]
+    spread = join(small, *spread)
+    spread = [spread, over_core(spread)]
+    taken = [*bulks, *other_bulks]
+    out = [shape(n.span * n.slots, LANES), shape(n.n_col * n.rows_c, LANES), shape(8, LANES)]
+    placed = pl.pallas_call(
+        functools.partial(place_kernel, n),
+        in_specs=[VMEM] * len(taken),
+        out_specs=[VMEM] * len(out),
+        out_shape=out,
+        compiler_params=room(*taken, *out),
+        cost_estimate=cheap(),
+    )(*taken)
+    taken = [*spread, *placed]
+    out = [shape(n.wide * n.nodes, LANES)] + [shape(n.wide * n.slots // CHUNKS, LANES)] * CHUNKS
+    scratch = [shape(n.nodes // CORES, n.total, LANES)]
+    columns, *updates = pl.pallas_call(
         functools.partial(work_kernel, n),
-        in_specs=[VMEM] * (CORES * (n.n_row + n.n_z)),
-        out_specs=[VMEM] * 2,
-        out_shape=[shape(n.wide * n.nodes, LANES), shape(n.wide * n.slots, LANES)],
-        scratch_shapes=[
-            pltpu.VMEM((n.nodes, n.total, LANES), jnp.float32),
-            pltpu.VMEM((n.span * n.slots, LANES), jnp.float32),
-            pltpu.VMEM((n.total, LANES), jnp.float32),
-            pltpu.VMEM((n.nodes, LANES, LANES), jnp.float32),
-        ],
-    )(*spread, *other_spread, *bulks, *other_bulks)
-    for i in range(len(steps)):
-        update = update + over_pair(update, i)
-    schur = view(diag_inverse) - update
+        in_specs=[VMEM] * len(taken),
+        out_specs=[VMEM] * len(out),
+        out_shape=out,
+        scratch_shapes=[pltpu.VMEM(a.shape, a.dtype) for a in scratch],
+        compiler_params=room(*taken, *out, *scratch),
+        cost_estimate=cheap(),
+    )(*taken)
+    for i in range(len(steps) - 1):
+        updates = [update + over_pair(update, i) for update in updates]
+    got = [over_pair(update, len(steps) - 1) for update in updates]
+    diag = view(diag_inverse)
+    schur = None
+    for h, pair in enumerate(zip(updates, got)):
+        taken = [diag, *pair] + ([] if schur is None else [schur])
+        schur = pl.pallas_call(
+            functools.partial(finish_kernel, h),
+            in_specs=[VMEM] * 3 + [pl.BlockSpec(memory_space=pl.ANY)] * (len(taken) - 3),
+            out_specs=pl.BlockSpec(memory_space=pl.ANY),
+            out_shape=shape(n.wide * n.slots, LANES),
+            scratch_shapes=[pltpu.VMEM(pair[0].shape, jnp.float32), pltpu.SemaphoreType.DMA],
+            input_output_aliases={} if schur is None else {3: 0},
+            compiler_params=room(*taken),
+        )(*taken)
     schur = jnp.transpose(schur.reshape(n.wide, n.tiles, n.nodes, LANES), (0, 2, 1, 3))
     return columns.reshape(n.wide, n.nodes, LANES), schur.reshape(n.wide, n.nodes, n.width)
 

time: 52.5 us -> 38.3 us (0.73)
  waiting for transfers between devices: 22.1 us -> 17.2 us
  local copies, waits for them, and re-layouts: 3.88 us -> 0.91 us
  Pallas kernels: 6.54 us -> 4.35 us
  starting transfers between devices: 17.1 us -> 15 us
  other arithmetic: 1.73 us -> 0.03 us
    ppermute x19 -> x15, waiting for transfers between devices: 22.1 us -> 17.2 us  [route(): return lax.ppermute(array, AXES, pairs)]
    unnamed x42 -> x8, local copies, waits for them, and re-layouts: 3.88 us -> 0.91 us
    ppermute x19 -> x15, starting transfers between devices: 17.1 us -> 15 us  [route(): return lax.ppermute(array, AXES, pairs)]
    pallas_call x1, Pallas kernels: 1.4 us -> 0.02 us  [fast(): pl.pallas_call(functools.partial(stack_kernel, n), in_specs=[VMEM] * n.n_...]
    add x1 -> x2, other arithmetic: 0.99 us -> 0.03 us  [fast(): updates = [update + over_pair(update, i) for update in updates]]
    pallas_call x2 -> x7, Pallas kernels: 5.14 us -> 4.32 us  [the longest x1 1.65 us: fast(): pl.pallas_call(functools.partial(pack_kernel, n), in_specs=[pl.BlockSpec(...]
    sub x1 -> x0, other arithmetic: 0.74 us -> none  [fast(): schur = view(diag_inverse) - update]
  transfers between devices with their start and end apart: 19 -> 15, of which waited for: 8 -> 10; matrix products, arithmetic and copies ran while one was open for 0% -> 0% of each run, Pallas kernels for 0% -> 2%
where the time goes in v2:
time: 38.3 us; the launch traced here: 38.2 us
  waiting for transfers between devices  17.2 us (45%)
  starting transfers between devices  15 us (39%)
  Pallas kernels  4.35 us (11%)
  local copies, waits for them, and re-layouts  0.91 us (2%)
  between operations  0.73 us (2%)
    ppermute x15, waiting for transfers between devices, route(): return lax.ppermute(array, AXES, pairs)  17.2 us
    ppermute x15, starting transfers between devices, route(): return lax.ppermute(array, AXES, pairs)  15 us
    pallas_call x1, Pallas kernels, fast(): pl.pallas_call(functools.partial(pack_kernel, n), in_specs=[pl.BlockSpec(...  1.65 us
    pallas_call x2, Pallas kernels, fast(): pl.pallas_call(functools.partial(finish_kernel, h), in_specs=[VMEM] * 3 +...  1.37 us
    pallas_call x1, Pallas kernels, fast(): pl.pallas_call(functools.partial(work_kernel, n), in_specs=[VMEM] * len(t...  1.21 us
    unnamed x8, local copies, waits for them, and re-layouts  0.91 us
  transfers between devices with their start and end apart: 15, of which 10 were waited for; matrix products, arithmetic and copies ran while one was open for 0% of the time, Pallas kernels for 2%

profile of v2, /device:TPU:0, one launch (start us, length us, event | category | flops | bytes accessed | tf_op | source)
XLA Modules:
  0.0 38.2 jit_solution(14874310643580152923)
XLA Ops:
  0.6 1.7 %shard_map.68 = (f32[200,128]{1,0:T(8,128)}, f32[32,128]{1,0:T(8,128)}, f32[32,128]{1,0:T(8,128)}, f32[32,128]{1,0:T(8,128)}) custom-call(f32[128,128]{1,0:T(8,128)} %bitcast.22, s32[2,16]{1,0:T(2,128)} %bitcast.24, f32[64,128]{1,0:T(8,128)} %bitcast.23, s32[1,2]{1,0:T(1,128)} %bitcast.25), custom_call_target="tpu_custom_call" | custom-call | flops 1 | bytes 1 | tf_op jit(solution)/shard_map/pallas_call | solution.py:287
  2.3 0.5 %collective-permute-start = (f32[200,128]{1,0:T(8,128)}, f32[200,128]{1,0:T(8,128)S(1)}, u32[]{:S(2)}, u32[]{:S(2)}) collective-permute-start(f32[200,128]{1,0:T(8,128)} %get-tuple-element.17.refs_0_), channel_id=1, source_target_pairs={{0,1},{1,0},{2,3},{3,2},{4,5},{5,4},{6,7},{7,6},{8,9},{9,8},{10,11... | collective-permute-start | bytes 307208 | tf_op jit(solution)/shard_map/ppermute | solution.py:264
  2.8 2.6 %collective-permute-start.1 = (f32[200,128]{1,0:T(8,128)}, f32[200,128]{1,0:T(8,128)S(1)}, u32[]{:S(2)}, u32[]{:S(2)}) collective-permute-start(f32[200,128]{1,0:T(8,128)} %get-tuple-element.17.refs_0_), channel_id=1, source_target_pairs={{0,2},{1,3},{2,0},{3,1},{4,6},{5,7},{6,4},{7,5},{8,10},{9,11},{10,... | collective-permute-start | bytes 307208 | tf_op jit(solution)/shard_map/ppermute | solution.py:264
  5.5 2.6 %collective-permute-start.2 = (f32[32,128]{1,0:T(8,128)}, f32[32,128]{1,0:T(8,128)S(1)}, u32[]{:S(2)}, u32[]{:S(2)}) collective-permute-start(f32[32,128]{1,0:T(8,128)} %get-tuple-element.18), channel_id=1, source_target_pairs={{0,4},{1,5},{2,6},{3,7},{4,0},{5,1},{6,2},{7,3},{8,12},{9,13},{10,... | collective-permute-start | bytes 49160 | tf_op jit(solution)/shard_map/ppermute | solution.py:264
  8.0 0.0 collective-permute-start.3
  8.0 0.0 collective-permute-done.refs_1_.refs_3_
  8.1 0.0 copy-start.1
  8.1 0.9 %copy-done.1 = f32[200,128]{1,0:T(8,128)S(1)} copy-done((f32[200,128]{1,0:T(8,128)S(1)}, f32[200,128]{1,0:T(8,128)}, u32[]{:S(2)}) %copy-start.1) | copy-done | bytes 102424
  8.9 0.0 copy-start.3
  9.0 1.3 %collective-permute-done.2.refs_0_ = f32[32,128]{1,0:T(8,128)S(1)} collective-permute-done((f32[32,128]{1,0:T(8,128)}, f32[32,128]{1,0:T(8,128)S(1)}, u32[]{:S(2)}, u32[]{:S(2)}) %collective-permute-start.2) | collective-permute-done | bytes 16416 | tf_op jit(solution)/shard_map/ppermute | solution.py:264
  10.3 3.5 %collective-permute-done.3.refs_1_ = f32[32,128]{1,0:T(8,128)S(1)} collective-permute-done((f32[32,128]{1,0:T(8,128)}, f32[32,128]{1,0:T(8,128)S(1)}, u32[]{:S(2)}, u32[]{:S(2)}) %collective-permute-start.3) | collective-permute-done | bytes 16416 | tf_op jit(solution)/shard_map/ppermute | solution.py:264
  13.8 0.0 collective-permute-done.1.bulk.refs_1_
  13.8 0.0 collective-permute-start.8
  13.8 0.0 copy-done.3
  13.8 0.0 copy-start.2
  13.9 1.6 %collective-permute-start.4 = (f32[128,128]{1,0:T(8,128)S(1)}, f32[128,128]{1,0:T(8,128)S(1)}, u32[]{:S(2)}, u32[]{:S(2)}) collective-permute-start(f32[128,128]{1,0:T(8,128)S(1)} %shard_map.70.refs_0_), channel_id=1, source_target_pairs={{0,8},{1,9},{2,10},{3,11},{4,12},{5,13},{6,14},{7,15},{8,0},{9,1},... | collective-permute-start | bytes 196616 | tf_op jit(solution)/shard_map/ppermute | solution.py:264
  15.4 1.5 %collective-permute-start.5 = (f32[128,128]{1,0:T(8,128)S(1)}, f32[128,128]{1,0:T(8,128)S(1)}, u32[]{:S(2)}, u32[]{:S(2)}) collective-permute-start(f32[128,128]{1,0:T(8,128)S(1)} %shard_map.70.refs_0_), channel_id=1, source_target_pairs={{0,16},{1,17},{2,18},{3,19},{4,20},{5,21},{6,22},{7,23},{8,24},{9,... | collective-permute-start | bytes 196616 | tf_op jit(solution)/shard_map/ppermute | solution.py:264
  16.9 0.5 %collective-permute-start.6 = (f32[128,128]{1,0:T(8,128)S(1)}, f32[128,128]{1,0:T(8,128)S(1)}, u32[]{:S(2)}, u32[]{:S(2)}) collective-permute-start(f32[128,128]{1,0:T(8,128)S(1)} %shard_map.70.refs_0_), channel_id=1, source_target_pairs={{0,24},{1,25},{2,26},{3,27},{4,28},{5,29},{6,30},{7,31},{8,16},{9,... | collective-permute-start | bytes 196616 | tf_op jit(solution)/shard_map/ppermute | solution.py:264
  17.4 1.1 %collective-permute-done.4.refs_1_ = f32[128,128]{1,0:T(8,128)S(1)} collective-permute-done((f32[128,128]{1,0:T(8,128)S(1)}, f32[128,128]{1,0:T(8,128)S(1)}, u32[]{:S(2)}, u32[]{:S(2)}) %collective-permute-start.4) | collective-permute-done | bytes 65568 | tf_op jit(solution)/shard_map/ppermute | solution.py:264
  18.6 1.7 %collective-permute-done.5.refs_2_ = f32[128,128]{1,0:T(8,128)S(1)} collective-permute-done((f32[128,128]{1,0:T(8,128)S(1)}, f32[128,128]{1,0:T(8,128)S(1)}, u32[]{:S(2)}, u32[]{:S(2)}) %collective-permute-start.5) | collective-permute-done | bytes 65568 | tf_op jit(solution)/shard_map/ppermute | solution.py:264
  20.3 1.8 %collective-permute-done.6.refs_3_ = f32[128,128]{1,0:T(8,128)S(1)} collective-permute-done((f32[128,128]{1,0:T(8,128)S(1)}, f32[128,128]{1,0:T(8,128)S(1)}, u32[]{:S(2)}, u32[]{:S(2)}) %collective-permute-start.6) | collective-permute-done | bytes 65568 | tf_op jit(solution)/shard_map/ppermute | solution.py:264
  22.1 0.1 collective-permute-start.7
  22.2 0.7 %collective-permute-done.8.refs_2_ = f32[400,128]{1,0:T(8,128)S(1)} collective-permute-done((f32[400,128]{1,0:T(8,128)S(1)}, f32[400,128]{1,0:T(8,128)S(1)}, u32[]{:S(2)}, u32[]{:S(2)}) %collective-permute-start.8) | collective-permute-done | bytes 204832 | tf_op jit(solution)/shard_map/ppermute | solution.py:264
  22.9 0.0 collective-permute-start.10
  22.9 0.5 %collective-permute-start.9 = (f32[200,128]{1,0:T(8,128)S(1)}, f32[200,128]{1,0:T(8,128)S(1)}, u32[]{:S(2)}, u32[]{:S(2)}) collective-permute-start(f32[200,128]{1,0:T(8,128)S(1)} %collective-permute-done.1.bulk.refs_1_), channel_id=1, source_target_pairs={{0,1},{1,0},{2,3},{3,2},{4,5},{5,4},{6,7},{7,6},{8,9},{9,8},{10,11... | collective-permute-start | bytes 307208 | tf_op jit(solution)/shard_map/ppermute | solution.py:264
  23.4 1.1 %collective-permute-done.9.refs_4_ = f32[200,128]{1,0:T(8,128)S(1)} collective-permute-done((f32[200,128]{1,0:T(8,128)S(1)}, f32[200,128]{1,0:T(8,128)S(1)}, u32[]{:S(2)}, u32[]{:S(2)}) %collective-permute-start.9) | collective-permute-done | bytes 102432 | tf_op jit(solution)/shard_map/ppermute | solution.py:264
  24.5 0.0 collective-permute-done.10.refs_5_
  24.5 0.0 copy-done.2
  24.5 0.1 shard_map.72
  24.6 0.0 collective-permute-done.7.refs_1_
  24.6 1.2 %shard_map.73 = (f32[128,128]{1,0:T(8,128)}, f32[256,128]{1,0:T(8,128)S(1)}, f32[256,128]{1,0:T(8,128)S(1)}) custom-call(f32[512,128]{1,0:T(8,128)S(1)} %shard_map.71.refs_0_, f32[512,128]{1,0:T(8,128)S(1)} %collective-permute-done.7.refs_1_, f32[1024,128]{1,0:T(8,128)S(1)} %get-tuple-element.24.refs_2_, f32[512,128]{1,0:T(8,128)S(1)} %get-tuple-element.25.refs_3_, ...), custom_call_target="tpu_custom_call" | custom-call | flops 1 | bytes 1 | tf_op jit(solution)/shard_map/pallas_call | solution.py:342
  25.8 1.5 %collective-permute-start.13 = (f32[256,128]{1,0:T(8,128)S(1)}, f32[256,128]{1,0:T(8,128)S(1)}, u32[]{:S(2)}, u32[]{:S(2)}) collective-permute-start(f32[256,128]{1,0:T(8,128)S(1)} %get-tuple-element.29), channel_id=1, source_target_pairs={{0,8},{1,17},{2,10},{3,19},{4,12},{5,21},{6,14},{7,23},{8,0},{9,25... | collective-permute-start | bytes 393224 | tf_op jit(solution)/shard_map/ppermute | solution.py:264
  27.3 0.5 %collective-permute-start.11 = (f32[256,128]{1,0:T(8,128)S(1)}, f32[256,128]{1,0:T(8,128)S(1)}, u32[]{:S(2)}, u32[]{:S(2)}) collective-permute-start(f32[256,128]{1,0:T(8,128)S(1)} %get-tuple-element.28), channel_id=1, source_target_pairs={{0,8},{1,17},{2,10},{3,19},{4,12},{5,21},{6,14},{7,23},{8,0},{9,25... | collective-permute-start | bytes 393224 | tf_op jit(solution)/shard_map/ppermute | solution.py:264
  27.9 2.9 %collective-permute-done.13 = f32[256,128]{1,0:T(8,128)S(1)} collective-permute-done((f32[256,128]{1,0:T(8,128)S(1)}, f32[256,128]{1,0:T(8,128)S(1)}, u32[]{:S(2)}, u32[]{:S(2)}) %collective-permute-start.13) | collective-permute-done | bytes 131104 | tf_op jit(solution)/shard_map/ppermute | solution.py:264
  30.8 0.0 copy-start
  30.8 1.6 %collective-permute-start.14 = (f32[256,128]{1,0:T(8,128)S(1)}, f32[256,128]{1,0:T(8,128)S(1)}, u32[]{:S(2)}, u32[]{:S(2)}) collective-permute-start(f32[256,128]{1,0:T(8,128)S(1)} %add.7.one), channel_id=1, source_target_pairs={{0,16},{1,9},{2,18},{3,11},{4,20},{5,13},{6,22},{7,15},{8,24},{9,1... | collective-permute-start | bytes 393224 | tf_op jit(solution)/shard_map/ppermute | solution.py:264
  32.4 0.0 collective-permute-done.11
  32.4 1.5 %collective-permute-start.12 = (f32[256,128]{1,0:T(8,128)S(1)}, f32[256,128]{1,0:T(8,128)S(1)}, u32[]{:S(2)}, u32[]{:S(2)}) collective-permute-start(f32[256,128]{1,0:T(8,128)S(1)} %add.6.one), channel_id=1, source_target_pairs={{0,16},{1,9},{2,18},{3,11},{4,20},{5,13},{6,22},{7,15},{8,24},{9,1... | collective-permute-start | bytes 393224 | tf_op jit(solution)/shard_map/ppermute | solution.py:264
  33.9 2.0 %collective-permute-done.14.two = f32[256,128]{1,0:T(8,128)S(1)} collective-permute-done((f32[256,128]{1,0:T(8,128)S(1)}, f32[256,128]{1,0:T(8,128)S(1)}, u32[]{:S(2)}, u32[]{:S(2)}) %collective-permute-start.14) | collective-permute-done | bytes 131104 | tf_op jit(solution)/shard_map/ppermute | solution.py:264
  35.9 0.0 copy-done
  35.9 0.7 %shard_map.74.refs_0_ = f32[512,128]{1,0:T(8,128)} custom-call(f32[512,128]{1,0:T(8,128)S(1)} %bitcast.19, f32[256,128]{1,0:T(8,128)S(1)} %add.7.one, f32[256,128]{1,0:T(8,128)S(1)} %collective-permute-done.14.two), custom_call_target="tpu_custom_call" | custom-call | tf_op jit(solution)/shard_map/pallas_call | solution.py:358
  36.6 0.9 %collective-permute-done.12.two = f32[256,128]{1,0:T(8,128)S(1)} collective-permute-done((f32[256,128]{1,0:T(8,128)S(1)}, f32[256,128]{1,0:T(8,128)S(1)}, u32[]{:S(2)}, u32[]{:S(2)}) %collective-permute-start.12) | collective-permute-done | bytes 131104 | tf_op jit(solution)/shard_map/ppermute | solution.py:264
  37.5 0.7 %shard_map.75 = f32[512,128]{1,0:T(8,128)} custom-call(f32[512,128]{1,0:T(8,128)S(1)} %bitcast.20, f32[256,128]{1,0:T(8,128)S(1)} %add.6.one, f32[256,128]{1,0:T(8,128)S(1)} %collective-permute-done.12.two, f32[512,128]{1,0:T(8,128)} %shard_map.74.refs_0_), custom_call_target="tpu_custom_call", output_to_operand_aliasing={{}: (3, {})} | custom-call | tf_op jit(solution)/shard_map/pallas_call | solution.py:358
  (5 shorter events, 0.1 us)
Async XLA Ops:
  2.3 5.8 %collective-permute-start = (f32[200,128]{1,0:T(8,128)}, f32[200,128]{1,0:T(8,128)S(1)}, u32[]{:S(2)}, u32[]{:S(2)}) collective-permute-start(f32[200,128]{1,0:T(8,128)} %get-tuple-element.17.refs_0_), channel_id=1, source_target_pairs={{0,1},{1,0},{2,3},{3,2},{4,5},{5,4},{6,7},{7,6},{8,9},{9,8},{10,11... | collective-permute-start | bytes 307208 | tf_op jit(solution)/shard_map/ppermute | solution.py:264
  2.8 11.0 %collective-permute-start.1 = (f32[200,128]{1,0:T(8,128)}, f32[200,128]{1,0:T(8,128)S(1)}, u32[]{:S(2)}, u32[]{:S(2)}) collective-permute-start(f32[200,128]{1,0:T(8,128)} %get-tuple-element.17.refs_0_), channel_id=1, source_target_pairs={{0,2},{1,3},{2,0},{3,1},{4,6},{5,7},{6,4},{7,5},{8,10},{9,11},{10,... | collective-permute-start | bytes 307208 | tf_op jit(solution)/shard_map/ppermute | solution.py:264
  5.5 4.8 %collective-permute-start.2 = (f32[32,128]{1,0:T(8,128)}, f32[32,128]{1,0:T(8,128)S(1)}, u32[]{:S(2)}, u32[]{:S(2)}) collective-permute-start(f32[32,128]{1,0:T(8,128)} %get-tuple-element.18), channel_id=1, source_target_pairs={{0,4},{1,5},{2,6},{3,7},{4,0},{5,1},{6,2},{7,3},{8,12},{9,13},{10,... | collective-permute-start | bytes 49160 | tf_op jit(solution)/shard_map/ppermute | solution.py:264
  8.0 5.8 %collective-permute-start.3 = (f32[32,128]{1,0:T(8,128)}, f32[32,128]{1,0:T(8,128)S(1)}, u32[]{:S(2)}, u32[]{:S(2)}) collective-permute-start(f32[32,128]{1,0:T(8,128)} %get-tuple-element.19), channel_id=1, source_target_pairs={{0,6},{1,7},{2,4},{3,5},{4,2},{5,3},{6,0},{7,1},{8,14},{9,15},{10,... | collective-permute-start | bytes 49160 | tf_op jit(solution)/shard_map/ppermute | solution.py:264
  8.1 0.9 %copy-start.1 = (f32[200,128]{1,0:T(8,128)S(1)}, f32[200,128]{1,0:T(8,128)}, u32[]{:S(2)}) copy-start(f32[200,128]{1,0:T(8,128)} %get-tuple-element.17.refs_0_) | copy-start | bytes 307204
  8.9 4.9 %copy-start.3 = (f32[32,128]{1,0:T(8,128)S(1)}, f32[32,128]{1,0:T(8,128)}, u32[]{:S(2)}) copy-start(f32[32,128]{1,0:T(8,128)} %get-tuple-element.16.own) | copy-start | bytes 49156
  13.8 9.1 %collective-permute-start.8 = (f32[400,128]{1,0:T(8,128)S(1)}, f32[400,128]{1,0:T(8,128)S(1)}, u32[]{:S(2)}, u32[]{:S(2)}) collective-permute-start(f32[400,128]{1,0:T(8,128)S(1)} %shard_map.69), channel_id=1, source_target_pairs={{0,4},{1,7},{2,6},{3,5},{4,0},{5,3},{6,2},{7,1},{8,12},{9,15},{10,... | collective-permute-start | bytes 614408 | tf_op jit(solution)/shard_map/ppermute | solution.py:264
  13.8 10.7 %copy-start.2 = (f32[200,128]{1,0:T(8,128)S(1)}, f32[200,128]{1,0:T(8,128)}, u32[]{:S(2)}) copy-start(f32[200,128]{1,0:T(8,128)} %get-tuple-element.17.refs_0_) | copy-start | bytes 307204
  13.9 4.7 %collective-permute-start.4 = (f32[128,128]{1,0:T(8,128)S(1)}, f32[128,128]{1,0:T(8,128)S(1)}, u32[]{:S(2)}, u32[]{:S(2)}) collective-permute-start(f32[128,128]{1,0:T(8,128)S(1)} %shard_map.70.refs_0_), channel_id=1, source_target_pairs={{0,8},{1,9},{2,10},{3,11},{4,12},{5,13},{6,14},{7,15},{8,0},{9,1},... | collective-permute-start | bytes 196616 | tf_op jit(solution)/shard_map/ppermute | solution.py:264
  15.4 4.9 %collective-permute-start.5 = (f32[128,128]{1,0:T(8,128)S(1)}, f32[128,128]{1,0:T(8,128)S(1)}, u32[]{:S(2)}, u32[]{:S(2)}) collective-permute-start(f32[128,128]{1,0:T(8,128)S(1)} %shard_map.70.refs_0_), channel_id=1, source_target_pairs={{0,16},{1,17},{2,18},{3,19},{4,20},{5,21},{6,22},{7,23},{8,24},{9,... | collective-permute-start | bytes 196616 | tf_op jit(solution)/shard_map/ppermute | solution.py:264
  16.9 5.2 %collective-permute-start.6 = (f32[128,128]{1,0:T(8,128)S(1)}, f32[128,128]{1,0:T(8,128)S(1)}, u32[]{:S(2)}, u32[]{:S(2)}) collective-permute-start(f32[128,128]{1,0:T(8,128)S(1)} %shard_map.70.refs_0_), channel_id=1, source_target_pairs={{0,24},{1,25},{2,26},{3,27},{4,28},{5,29},{6,30},{7,31},{8,16},{9,... | collective-permute-start | bytes 196616 | tf_op jit(solution)/shard_map/ppermute | solution.py:264
  22.1 2.5 %collective-permute-start.7 = (f32[512,128]{1,0:T(8,128)S(1)}, f32[512,128]{1,0:T(8,128)S(1)}, u32[]{:S(2)}, u32[]{:S(2)}) collective-permute-start(f32[512,128]{1,0:T(8,128)S(1)} %shard_map.71.refs_0_), channel_id=1, source_target_pairs={{0,1},{1,0},{2,3},{3,2},{4,5},{5,4},{6,7},{7,6},{8,9},{9,8},{10,11... | collective-permute-start | bytes 786440 | tf_op jit(solution)/shard_map/ppermute | solution.py:264
  22.9 1.6 %collective-permute-start.10 = (f32[400,128]{1,0:T(8,128)S(1)}, f32[400,128]{1,0:T(8,128)S(1)}, u32[]{:S(2)}, u32[]{:S(2)}) collective-permute-start(f32[400,128]{1,0:T(8,128)S(1)} %collective-permute-done.8.refs_2_), channel_id=1, source_target_pairs={{0,1},{1,0},{2,3},{3,2},{4,5},{5,4},{6,7},{7,6},{8,9},{9,8},{10,11... | collective-permute-start | bytes 614408 | tf_op jit(solution)/shard_map/ppermute | solution.py:264
  22.9 1.6 %collective-permute-start.9 = (f32[200,128]{1,0:T(8,128)S(1)}, f32[200,128]{1,0:T(8,128)S(1)}, u32[]{:S(2)}, u32[]{:S(2)}) collective-permute-start(f32[200,128]{1,0:T(8,128)S(1)} %collective-permute-done.1.bulk.refs_1_), channel_id=1, source_target_pairs={{0,1},{1,0},{2,3},{3,2},{4,5},{5,4},{6,7},{7,6},{8,9},{9,8},{10,11... | collective-permute-start | bytes 307208 | tf_op jit(solution)/shard_map/ppermute | solution.py:264
  25.8 5.0 %collective-permute-start.13 = (f32[256,128]{1,0:T(8,128)S(1)}, f32[256,128]{1,0:T(8,128)S(1)}, u32[]{:S(2)}, u32[]{:S(2)}) collective-permute-start(f32[256,128]{1,0:T(8,128)S(1)} %get-tuple-element.29), channel_id=1, source_target_pairs={{0,8},{1,17},{2,10},{3,19},{4,12},{5,21},{6,14},{7,23},{8,0},{9,25... | collective-permute-start | bytes 393224 | tf_op jit(solution)/shard_map/ppermute | solution.py:264
  27.3 5.1 %collective-permute-start.11 = (f32[256,128]{1,0:T(8,128)S(1)}, f32[256,128]{1,0:T(8,128)S(1)}, u32[]{:S(2)}, u32[]{:S(2)}) collective-permute-start(f32[256,128]{1,0:T(8,128)S(1)} %get-tuple-element.28), channel_id=1, source_target_pairs={{0,8},{1,17},{2,10},{3,19},{4,12},{5,21},{6,14},{7,23},{8,0},{9,25... | collective-permute-start | bytes 393224 | tf_op jit(solution)/shard_map/ppermute | solution.py:264
  30.8 5.0 %copy-start = (f32[64,2,512]{2,1,0:T(2,128)S(1)}, f32[64,2,512]{2,1,0:T(2,128)}, u32[]{:S(2)}) copy-start(f32[64,2,512]{2,1,0:T(2,128)} %param.9) | copy-start | bytes 786436
  30.8 5.0 %collective-permute-start.14 = (f32[256,128]{1,0:T(8,128)S(1)}, f32[256,128]{1,0:T(8,128)S(1)}, u32[]{:S(2)}, u32[]{:S(2)}) collective-permute-start(f32[256,128]{1,0:T(8,128)S(1)} %add.7.one), channel_id=1, source_target_pairs={{0,16},{1,9},{2,18},{3,11},{4,20},{5,13},{6,22},{7,15},{8,24},{9,1... | collective-permute-start | bytes 393224 | tf_op jit(solution)/shard_map/ppermute | solution.py:264
  32.4 5.0 %collective-permute-start.12 = (f32[256,128]{1,0:T(8,128)S(1)}, f32[256,128]{1,0:T(8,128)S(1)}, u32[]{:S(2)}, u32[]{:S(2)}) collective-permute-start(f32[256,128]{1,0:T(8,128)S(1)} %add.6.one), channel_id=1, source_target_pairs={{0,16},{1,9},{2,18},{3,11},{4,20},{5,13},{6,22},{7,15},{8,24},{9,1... | collective-permute-start | bytes 393224 | tf_op jit(solution)/shard_map/ppermute | solution.py:264

commit v3 on v2

--- a/solution.py
+++ b/solution.py
@@ -17,10 +17,6 @@
 
 def room(*arrays):
     return pltpu.CompilerParams(vmem_limit_bytes=8 * sum(math.prod(a.shape) for a in arrays) + (1 << 20))
-
-
-def cheap():
-    return pl.CostEstimate(flops=1, bytes_accessed=1, transcendentals=0)
 
 
 def exact(a, b, contract):
@@ -120,9 +116,7 @@
     return r, lax.div(c, CORES), lax.rem(c, CORES)
 
 
-def pack_kernel(n, factor_h, listed_h, inv_h, pattern_h, bulk, *rest):
-    smalls = rest[: n.n_z - 1]
-    factor, listed_t, inv_t, pattern_t, wide_l, sems = rest[n.n_z - 1 :]
+def pack_kernel(n, factor_h, listed_h, inv_h, pattern_h, bulk, small, factor, listed_t, inv_t, pattern_t, wide_l, sems):
     pairs = ((factor_h, factor), (listed_h, listed_t), (inv_h, inv_t), (pattern_h, pattern_t))
     copies = [pltpu.make_async_copy(a, b, sems.at[i]) for i, (a, b) in enumerate(pairs)]
     for copy in copies:
@@ -151,26 +145,38 @@
         for p in range(n.pattern[0]):
             keep = jnp.where(tile == p, pattern_t[q : q + 1, p : p + 1].astype(jnp.float32), keep)
         bulk[pl.ds(n.m_rows + q * deep, deep), :] = inv_t[pl.ds(q * deep, deep), :] * keep
-    for s, small in zip((0, *range(CORES, n.n_z)), smalls):
-        cut(n, bulk, z ^ s, small, 0)
-
-
-def cut(n, bulk, want, out, at):
+    cut(n, bulk, 0, z, small, 0)
+
+
+def choose(core, pair):
+    return jnp.where(core == 0, pair[0], pair[1])
+
+
+def cut(n, bulk, start, want, out, at):
     for k in range(n.nodes):
         piece = None
         for t in range(n.tiles):
-            load = bulk[pl.ds(t * n.nodes + k, n.own, stride=n.slots), :]
+            load = bulk[pl.ds(start + t * n.nodes + k, n.own, stride=n.slots), :]
             piece = load if piece is None else jnp.where(want == t, load, piece)
         out[pl.ds(at + k * n.own, n.own), :] = piece
+
+
+def both_kernel(n, bulk, other, both, *smalls):
+    _, z, core = spot()
+    both[pl.ds(0, n.bulk), :] = bulk[...]
+    both[pl.ds(n.bulk, n.bulk), :] = other[...]
+    for pair, small in zip(n.pairs, smalls):
+        for i in range(CORES):
+            cut(n, both, i * n.bulk, z ^ choose(core, pair), small, i * n.small)
 
 
 def stack_kernel(n, own, bulk, *refs):
     out = refs[-1]
     _, z, _ = spot()
     out[pl.ds(0, n.small), :] = own[...]
-    cut(n, bulk, z, out, n.small)
-    for s, ref in enumerate(refs[:-1]):
-        out[pl.ds((s + CORES) * n.small, n.small), :] = ref[...]
+    cut(n, bulk, 0, z, out, n.small)
+    for p, ref in enumerate(refs[:-1]):
+        out[pl.ds((p + 1) * CORES * n.small, CORES * n.small), :] = ref[...]
 
 
 def join_kernel(n, *refs):
@@ -181,14 +187,16 @@
         at += ref.shape[0]
 
 
-def choose(core, pair):
-    return jnp.where(core == 0, pair[0], pair[1])
-
-
-def place_kernel(n, *refs):
-    half = len(refs[:-3]) // CORES
-    m_row, p_t, mask_ref = refs[-3:]
-    _, z, core = spot()
+def slots(n, z, owner):
+    found = [(z, owner), (z ^ 1, owner)]
+    for pair in n.pairs:
+        found += [(z ^ choose(owner, pair), owner ^ i) for i in range(CORES)]
+    return [a * CORES + b for a, b in found]
+
+
+def work_kernel(n, mine, theirs, bulk, other, columns, *refs):
+    *updates, m_all, m_row, p_t, mask_ref = refs
+    r, z, core = spot()
     mask_ref[...] = jnp.zeros((8, LANES), jnp.float32)
 
     def put(ref, at, c):
@@ -196,33 +204,22 @@
         p_t[pl.ds(c * n.rows_c, n.rows_c), :] = ref[pl.ds(at + n.m_rows, n.rows_c), :]
         mask_ref[...] += ref[pl.ds(at + n.m_rows + n.rows_c, 8), :]
 
-    for q in range(CORES):
-        owner = core ^ q
-        own, near, *rest = refs[q * half : (q + 1) * half]
-        put(own, 0, z * CORES + owner)
-        put(near, 0, (z ^ 1) * CORES + owner)
-        for pair, ref in zip(n.pairs, rest):
-            for i in range(CORES):
-                put(ref, i * n.bulk, (z ^ choose(owner, pair)) * CORES + (owner ^ i))
-
-
-def work_kernel(n, *refs):
-    smalls = refs[:CORES]
-    m_row, p_t, mask_ref, columns = refs[CORES : CORES + 4]
-    *updates, m_all = refs[CORES + 4 :]
-    r, z, core = spot()
     lane = lax.broadcasted_iota(jnp.int32, (n.own, LANES), 1)
     left = lane < n.wide
     first = core == 0
-    for q in range(CORES):
-        for d in range(n.n_row):
-            for s in range(n.n_z):
-                c = (z ^ s) * CORES + (core ^ q)
+    head = n.n_row * n.n_z * n.small
+    for ref, own, owner in ((mine, bulk, core), (theirs, other, core ^ 1)):
+        for s, c in enumerate(slots(n, z, owner)):
+            if s == 0:
+                put(own, 0, c)
+            else:
+                put(ref, head + (s - 1) * n.bulk, c)
+            for d in range(n.n_row):
                 at = (r ^ d) * n.span + c * n.own
                 for k in range(0, n.nodes, CORES):
                     start = (d * n.n_z + s) * n.small + k * n.own
-                    one = smalls[q][pl.ds(start, n.own), :]
-                    two = smalls[q][pl.ds(start + n.own, n.own), :]
+                    one = ref[pl.ds(start, n.own), :]
+                    two = ref[pl.ds(start + n.own, n.own), :]
                     turned = pltpu.roll(jnp.where(first, two, one), n.wide, 1)
                     both = jnp.where(left == first, jnp.where(first, one, two), turned)
                     m_all[k // CORES, pl.ds(at, n.own), :] = both
@@ -282,17 +279,16 @@
         split = array.reshape(lead, n.nodes, n.tiles, LANES)
         return jnp.transpose(split, (0, 2, 1, 3)).reshape(lead * n.slots, LANES)
 
-    taken = [view(factor), listed.T, inv_known.T, pattern.T]
-    out = [shape(n.bulk, LANES)] + [shape(n.small, LANES)] * (n.n_z - 1)
-    bulk, *smalls = pl.pallas_call(
+    taken = [pltpu.with_memory_space_constraint(a, pltpu.HBM) for a in (view(factor), listed.T, inv_known.T, pattern.T)]
+    out = [shape(n.bulk, LANES), shape(n.small, LANES)]
+    bulk, own_small = pl.pallas_call(
         functools.partial(pack_kernel, n),
         in_specs=[pl.BlockSpec(memory_space=pltpu.HBM)] * 4,
-        out_specs=[VMEM] * len(out),
+        out_specs=[VMEM] * 2,
         out_shape=out,
         scratch_shapes=[pltpu.VMEM(a.shape, a.dtype) for a in taken]
         + [pltpu.VMEM((8, LANES), jnp.float32), pltpu.SemaphoreType.DMA((len(taken),))],
-
-        cost_estimate=cheap(),
+        compiler_params=room(*out, *taken),
     )(*taken)
 
     def join(*arrays):
@@ -309,36 +305,36 @@
         return route(array, lambda r, z, core: (r, z ^ pair[core], core))
 
     near = over_z(bulk, 1)
-    far = [over_z(small, s) for s, small in zip(range(CORES, n.n_z), smalls[1:])]
     other = over_core(bulk)
-    both, near, far = lax.optimization_barrier((join(bulk, other), near, far))
+    out = [shape(CORES * n.bulk, LANES)] + [shape(CORES * n.small, LANES)] * len(n.pairs)
+    both, *far = pl.pallas_call(
+        functools.partial(both_kernel, n),
+        in_specs=[VMEM] * 2,
+        out_specs=[VMEM] * len(out),
+        out_shape=out,
+        compiler_params=room(*out),
+    )(bulk, other)
+    far = [over_pair_z(small, pair) for small, pair in zip(far, n.pairs)]
+    both, near, far = lax.optimization_barrier((both, near, far))
     out = shape(n.n_z * n.small, LANES)
     small = pl.pallas_call(
         functools.partial(stack_kernel, n),
-        in_specs=[VMEM] * n.n_z,
+        in_specs=[VMEM] * (2 + len(far)),
         out_specs=VMEM,
         out_shape=out,
         compiler_params=room(out),
-    )(smalls[0], near, *far)
+    )(own_small, near, *far)
     bulks = [over_pair_z(both, pair) for pair in n.pairs]
     spread = [over_row(small, d) for d in range(1, n.n_row)]
-    bulks = [bulk, near, *bulks]
-    other_bulks = [other] + [over_core(b) for b in bulks[1:]]
-    spread = join(small, *spread)
-    spread = [spread, over_core(spread)]
-    taken = [*bulks, *other_bulks]
-    out = [shape(n.span * n.slots, LANES), shape(n.n_col * n.rows_c, LANES), shape(8, LANES)]
-    placed = pl.pallas_call(
-        functools.partial(place_kernel, n),
-        in_specs=[VMEM] * len(taken),
-        out_specs=[VMEM] * len(out),
-        out_shape=out,
-        compiler_params=room(*taken, *out),
-        cost_estimate=cheap(),
-    )(*taken)
-    taken = [*spread, *placed]
+    mine = join(small, *spread, near, *bulks)
+    taken = [mine, over_core(mine), bulk, other]
     out = [shape(n.wide * n.nodes, LANES)] + [shape(n.wide * n.slots // CHUNKS, LANES)] * CHUNKS
-    scratch = [shape(n.nodes // CORES, n.total, LANES)]
+    scratch = [
+        shape(n.nodes // CORES, n.total, LANES),
+        shape(n.span * n.slots, LANES),
+        shape(n.n_col * n.rows_c, LANES),
+        shape(8, LANES),
+    ]
     columns, *updates = pl.pallas_call(
         functools.partial(work_kernel, n),
         in_specs=[VMEM] * len(taken),
@@ -346,7 +342,6 @@
         out_shape=out,
         scratch_shapes=[pltpu.VMEM(a.shape, a.dtype) for a in scratch],
         compiler_params=room(*taken, *out, *scratch),
-        cost_estimate=cheap(),
     )(*taken)
     for i in range(len(steps) - 1):
         updates = [update + over_pair(update, i) for update in updates]

time: 38.3 us -> 36.6 us (0.956)
  waiting for transfers between devices: 17.2 us -> 14.6 us
  starting transfers between devices: 15 us -> 17.4 us
  local copies, waits for them, and re-layouts: 0.91 us -> 0.01 us
  Pallas kernels: 4.35 us -> 3.69 us
    ppermute x15 -> x12, waiting for transfers between devices: 17.2 us -> 14.6 us  [route(): return lax.ppermute(array, AXES, pairs)]
    ppermute x15 -> x12, starting transfers between devices: 15 us -> 17.4 us  [route(): return lax.ppermute(array, AXES, pairs)]
    unnamed x8 -> x2, local copies, waits for them, and re-layouts: 0.91 us -> 0.01 us
    pallas_call x1, Pallas kernels: 1.65 us -> 1.01 us  [fast(): pl.pallas_call(functools.partial(pack_kernel, n), in_specs=[pl.BlockSpec(...]
  transfers between devices with their start and end apart: 15 -> 12, of which waited for: 10 -> 10; matrix products, arithmetic and copies ran while one was open for 0% -> 0% of each run, Pallas kernels for 2% -> 2%
where the time goes in v3:
time: 36.6 us; the launch traced here: 36.4 us
  starting transfers between devices  17.4 us (48%)
  waiting for transfers between devices  14.6 us (40%)
  Pallas kernels  3.69 us (10%)
  between operations  0.69 us (2%)
    ppermute x12, starting transfers between devices, route(): return lax.ppermute(array, AXES, pairs)  17.4 us
    ppermute x12, waiting for transfers between devices, route(): return lax.ppermute(array, AXES, pairs)  14.6 us
    pallas_call x2, Pallas kernels, fast(): pl.pallas_call(functools.partial(finish_kernel, h), in_specs=[VMEM] * 3 +...  1.37 us
    pallas_call x1, Pallas kernels, fast(): pl.pallas_call(functools.partial(work_kernel, n), in_specs=[VMEM] * len(t...  1.22 us
    pallas_call x1, Pallas kernels, fast(): pl.pallas_call(functools.partial(pack_kernel, n), in_specs=[pl.BlockSpec(...  1.01 us
  transfers between devices with their start and end apart: 12, of which 10 were waited for; matrix products, arithmetic and copies ran while one was open for 0% of the time, Pallas kernels for 2%

profile of v3, /device:TPU:0, one launch (start us, length us, event | category | flops | bytes accessed | tf_op | source)
XLA Modules:
  0.0 36.4 jit_solution(7473561268992381972)
XLA Ops:
  0.6 1.0 %shard_map.68 = (f32[200,128]{1,0:T(8,128)S(1)}, f32[32,128]{1,0:T(8,128)S(1)}) custom-call(f32[128,128]{1,0:T(8,128)} %bitcast.22, s32[2,16]{1,0:T(2,128)} %bitcast.24, f32[64,128]{1,0:T(8,128)} %bitcast.23, s32[1,2]{1,0:T(1,128)} %bitcast.25), custom_call_target="tpu_custom_call" | custom-call | tf_op jit(solution)/shard_map/pallas_call | solution.py:284
  1.6 0.5 %collective-permute-start = (f32[200,128]{1,0:T(8,128)S(1)}, f32[200,128]{1,0:T(8,128)S(1)}, u32[]{:S(2)}, u32[]{:S(2)}) collective-permute-start(f32[200,128]{1,0:T(8,128)S(1)} %get-tuple-element.13.bulk), channel_id=1, source_target_pairs={{0,1},{1,0},{2,3},{3,2},{4,5},{5,4},{6,7},{7,6},{8,9},{9,8},{10,11... | collective-permute-start | bytes 307208 | tf_op jit(solution)/shard_map/ppermute | solution.py:261
  2.2 2.6 %collective-permute-start.1 = (f32[200,128]{1,0:T(8,128)S(1)}, f32[200,128]{1,0:T(8,128)S(1)}, u32[]{:S(2)}, u32[]{:S(2)}) collective-permute-start(f32[200,128]{1,0:T(8,128)S(1)} %get-tuple-element.13.bulk), channel_id=1, source_target_pairs={{0,2},{1,3},{2,0},{3,1},{4,6},{5,7},{6,4},{7,5},{8,10},{9,11},{10,... | collective-permute-start | bytes 307208 | tf_op jit(solution)/shard_map/ppermute | solution.py:261
  4.8 0.0 collective-permute-done.other
  4.9 2.7 %collective-permute-start.2 = (f32[64,128]{1,0:T(8,128)S(1)}, f32[64,128]{1,0:T(8,128)S(1)}, u32[]{:S(2)}, u32[]{:S(2)}) collective-permute-start(f32[64,128]{1,0:T(8,128)S(1)} %get-tuple-element.15), channel_id=1, source_target_pairs={{0,4},{1,7},{2,6},{3,5},{4,0},{5,3},{6,2},{7,1},{8,12},{9,15},{10,... | collective-permute-start | bytes 98312 | tf_op jit(solution)/shard_map/ppermute | solution.py:261
  7.5 0.8 %collective-permute-done.1.bulk.refs_4_ = f32[200,128]{1,0:T(8,128)S(1)} collective-permute-done((f32[200,128]{1,0:T(8,128)S(1)}, f32[200,128]{1,0:T(8,128)S(1)}, u32[]{:S(2)}, u32[]{:S(2)}) %collective-permute-start.1) | collective-permute-done | bytes 102432 | tf_op jit(solution)/shard_map/ppermute | solution.py:261
  8.3 1.4 %collective-permute-done.2.refs_0_ = f32[64,128]{1,0:T(8,128)S(1)} collective-permute-done((f32[64,128]{1,0:T(8,128)S(1)}, f32[64,128]{1,0:T(8,128)S(1)}, u32[]{:S(2)}, u32[]{:S(2)}) %collective-permute-start.2) | collective-permute-done | bytes 32800 | tf_op jit(solution)/shard_map/ppermute | solution.py:261
  9.7 2.9 %collective-permute-start.6 = (f32[400,128]{1,0:T(8,128)S(1)}, f32[400,128]{1,0:T(8,128)S(1)}, u32[]{:S(2)}, u32[]{:S(2)}) collective-permute-start(f32[400,128]{1,0:T(8,128)S(1)} %get-tuple-element.18), channel_id=1, source_target_pairs={{0,4},{1,7},{2,6},{3,5},{4,0},{5,3},{6,2},{7,1},{8,12},{9,15},{10,... | collective-permute-start | bytes 614408 | tf_op jit(solution)/shard_map/ppermute | solution.py:261
  12.6 2.5 %collective-permute-start.5 = (f32[128,128]{1,0:T(8,128)S(1)}, f32[128,128]{1,0:T(8,128)S(1)}, u32[]{:S(2)}, u32[]{:S(2)}) collective-permute-start(f32[128,128]{1,0:T(8,128)S(1)} %shard_map.70.refs_0_), channel_id=1, source_target_pairs={{0,24},{1,25},{2,26},{3,27},{4,28},{5,29},{6,30},{7,31},{8,16},{9,... | collective-permute-start | bytes 196616 | tf_op jit(solution)/shard_map/ppermute | solution.py:261
  15.2 0.5 %collective-permute-start.4 = (f32[128,128]{1,0:T(8,128)S(1)}, f32[128,128]{1,0:T(8,128)S(1)}, u32[]{:S(2)}, u32[]{:S(2)}) collective-permute-start(f32[128,128]{1,0:T(8,128)S(1)} %shard_map.70.refs_0_), channel_id=1, source_target_pairs={{0,16},{1,17},{2,18},{3,19},{4,20},{5,21},{6,22},{7,23},{8,24},{9,... | collective-permute-start | bytes 196616 | tf_op jit(solution)/shard_map/ppermute | solution.py:261
  15.7 0.5 %collective-permute-start.3 = (f32[128,128]{1,0:T(8,128)S(1)}, f32[128,128]{1,0:T(8,128)S(1)}, u32[]{:S(2)}, u32[]{:S(2)}) collective-permute-start(f32[128,128]{1,0:T(8,128)S(1)} %shard_map.70.refs_0_), channel_id=1, source_target_pairs={{0,8},{1,9},{2,10},{3,11},{4,12},{5,13},{6,14},{7,15},{8,0},{9,1},... | collective-permute-start | bytes 196616 | tf_op jit(solution)/shard_map/ppermute | solution.py:261
  16.2 1.7 %collective-permute-done.5.refs_3_ = f32[128,128]{1,0:T(8,128)S(1)} collective-permute-done((f32[128,128]{1,0:T(8,128)S(1)}, f32[128,128]{1,0:T(8,128)S(1)}, u32[]{:S(2)}, u32[]{:S(2)}) %collective-permute-start.5) | collective-permute-done | bytes 65568 | tf_op jit(solution)/shard_map/ppermute | solution.py:261
  17.9 1.5 %collective-permute-done.4.refs_2_ = f32[128,128]{1,0:T(8,128)S(1)} collective-permute-done((f32[128,128]{1,0:T(8,128)S(1)}, f32[128,128]{1,0:T(8,128)S(1)}, u32[]{:S(2)}, u32[]{:S(2)}) %collective-permute-start.4) | collective-permute-done | bytes 65568 | tf_op jit(solution)/shard_map/ppermute | solution.py:261
  19.4 0.5 %collective-permute-done.3.refs_1_ = f32[128,128]{1,0:T(8,128)S(1)} collective-permute-done((f32[128,128]{1,0:T(8,128)S(1)}, f32[128,128]{1,0:T(8,128)S(1)}, u32[]{:S(2)}, u32[]{:S(2)}) %collective-permute-start.3) | collective-permute-done | bytes 65568 | tf_op jit(solution)/shard_map/ppermute | solution.py:261
  19.9 0.9 %collective-permute-done.6.refs_5_ = f32[400,128]{1,0:T(8,128)S(1)} collective-permute-done((f32[400,128]{1,0:T(8,128)S(1)}, f32[400,128]{1,0:T(8,128)S(1)}, u32[]{:S(2)}, u32[]{:S(2)}) %collective-permute-start.6) | collective-permute-done | bytes 204832 | tf_op jit(solution)/shard_map/ppermute | solution.py:261
  20.8 0.1 collective-permute-start.7
  20.9 2.0 %collective-permute-done.7.theirs = f32[1112,128]{1,0:T(8,128)S(1)} collective-permute-done((f32[1112,128]{1,0:T(8,128)S(1)}, f32[1112,128]{1,0:T(8,128)S(1)}, u32[]{:S(2)}, u32[]{:S(2)}) %collective-permute-start.7) | collective-permute-done | bytes 569376 | tf_op jit(solution)/shard_map/ppermute | solution.py:261
  22.9 1.2 %shard_map.72 = (f32[128,128]{1,0:T(8,128)}, f32[256,128]{1,0:T(8,128)S(1)}, f32[256,128]{1,0:T(8,128)S(1)}) custom-call(f32[1112,128]{1,0:T(8,128)S(1)} %shard_map.71.mine, f32[1112,128]{1,0:T(8,128)S(1)} %collective-permute-done.7.theirs, f32[200,128]{1,0:T(8,128)S(1)} %get-tuple-element.13.bulk, f32[200,128]{1,0:T(8,128)S(1)} %collective-permute-done.other), custom_call_target="tpu_custom_call" | custom-call | tf_op jit(solution)/shard_map/pallas_call | solution.py:338
  24.1 1.5 %collective-permute-start.10 = (f32[256,128]{1,0:T(8,128)S(1)}, f32[256,128]{1,0:T(8,128)S(1)}, u32[]{:S(2)}, u32[]{:S(2)}) collective-permute-start(f32[256,128]{1,0:T(8,128)S(1)} %get-tuple-element.21), channel_id=1, source_target_pairs={{0,8},{1,17},{2,10},{3,19},{4,12},{5,21},{6,14},{7,23},{8,0},{9,25... | collective-permute-start | bytes 393224 | tf_op jit(solution)/shard_map/ppermute | solution.py:261
  25.6 0.5 %collective-permute-start.8 = (f32[256,128]{1,0:T(8,128)S(1)}, f32[256,128]{1,0:T(8,128)S(1)}, u32[]{:S(2)}, u32[]{:S(2)}) collective-permute-start(f32[256,128]{1,0:T(8,128)S(1)} %get-tuple-element.20), channel_id=1, source_target_pairs={{0,8},{1,17},{2,10},{3,19},{4,12},{5,21},{6,14},{7,23},{8,0},{9,25... | collective-permute-start | bytes 393224 | tf_op jit(solution)/shard_map/ppermute | solution.py:261
  26.1 2.9 %collective-permute-done.10 = f32[256,128]{1,0:T(8,128)S(1)} collective-permute-done((f32[256,128]{1,0:T(8,128)S(1)}, f32[256,128]{1,0:T(8,128)S(1)}, u32[]{:S(2)}, u32[]{:S(2)}) %collective-permute-start.10) | collective-permute-done | bytes 131104 | tf_op jit(solution)/shard_map/ppermute | solution.py:261
  29.1 0.0 copy-start
  29.1 1.6 %collective-permute-start.11 = (f32[256,128]{1,0:T(8,128)S(1)}, f32[256,128]{1,0:T(8,128)S(1)}, u32[]{:S(2)}, u32[]{:S(2)}) collective-permute-start(f32[256,128]{1,0:T(8,128)S(1)} %add.7.one), channel_id=1, source_target_pairs={{0,16},{1,9},{2,18},{3,11},{4,20},{5,13},{6,22},{7,15},{8,24},{9,1... | collective-permute-start | bytes 393224 | tf_op jit(solution)/shard_map/ppermute | solution.py:261
  30.7 0.0 collective-permute-done.8
  30.7 1.5 %collective-permute-start.9 = (f32[256,128]{1,0:T(8,128)S(1)}, f32[256,128]{1,0:T(8,128)S(1)}, u32[]{:S(2)}, u32[]{:S(2)}) collective-permute-start(f32[256,128]{1,0:T(8,128)S(1)} %add.6.one), channel_id=1, source_target_pairs={{0,16},{1,9},{2,18},{3,11},{4,20},{5,13},{6,22},{7,15},{8,24},{9,1... | collective-permute-start | bytes 393224 | tf_op jit(solution)/shard_map/ppermute | solution.py:261
  32.2 2.0 %collective-permute-done.11.two = f32[256,128]{1,0:T(8,128)S(1)} collective-permute-done((f32[256,128]{1,0:T(8,128)S(1)}, f32[256,128]{1,0:T(8,128)S(1)}, u32[]{:S(2)}, u32[]{:S(2)}) %collective-permute-start.11) | collective-permute-done | bytes 131104 | tf_op jit(solution)/shard_map/ppermute | solution.py:261
  34.1 0.0 copy-done
  34.1 0.7 %shard_map.73.refs_0_ = f32[512,128]{1,0:T(8,128)} custom-call(f32[512,128]{1,0:T(8,128)S(1)} %bitcast.19, f32[256,128]{1,0:T(8,128)S(1)} %add.7.one, f32[256,128]{1,0:T(8,128)S(1)} %collective-permute-done.11.two), custom_call_target="tpu_custom_call" | custom-call | tf_op jit(solution)/shard_map/pallas_call | solution.py:353
  34.8 0.9 %collective-permute-done.9.two = f32[256,128]{1,0:T(8,128)S(1)} collective-permute-done((f32[256,128]{1,0:T(8,128)S(1)}, f32[256,128]{1,0:T(8,128)S(1)}, u32[]{:S(2)}, u32[]{:S(2)}) %collective-permute-start.9) | collective-permute-done | bytes 131104 | tf_op jit(solution)/shard_map/ppermute | solution.py:261
  35.7 0.7 %shard_map.74 = f32[512,128]{1,0:T(8,128)} custom-call(f32[512,128]{1,0:T(8,128)S(1)} %bitcast.20, f32[256,128]{1,0:T(8,128)S(1)} %add.6.one, f32[256,128]{1,0:T(8,128)S(1)} %collective-permute-done.9.two, f32[512,128]{1,0:T(8,128)} %shard_map.73.refs_0_), custom_call_target="tpu_custom_call", output_to_operand_aliasing={{}: (3, {})} | custom-call | tf_op jit(solution)/shard_map/pallas_call | solution.py:353
  (5 shorter events, 0.1 us)
Async XLA Ops:
  1.6 3.2 %collective-permute-start = (f32[200,128]{1,0:T(8,128)S(1)}, f32[200,128]{1,0:T(8,128)S(1)}, u32[]{:S(2)}, u32[]{:S(2)}) collective-permute-start(f32[200,128]{1,0:T(8,128)S(1)} %get-tuple-element.13.bulk), channel_id=1, source_target_pairs={{0,1},{1,0},{2,3},{3,2},{4,5},{5,4},{6,7},{7,6},{8,9},{9,8},{10,11... | collective-permute-start | bytes 307208 | tf_op jit(solution)/shard_map/ppermute | solution.py:261
  2.2 6.1 %collective-permute-start.1 = (f32[200,128]{1,0:T(8,128)S(1)}, f32[200,128]{1,0:T(8,128)S(1)}, u32[]{:S(2)}, u32[]{:S(2)}) collective-permute-start(f32[200,128]{1,0:T(8,128)S(1)} %get-tuple-element.13.bulk), channel_id=1, source_target_pairs={{0,2},{1,3},{2,0},{3,1},{4,6},{5,7},{6,4},{7,5},{8,10},{9,11},{10,... | collective-permute-start | bytes 307208 | tf_op jit(solution)/shard_map/ppermute | solution.py:261
  4.9 4.9 %collective-permute-start.2 = (f32[64,128]{1,0:T(8,128)S(1)}, f32[64,128]{1,0:T(8,128)S(1)}, u32[]{:S(2)}, u32[]{:S(2)}) collective-permute-start(f32[64,128]{1,0:T(8,128)S(1)} %get-tuple-element.15), channel_id=1, source_target_pairs={{0,4},{1,7},{2,6},{3,5},{4,0},{5,3},{6,2},{7,1},{8,12},{9,15},{10,... | collective-permute-start | bytes 98312 | tf_op jit(solution)/shard_map/ppermute | solution.py:261
  9.7 11.0 %collective-permute-start.6 = (f32[400,128]{1,0:T(8,128)S(1)}, f32[400,128]{1,0:T(8,128)S(1)}, u32[]{:S(2)}, u32[]{:S(2)}) collective-permute-start(f32[400,128]{1,0:T(8,128)S(1)} %get-tuple-element.18), channel_id=1, source_target_pairs={{0,4},{1,7},{2,6},{3,5},{4,0},{5,3},{6,2},{7,1},{8,12},{9,15},{10,... | collective-permute-start | bytes 614408 | tf_op jit(solution)/shard_map/ppermute | solution.py:261
  12.6 5.3 %collective-permute-start.5 = (f32[128,128]{1,0:T(8,128)S(1)}, f32[128,128]{1,0:T(8,128)S(1)}, u32[]{:S(2)}, u32[]{:S(2)}) collective-permute-start(f32[128,128]{1,0:T(8,128)S(1)} %shard_map.70.refs_0_), channel_id=1, source_target_pairs={{0,24},{1,25},{2,26},{3,27},{4,28},{5,29},{6,30},{7,31},{8,16},{9,... | collective-permute-start | bytes 196616 | tf_op jit(solution)/shard_map/ppermute | solution.py:261
  15.2 4.3 %collective-permute-start.4 = (f32[128,128]{1,0:T(8,128)S(1)}, f32[128,128]{1,0:T(8,128)S(1)}, u32[]{:S(2)}, u32[]{:S(2)}) collective-permute-start(f32[128,128]{1,0:T(8,128)S(1)} %shard_map.70.refs_0_), channel_id=1, source_target_pairs={{0,16},{1,17},{2,18},{3,19},{4,20},{5,21},{6,22},{7,23},{8,24},{9,... | collective-permute-start | bytes 196616 | tf_op jit(solution)/shard_map/ppermute | solution.py:261
  15.7 4.3 %collective-permute-start.3 = (f32[128,128]{1,0:T(8,128)S(1)}, f32[128,128]{1,0:T(8,128)S(1)}, u32[]{:S(2)}, u32[]{:S(2)}) collective-permute-start(f32[128,128]{1,0:T(8,128)S(1)} %shard_map.70.refs_0_), channel_id=1, source_target_pairs={{0,8},{1,9},{2,10},{3,11},{4,12},{5,13},{6,14},{7,15},{8,0},{9,1},... | collective-permute-start | bytes 196616 | tf_op jit(solution)/shard_map/ppermute | solution.py:261
  20.8 2.0 %collective-permute-start.7 = (f32[1112,128]{1,0:T(8,128)S(1)}, f32[1112,128]{1,0:T(8,128)S(1)}, u32[]{:S(2)}, u32[]{:S(2)}) collective-permute-start(f32[1112,128]{1,0:T(8,128)S(1)} %shard_map.71.mine), channel_id=1, source_target_pairs={{0,1},{1,0},{2,3},{3,2},{4,5},{5,4},{6,7},{7,6},{8,9},{9,8},{10,11... | collective-permute-start | bytes 1708040 | tf_op jit(solution)/shard_map/ppermute | solution.py:261
  24.1 5.0 %collective-permute-start.10 = (f32[256,128]{1,0:T(8,128)S(1)}, f32[256,128]{1,0:T(8,128)S(1)}, u32[]{:S(2)}, u32[]{:S(2)}) collective-permute-start(f32[256,128]{1,0:T(8,128)S(1)} %get-tuple-element.21), channel_id=1, source_target_pairs={{0,8},{1,17},{2,10},{3,19},{4,12},{5,21},{6,14},{7,23},{8,0},{9,25... | collective-permute-start | bytes 393224 | tf_op jit(solution)/shard_map/ppermute | solution.py:261
  25.6 5.1 %collective-permute-start.8 = (f32[256,128]{1,0:T(8,128)S(1)}, f32[256,128]{1,0:T(8,128)S(1)}, u32[]{:S(2)}, u32[]{:S(2)}) collective-permute-start(f32[256,128]{1,0:T(8,128)S(1)} %get-tuple-element.20), channel_id=1, source_target_pairs={{0,8},{1,17},{2,10},{3,19},{4,12},{5,21},{6,14},{7,23},{8,0},{9,25... | collective-permute-start | bytes 393224 | tf_op jit(solution)/shard_map/ppermute | solution.py:261
  29.1 5.0 %copy-start = (f32[64,2,512]{2,1,0:T(2,128)S(1)}, f32[64,2,512]{2,1,0:T(2,128)}, u32[]{:S(2)}) copy-start(f32[64,2,512]{2,1,0:T(2,128)} %param.9) | copy-start | bytes 786436
  29.1 5.0 %collective-permute-start.11 = (f32[256,128]{1,0:T(8,128)S(1)}, f32[256,128]{1,0:T(8,128)S(1)}, u32[]{:S(2)}, u32[]{:S(2)}) collective-permute-start(f32[256,128]{1,0:T(8,128)S(1)} %add.7.one), channel_id=1, source_target_pairs={{0,16},{1,9},{2,18},{3,11},{4,20},{5,13},{6,22},{7,15},{8,24},{9,1... | collective-permute-start | bytes 393224 | tf_op jit(solution)/shard_map/ppermute | solution.py:261
  30.7 5.0 %collective-permute-start.9 = (f32[256,128]{1,0:T(8,128)S(1)}, f32[256,128]{1,0:T(8,128)S(1)}, u32[]{:S(2)}, u32[]{:S(2)}) collective-permute-start(f32[256,128]{1,0:T(8,128)S(1)} %add.6.one), channel_id=1, source_target_pairs={{0,16},{1,9},{2,18},{3,11},{4,20},{5,13},{6,22},{7,15},{8,24},{9,1... | collective-permute-start | bytes 393224 | tf_op jit(solution)/shard_map/ppermute | solution.py:261

commit v4 on v3

v4 whole, which is shorter than its diff:
```python
import functools
import math

import jax
import jax.numpy as jnp
from jax import lax
from jax.experimental import pallas as pl
from jax.experimental.pallas import tpu as pltpu
from jax.sharding import PartitionSpec as P

LANES = 128
CORES = 2
AXES = ("row", "col")
VMEM = pl.BlockSpec(memory_space=pltpu.VMEM)


def room(*arrays):
    return pltpu.CompilerParams(vmem_limit_bytes=8 * sum(math.prod(a.shape) for a in arrays) + (1 << 20))


def exact(a, b, contract):
    return lax.dot_general(
        a, b, (contract, ((), ())), precision=lax.Precision.HIGHEST, preferred_element_type=jnp.float32
    )


def halves(x):
    high = x.astype(jnp.bfloat16)
    return high, (x - high.astype(jnp.float32)).astype(jnp.bfloat16)


def product(a, b):
    (ah, al), (bh, bl) = halves(a), halves(b)

    def dot(x, y):
        return lax.dot_general(x, y, (((1,), (0,)), ((), ())), preferred_element_type=jnp.float32)

    return dot(ah, bh) + (dot(ah, bl) + dot(al, bh))


def supernode_pass(present, masked, listed_f, diag_part, ratio):
    row_block, row_listed = (
        lax.all_gather(masked, "col", axis=0, tiled=True),
        lax.all_gather(listed_f, "col", axis=0, tiled=True),
    )
    held = lax.psum_scatter(
        jnp.einsum("ij,ika->jka", present, row_block, precision=lax.Precision.HIGHEST),
        "row",
        scatter_dimension=0,
        tiled=True,
    )
    count_row = lax.axis_size("row")
    count_col = lax.axis_size("col")
    local_rows = held.shape[0]
    nodes = held.shape[1]
    narrow = held.shape[2] // count_col
    by_column = lax.all_to_all(held[None], "col", split_axis=3, concat_axis=0, tiled=True)
    grouped = by_column.reshape(count_row, 1, ratio, local_rows, nodes, narrow)
    moved = lax.all_to_all(grouped, "row", split_axis=0, concat_axis=1, tiled=True)
    ordered = jnp.transpose(moved[0], (1, 0, 2, 3, 4)).reshape(
        ratio * count_row * local_rows, nodes, narrow
    )
    summed = jnp.transpose(ordered, (2, 1, 0))
    columns = -summed * jnp.transpose(row_listed)[None, :, :]
    update = jnp.einsum("akj,jkb->akb", columns, row_block, precision=lax.Precision.HIGHEST)
    schur = diag_part - lax.psum(update, "row")
    return (columns, schur)


def general(inv_known, pattern, factor, listed, diag_inverse):
    tile = inv_known.shape[0] // pattern.shape[0]
    flags = pattern.astype(jnp.float32)
    spread = jnp.repeat(jnp.repeat(flags, tile, axis=0), tile, axis=1)
    present = inv_known * spread
    listed_f = listed.astype(jnp.float32)
    masked = factor * listed_f[:, :, None]
    ratio = lax.axis_size("col") // lax.axis_size("row")
    return supernode_pass(present, masked, listed_f, diag_inverse, ratio)


class Sizes:
    def __init__(self, inv_known, pattern, factor, diag_inverse):
        self.n_row = lax.axis_size("row")
        self.n_col = lax.axis_size("col")
        self.n_z = self.n_col // CORES
        self.own = factor.shape[0]
        self.nodes = factor.shape[1]
        self.width = factor.shape[2]
        self.tiles = self.width // LANES
        self.slots = self.tiles * self.nodes
        self.rows_r = inv_known.shape[0]
        self.rows_c = inv_known.shape[1]
        self.wide = diag_inverse.shape[0]
        self.pattern = pattern.shape
        self.span = self.n_col * self.own
        self.m_rows = self.own * self.slots
        self.bulk = self.m_rows + self.rows_c + 8
        self.total = self.n_row * self.rows_r

    def fits(self):
        return (
            self.n_col % CORES == 0
            and self.n_row == 2 * CORES
            and self.n_z == 2 * CORES
            and self.wide * CORES == LANES
            and self.rows_r == LANES
            and self.span == LANES
            and self.width % LANES == 0
            and self.slots % 8 == 0
            and self.own % 8 == 0
            and self.rows_c % 8 == 0
            and self.nodes % CORES == 0
            and self.nodes <= 8
        )


def spot():
    r = lax.axis_index("row")
    c = lax.axis_index("col")
    return r, lax.div(c, CORES), lax.rem(c, CORES)


def pack_kernel(n, factor_h, listed_h, inv_h, pattern_h, bulk, factor, listed_t, inv_t, pattern_t, wide_l, sems):
    pairs = ((factor_h, factor), (listed_h, listed_t), (inv_h, inv_t), (pattern_h, pattern_t))
    copies = [pltpu.make_async_copy(a, b, sems.at[i]) for i, (a, b) in enumerate(pairs)]
    for copy in copies:
        copy.start()
    for copy in copies:
        copy.wait()
    _, z, core = spot()
    col = z * CORES + core
    wide_l[...] = jnp.zeros((8, LANES), jnp.float32)
    wide_l[pl.ds(0, n.nodes), pl.ds(0, n.own)] = listed_t[...].astype(jnp.float32)
    flags = wide_l[...]
    row = lax.broadcasted_iota(jnp.int32, (n.m_rows, LANES), 0)
    lane = lax.broadcasted_iota(jnp.int32, (n.m_rows, LANES), 1)
    node = lax.rem(row, n.nodes)
    mine = jnp.zeros((n.m_rows, LANES), jnp.float32)
    for k in range(n.nodes):
        mine = jnp.where(node == k, flags[k : k + 1, :], mine)
    keep = jnp.sum(jnp.where(lane == lax.div(row, n.slots), mine, 0.0), axis=1, keepdims=True)
    bulk[pl.ds(0, n.m_rows), :] = factor[...] * keep
    bulk[pl.ds(n.m_rows + n.rows_c, 8), :] = pltpu.roll(flags, col * n.own, 1)
    high = n.rows_r // n.pattern[0]
    deep = n.rows_c // n.pattern[1]
    tile = lax.div(lax.broadcasted_iota(jnp.int32, (1, LANES), 1), high)
    for q in range(n.pattern[1]):
        keep = jnp.zeros((1, LANES), jnp.float32)
        for p in range(n.pattern[0]):
            keep = jnp.where(tile == p, pattern_t[q : q + 1, p : p + 1].astype(jnp.float32), keep)
        bulk[pl.ds(n.m_rows + q * deep, deep), :] = inv_t[pl.ds(q * deep, deep), :] * keep


def join_kernel(n, *refs):
    out = refs[-1]
    at = 0
    for ref in refs[:-1]:
        out[pl.ds(at, ref.shape[0]), :] = ref[...]
        at += ref.shape[0]


def cut_kernel(n, low, f_outer, s_outer, f_far, s_far, one, two):
    one[pl.ds(0, n.bulk), :] = f_outer[pl.ds(0, n.bulk), :]
    one[pl.ds(n.bulk, low), :] = f_far[pl.ds(0, low), :]
    two[pl.ds(0, n.bulk - low), :] = s_far[pl.ds(low, n.bulk - low), :]
    two[pl.ds(n.bulk - low, n.bulk), :] = s_outer[pl.ds(n.bulk, n.bulk), :]


def put(n, ref, at, r2, c2, m_all, m_sel, p_t, mask):
    _, z, core = spot()
    first = core == 0
    left = lax.broadcasted_iota(jnp.int32, (n.own, LANES), 1) < n.wide
    row = r2 * n.span + c2 * n.own
    m_all[pl.ds(row * n.slots, n.m_rows), :] = ref[pl.ds(at, n.m_rows), :]
    p_t[r2, pl.ds(c2 * n.rows_c, n.rows_c), :] = ref[pl.ds(at + n.m_rows, n.rows_c), :]
    mask[r2, c2] = ref[pl.ds(at + n.m_rows + n.rows_c, 8), :]
    for k in range(0, n.nodes, CORES):
        pair = []
        for i in range(CORES):
            piece = None
            for t in range(n.tiles):
                load = ref[pl.ds(at + t * n.nodes + k + i, n.own, stride=n.slots), :]
                piece = load if piece is None else jnp.where(z == t, load, piece)
            pair.append(piece)
        one, two = pair
        turned = pltpu.roll(jnp.where(first, two, one), n.wide, 1)
        m_sel[k // CORES, pl.ds(row, n.own), :] = jnp.where(left == first, jnp.where(first, one, two), turned)


def fill(n, pieces, mine, theirs, *refs):
    r, z, core = spot()
    for ref, owner in ((mine, core), (theirs, core ^ 1)):
        at = 0
        for shift, shells in pieces:
            for s in shells:
                put(n, ref, at, r ^ choose(owner, shift), (z ^ s) * CORES + owner, *refs)
                at += n.bulk


def fill_kernel(n, pieces, *refs):
    count = len(pieces)
    for i, group in enumerate(pieces):
        fill(n, group, refs[i], refs[count + i], *refs[2 * count :])


def work_kernel(n, pieces, mine, theirs, *refs):
    diag, columns, schur, *store = refs[4:]
    fill(n, pieces, mine, theirs, *store)
    m_all, m_sel, p_t, masks = store
    r, _, _ = spot()
    mask = []
    for i in range(n.n_row):
        total = masks[i, 0]
        for c in range(1, n.n_col):
            total += masks[i, c]
        mask.append(total)
    p_all = jnp.concatenate([p_t[i] for i in range(n.n_row)], axis=1)
    for k in range(n.nodes):
        if k % CORES == 0:
            x_t = product(m_sel[k // CORES].T, p_all)
        at = k % CORES * n.wide
        spread = jnp.concatenate([m[k : k + 1, :] for m in mask], axis=1)
        part = -x_t[at : at + n.wide, :] * spread
        own = part[:, :LANES]
        for i in range(1, n.n_row):
            own = jnp.where(r == i, part[:, i * LANES : (i + 1) * LANES], own)
        columns[pl.ds(k, n.wide, stride=n.nodes), :] = own
        sides = [m_all[pl.ds(t * n.nodes + k, n.total, stride=n.slots), :] for t in range(n.tiles)]
        wide = product(part, jnp.concatenate(sides, axis=1))
        for t in range(n.tiles):
            line = pl.ds(t * n.nodes + k, n.wide, stride=n.slots)
            schur[line, :] = diag[line, :] - wide[:, t * LANES : (t + 1) * LANES]


def choose(core, pair):
    return jnp.where(core == 0, pair[0], pair[1])


def fast(n, inv_known, pattern, factor, listed, diag_inverse):
    def shape(*dims):
        return jax.ShapeDtypeStruct(dims, jnp.float32)

    def route(array, change):
        pairs = []
        for r in range(n.n_row):
            for z in range(n.n_z):
                for core in range(CORES):
                    r2, z2, core2 = change(r, z, core)
                    pairs.append(((r * n.n_z + z) * CORES + core, (r2 * n.n_z + z2) * CORES + core2))
        return lax.ppermute(array, AXES, pairs)

    def over_z(array, s):
        return route(array, lambda r, z, core: (r, z ^ s, core))

    def over_core(array):
        return route(array, lambda r, z, core: (r, z, core ^ 1))

    steps = [1 << i for i in range(n.n_row.bit_length() - 1)]

    def over_pair(array, i):
        return route(array, lambda r, z, core: (r ^ (steps[i] if core == 0 else steps[-1 - i]), z, core))

    def view(array):
        lead = array.shape[0]
        split = array.reshape(lead, n.nodes, n.tiles, LANES)
        return jnp.transpose(split, (0, 2, 1, 3)).reshape(lead * n.slots, LANES)

    taken = [pltpu.with_memory_space_constraint(a, pltpu.HBM) for a in (view(factor), listed.T, inv_known.T, pattern.T)]
    out = shape(n.bulk, LANES)
    bulk = pl.pallas_call(
        functools.partial(pack_kernel, n),
        in_specs=[pl.BlockSpec(memory_space=pltpu.HBM)] * 4,
        out_specs=VMEM,
        out_shape=out,
        scratch_shapes=[pltpu.VMEM(a.shape, a.dtype) for a in taken]
        + [pltpu.VMEM((8, LANES), jnp.float32), pltpu.SemaphoreType.DMA((len(taken),))],
        compiler_params=room(out, *taken),
    )(*taken)

    def join(*arrays):
        out = shape(sum(a.shape[0] for a in arrays), LANES)
        return pl.pallas_call(
            functools.partial(join_kernel, n),
            in_specs=[VMEM] * len(arrays),
            out_specs=VMEM,
            out_shape=out,
            compiler_params=room(out),
        )(*arrays)

    one, two = steps
    side, turn, both = (one, two), (two, one), (one ^ two, one ^ two)
    near, across = 1, n.n_z - 1
    z1, z3 = over_z(bulk, near), over_z(bulk, across)
    z2 = over_z(z1, across)
    early = [bulk, over_pair(bulk, 0), over_pair(bulk, 1)]
    early.append(over_pair(early[1], 1))
    early, z1, z3 = lax.optimization_barrier((early, z1, z3))
    outer = join(z1, z3)
    trip = [over_pair(outer, 0), over_pair(outer, 1), over_pair(z2, 0), over_pair(z2, 1)]
    trip = lax.optimization_barrier(trip)
    low = (n.bulk // 2 + 7) // 8 * 8
    out = [shape(n.bulk + low, LANES), shape(2 * n.bulk - low, LANES)]
    ends = pl.pallas_call(
        functools.partial(cut_kernel, n, low),
        in_specs=[VMEM] * 4,
        out_specs=[VMEM] * 2,
        out_shape=out,
        compiler_params=room(*out),
    )(*trip)
    last = join(over_pair(ends[0], 1), over_pair(ends[1], 0))
    part = [join(*early, outer, z2)]
    part.append(join(*trip))
    here = (0, 0)
    shell, beyond = (near, across), (near ^ across,)
    pieces = [(here, (0,)), (side, (0,)), (turn, (0,)), (both, (0,)), (here, shell), (here, beyond)]
    pieces = [pieces, [(side, shell), (turn, shell), (side, beyond), (turn, beyond)]]
    store = [
        shape(n.total * n.slots, LANES),
        shape(n.nodes // CORES, n.total, LANES),
        shape(n.n_row, n.n_col * n.rows_c, LANES),
        shape(n.n_row, n.n_col, 8, LANES),
    ]
    taken = [*part, *[over_core(p) for p in part]]
    placed = pl.pallas_call(
        functools.partial(fill_kernel, n, pieces),
        in_specs=[VMEM] * len(taken),
        out_specs=[VMEM] * 4,
        out_shape=store,
        compiler_params=room(*taken, *store),
    )(*taken)
    pieces = [(both, (near, near ^ across, across))]
    taken = [last, over_core(last), *placed, view(diag_inverse)]
    out = [shape(n.wide * n.nodes, LANES), shape(n.wide * n.slots, LANES), *store]
    columns, schur, *_ = pl.pallas_call(
        functools.partial(work_kernel, n, pieces),
        in_specs=[VMEM] * len(taken),
        out_specs=[VMEM] * len(out),
        out_shape=out,
        input_output_aliases={2 + i: 2 + i for i in range(4)},
        compiler_params=room(*taken, *out),
    )(*taken)
    schur = jnp.transpose(schur.reshape(n.wide, n.tiles, n.nodes, LANES), (0, 2, 1, 3))
    return columns.reshape(n.wide, n.nodes, LANES), schur.reshape(n.wide, n.nodes, n.width)


def local(inv_known, pattern, factor, listed, diag_inverse):
    n = Sizes(inv_known, pattern, factor, diag_inverse)
    plan = functools.partial(fast, n) if n.fits() else general
    return plan(inv_known, pattern, factor, listed, diag_inverse)


def solution(mesh):
    in_specs = (
        P("row", "col"),
        P("row", "col"),
        P(("row", "col"), None, None),
        P(("row", "col"), None),
        P("col", None, None),
    )
    out_specs = (P("col", None, "row"), P("col", None, None))
    return jax.shard_map(local, mesh=mesh, in_specs=in_specs, out_specs=out_specs, check_vma=False)
```

time: 36.6 us -> 34.4 us (0.940)
  waiting for transfers between devices: 14.6 us -> 11 us
  starting transfers between devices: 17.4 us -> 18.6 us
    ppermute x12 -> x15, waiting for transfers between devices: 14.6 us -> 11 us  [route(): return lax.ppermute(array, AXES, pairs)]
    ppermute x12 -> x15, starting transfers between devices: 17.4 us -> 18.6 us  [route(): return lax.ppermute(array, AXES, pairs)]
    pallas_call x5 -> x3, Pallas kernels: 2.65 us -> 2.82 us  [the longest x1 2.19 us: fast(): pl.pallas_call(functools.partial(work_kernel, n, pieces), in_specs=[VMEM]...]
  transfers between devices with their start and end apart: 12 -> 15, of which waited for: 10 -> 6; matrix products, arithmetic and copies ran while one was open for 0% -> 0% of each run, Pallas kernels for 2% -> 2%
where the time goes in v4:
time: 34.4 us; the launch traced here: 34.2 us
  starting transfers between devices  18.6 us (54%)
  waiting for transfers between devices  11 us (32%)
  Pallas kernels  3.94 us (11%)
  between operations  0.73 us (2%)
    ppermute x15, starting transfers between devices, route(): return lax.ppermute(array, AXES, pairs)  18.6 us
    ppermute x15, waiting for transfers between devices, route(): return lax.ppermute(array, AXES, pairs)  11 us
    pallas_call x1, Pallas kernels, fast(): pl.pallas_call(functools.partial(work_kernel, n, pieces), in_specs=[VMEM]...  2.19 us
    pallas_call x1, Pallas kernels, fast(): pl.pallas_call(functools.partial(pack_kernel, n), in_specs=[pl.BlockSpec(...  1 us
  transfers between devices with their start and end apart: 15, of which 6 were waited for; matrix products, arithmetic and copies ran while one was open for 0% of the time, Pallas kernels for 2%

profile of v4, /device:TPU:0, one launch (start us, length us, event | category | flops | bytes accessed | tf_op | source)
XLA Modules:
  0.0 34.2 jit_solution(6628465548300559608)
XLA Ops:
  0.6 1.0 %shard_map.68.refs_0_ = f32[200,128]{1,0:T(8,128)S(1)} custom-call(f32[128,128]{1,0:T(8,128)} %bitcast.20, s32[2,16]{1,0:T(2,128)} %bitcast.22, f32[64,128]{1,0:T(8,128)} %bitcast.21, s32[1,2]{1,0:T(1,128)} %bitcast.23), custom_call_target="tpu_custom_call" | custom-call | tf_op jit(solution)/shard_map/pallas_call | solution.py:270
  1.6 3.0 %collective-permute-start = (f32[200,128]{1,0:T(8,128)S(1)}, f32[200,128]{1,0:T(8,128)S(1)}, u32[]{:S(2)}, u32[]{:S(2)}) collective-permute-start(f32[200,128]{1,0:T(8,128)S(1)} %shard_map.68.refs_0_), channel_id=1, source_target_pairs={{0,8},{1,17},{2,10},{3,19},{4,12},{5,21},{6,14},{7,23},{8,0},{9,25... | collective-permute-start | bytes 307208 | tf_op jit(solution)/shard_map/ppermute | solution.py:250
  4.6 1.6 %collective-permute-start.3 = (f32[200,128]{1,0:T(8,128)S(1)}, f32[200,128]{1,0:T(8,128)S(1)}, u32[]{:S(2)}, u32[]{:S(2)}) collective-permute-start(f32[200,128]{1,0:T(8,128)S(1)} %shard_map.68.refs_0_), channel_id=1, source_target_pairs={{0,2},{1,3},{2,0},{3,1},{4,6},{5,7},{6,4},{7,5},{8,10},{9,11},{10,... | collective-permute-start | bytes 307208 | tf_op jit(solution)/shard_map/ppermute | solution.py:250
  6.2 2.5 %collective-permute-start.4 = (f32[200,128]{1,0:T(8,128)S(1)}, f32[200,128]{1,0:T(8,128)S(1)}, u32[]{:S(2)}, u32[]{:S(2)}) collective-permute-start(f32[200,128]{1,0:T(8,128)S(1)} %shard_map.68.refs_0_), channel_id=1, source_target_pairs={{0,6},{1,7},{2,4},{3,5},{4,2},{5,3},{6,0},{7,1},{8,14},{9,15},{10,... | collective-permute-start | bytes 307208 | tf_op jit(solution)/shard_map/ppermute | solution.py:250
  8.7 1.5 %collective-permute-start.1 = (f32[200,128]{1,0:T(8,128)S(1)}, f32[200,128]{1,0:T(8,128)S(1)}, u32[]{:S(2)}, u32[]{:S(2)}) collective-permute-start(f32[200,128]{1,0:T(8,128)S(1)} %shard_map.68.refs_0_), channel_id=1, source_target_pairs={{0,16},{1,9},{2,18},{3,11},{4,20},{5,13},{6,22},{7,15},{8,24},{9,1... | collective-permute-start | bytes 307208 | tf_op jit(solution)/shard_map/ppermute | solution.py:250
  10.2 0.0 collective-permute-done.refs_1_
  10.2 0.5 %collective-permute-start.2 = (f32[200,128]{1,0:T(8,128)S(1)}, f32[200,128]{1,0:T(8,128)S(1)}, u32[]{:S(2)}, u32[]{:S(2)}) collective-permute-start(f32[200,128]{1,0:T(8,128)S(1)} %collective-permute-done.refs_1_), channel_id=1, source_target_pairs={{0,16},{1,9},{2,18},{3,11},{4,20},{5,13},{6,22},{7,15},{8,24},{9,1... | collective-permute-start | bytes 307208 | tf_op jit(solution)/shard_map/ppermute | solution.py:250
  10.7 0.0 collective-permute-done.3.refs_0_
  10.7 3.3 %collective-permute-start.7 = (f32[200,128]{1,0:T(8,128)S(1)}, f32[200,128]{1,0:T(8,128)S(1)}, u32[]{:S(2)}, u32[]{:S(2)}) collective-permute-start(f32[200,128]{1,0:T(8,128)S(1)} %collective-permute-done.3.refs_0_), channel_id=1, source_target_pairs={{0,6},{1,7},{2,4},{3,5},{4,2},{5,3},{6,0},{7,1},{8,14},{9,15},{10,... | collective-permute-start | bytes 307208 | tf_op jit(solution)/shard_map/ppermute | solution.py:250
  14.0 0.0 collective-permute-done.4.refs_1_
  14.0 0.0 collective-permute-done.1.refs_2_
  14.0 0.9 %collective-permute-done.2.refs_3_ = f32[200,128]{1,0:T(8,128)S(1)} collective-permute-done((f32[200,128]{1,0:T(8,128)S(1)}, f32[200,128]{1,0:T(8,128)S(1)}, u32[]{:S(2)}, u32[]{:S(2)}) %collective-permute-start.2) | collective-permute-done | bytes 102432 | tf_op jit(solution)/shard_map/ppermute | solution.py:250
  14.9 1.2 %collective-permute-start.6 = (f32[400,128]{1,0:T(8,128)S(1)}, f32[400,128]{1,0:T(8,128)S(1)}, u32[]{:S(2)}, u32[]{:S(2)}) collective-permute-start(f32[400,128]{1,0:T(8,128)S(1)} %shard_map.69.refs_4_), channel_id=1, source_target_pairs={{0,16},{1,9},{2,18},{3,11},{4,20},{5,13},{6,22},{7,15},{8,24},{9,1... | collective-permute-start | bytes 614408 | tf_op jit(solution)/shard_map/ppermute | solution.py:250
  16.1 0.5 %collective-permute-start.5 = (f32[400,128]{1,0:T(8,128)S(1)}, f32[400,128]{1,0:T(8,128)S(1)}, u32[]{:S(2)}, u32[]{:S(2)}) collective-permute-start(f32[400,128]{1,0:T(8,128)S(1)} %shard_map.69.refs_4_), channel_id=1, source_target_pairs={{0,8},{1,17},{2,10},{3,19},{4,12},{5,21},{6,14},{7,23},{8,0},{9,25... | collective-permute-start | bytes 614408 | tf_op jit(solution)/shard_map/ppermute | solution.py:250
  16.6 0.7 %collective-permute-done.7.refs_5_ = f32[200,128]{1,0:T(8,128)S(1)} collective-permute-done((f32[200,128]{1,0:T(8,128)S(1)}, f32[200,128]{1,0:T(8,128)S(1)}, u32[]{:S(2)}, u32[]{:S(2)}) %collective-permute-start.7) | collective-permute-done | bytes 102432 | tf_op jit(solution)/shard_map/ppermute | solution.py:250
  17.3 1.4 %collective-permute-start.9 = (f32[200,128]{1,0:T(8,128)S(1)}, f32[200,128]{1,0:T(8,128)S(1)}, u32[]{:S(2)}, u32[]{:S(2)}) collective-permute-start(f32[200,128]{1,0:T(8,128)S(1)} %collective-permute-done.7.refs_5_), channel_id=1, source_target_pairs={{0,16},{1,9},{2,18},{3,11},{4,20},{5,13},{6,22},{7,15},{8,24},{9,1... | collective-permute-start | bytes 307208 | tf_op jit(solution)/shard_map/ppermute | solution.py:250
  18.7 0.6 %collective-permute-start.8 = (f32[200,128]{1,0:T(8,128)S(1)}, f32[200,128]{1,0:T(8,128)S(1)}, u32[]{:S(2)}, u32[]{:S(2)}) collective-permute-start(f32[200,128]{1,0:T(8,128)S(1)} %collective-permute-done.7.refs_5_), channel_id=1, source_target_pairs={{0,8},{1,17},{2,10},{3,19},{4,12},{5,21},{6,14},{7,23},{8,0},{9,25... | collective-permute-start | bytes 307208 | tf_op jit(solution)/shard_map/ppermute | solution.py:250
  19.4 0.1 collective-permute-start.13
  19.5 4.0 %collective-permute-done.9.s_far.refs_3_ = f32[200,128]{1,0:T(8,128)S(1)} collective-permute-done((f32[200,128]{1,0:T(8,128)S(1)}, f32[200,128]{1,0:T(8,128)S(1)}, u32[]{:S(2)}, u32[]{:S(2)}) %collective-permute-start.9) | collective-permute-done | bytes 102432 | tf_op jit(solution)/shard_map/ppermute | solution.py:250
  23.5 0.0 collective-permute-done.8.f_far.refs_2_
  23.5 0.0 collective-permute-done.6.s_outer.refs_1_
  23.5 0.0 collective-permute-done.5.f_outer.refs_0_
  23.6 0.0 copy-start
  23.6 0.1 collective-permute-start.14
  23.7 0.5 %collective-permute-start.10 = (f32[304,128]{1,0:T(8,128)S(1)}, f32[304,128]{1,0:T(8,128)S(1)}, u32[]{:S(2)}, u32[]{:S(2)}) collective-permute-start(f32[304,128]{1,0:T(8,128)S(1)} %get-tuple-element.26), channel_id=1, source_target_pairs={{0,16},{1,9},{2,18},{3,11},{4,20},{5,13},{6,22},{7,15},{8,24},{9,1... | collective-permute-start | bytes 466952 | tf_op jit(solution)/shard_map/ppermute | solution.py:250
  24.2 1.7 %collective-permute-start.11 = (f32[296,128]{1,0:T(8,128)S(1)}, f32[296,128]{1,0:T(8,128)S(1)}, u32[]{:S(2)}, u32[]{:S(2)}) collective-permute-start(f32[296,128]{1,0:T(8,128)S(1)} %get-tuple-element.27), channel_id=1, source_target_pairs={{0,8},{1,17},{2,10},{3,19},{4,12},{5,21},{6,14},{7,23},{8,0},{9,25... | collective-permute-start | bytes 454664 | tf_op jit(solution)/shard_map/ppermute | solution.py:250
  26.0 4.2 %collective-permute-done.11.refs_1_ = f32[296,128]{1,0:T(8,128)S(1)} collective-permute-done((f32[296,128]{1,0:T(8,128)S(1)}, f32[296,128]{1,0:T(8,128)S(1)}, u32[]{:S(2)}, u32[]{:S(2)}) %collective-permute-start.11) | collective-permute-done | bytes 151584 | tf_op jit(solution)/shard_map/ppermute | solution.py:250
  30.1 0.2 collective-permute-done.10.refs_0_
  30.4 0.1 collective-permute-start.12
  30.4 0.0 collective-permute-done.13.refs_2_
  30.5 0.0 collective-permute-done.14.refs_3_
  30.5 0.6 %shard_map.74 = (f32[4096,128]{1,0:T(8,128)S(1)}, f32[1,512,128]{2,1,0:T(8,128)S(1)}, f32[4,512,128]{2,1,0:T(8,128)S(1)}, f32[4,8,8,128]{3,2,1,0:T(8,128)S(1)}) custom-call(f32[1400,128]{1,0:T(8,128)S(1)} %shard_map.72.refs_0_, f32[1200,128]{1,0:T(8,128)S(1)} %shard_map.73.refs_1_, f32[1400,128]{1,0:T(8,128)S(1)} %collective-permute-done.13.refs_2_, ...), custom_call_target="tpu_custom_call" | custom-call | tf_op jit(solution)/shard_map/pallas_call | solution.py:324
  31.1 1.0 %collective-permute-done.12.theirs = f32[600,128]{1,0:T(8,128)S(1)} collective-permute-done((f32[600,128]{1,0:T(8,128)S(1)}, f32[600,128]{1,0:T(8,128)S(1)}, u32[]{:S(2)}, u32[]{:S(2)}) %collective-permute-start.12) | collective-permute-done | bytes 307232 | tf_op jit(solution)/shard_map/ppermute | solution.py:250
  32.0 0.0 copy-done
  32.0 2.2 %shard_map.75 = (f32[128,128]{1,0:T(8,128)}, f32[512,128]{1,0:T(8,128)}, f32[4096,128]{1,0:T(8,128)S(1)}, f32[1,512,128]{2,1,0:T(8,128)S(1)}, f32[4,512,128]{2,1,0:T(8,128)S(1)}, /*index=5*/f32[4,8,8,128]{3,2,1,0:T(8,128)S(1)}) custom-call(f32[600,128]{1,0:T(8,128)S(1)} %shard_map.71.mine, ...), custom_call_target="tpu_custom_call", output_to_operand_aliasing={{2}: (2, {}), {3}: (3, {}), {4}: (4, {}), {5}: (5, {})} | custom-call | tf_op jit(solution)/shard_map/pallas_call | solution.py:334
  (5 shorter events, 0.2 us)
Async XLA Ops:
  1.6 8.6 %collective-permute-start = (f32[200,128]{1,0:T(8,128)S(1)}, f32[200,128]{1,0:T(8,128)S(1)}, u32[]{:S(2)}, u32[]{:S(2)}) collective-permute-start(f32[200,128]{1,0:T(8,128)S(1)} %shard_map.68.refs_0_), channel_id=1, source_target_pairs={{0,8},{1,17},{2,10},{3,19},{4,12},{5,21},{6,14},{7,23},{8,0},{9,25... | collective-permute-start | bytes 307208 | tf_op jit(solution)/shard_map/ppermute | solution.py:250
  4.6 6.1 %collective-permute-start.3 = (f32[200,128]{1,0:T(8,128)S(1)}, f32[200,128]{1,0:T(8,128)S(1)}, u32[]{:S(2)}, u32[]{:S(2)}) collective-permute-start(f32[200,128]{1,0:T(8,128)S(1)} %shard_map.68.refs_0_), channel_id=1, source_target_pairs={{0,2},{1,3},{2,0},{3,1},{4,6},{5,7},{6,4},{7,5},{8,10},{9,11},{10,... | collective-permute-start | bytes 307208 | tf_op jit(solution)/shard_map/ppermute | solution.py:250
  6.2 7.8 %collective-permute-start.4 = (f32[200,128]{1,0:T(8,128)S(1)}, f32[200,128]{1,0:T(8,128)S(1)}, u32[]{:S(2)}, u32[]{:S(2)}) collective-permute-start(f32[200,128]{1,0:T(8,128)S(1)} %shard_map.68.refs_0_), channel_id=1, source_target_pairs={{0,6},{1,7},{2,4},{3,5},{4,2},{5,3},{6,0},{7,1},{8,14},{9,15},{10,... | collective-permute-start | bytes 307208 | tf_op jit(solution)/shard_map/ppermute | solution.py:250
  8.7 5.3 %collective-permute-start.1 = (f32[200,128]{1,0:T(8,128)S(1)}, f32[200,128]{1,0:T(8,128)S(1)}, u32[]{:S(2)}, u32[]{:S(2)}) collective-permute-start(f32[200,128]{1,0:T(8,128)S(1)} %shard_map.68.refs_0_), channel_id=1, source_target_pairs={{0,16},{1,9},{2,18},{3,11},{4,20},{5,13},{6,22},{7,15},{8,24},{9,1... | collective-permute-start | bytes 307208 | tf_op jit(solution)/shard_map/ppermute | solution.py:250
  10.2 4.7 %collective-permute-start.2 = (f32[200,128]{1,0:T(8,128)S(1)}, f32[200,128]{1,0:T(8,128)S(1)}, u32[]{:S(2)}, u32[]{:S(2)}) collective-permute-start(f32[200,128]{1,0:T(8,128)S(1)} %collective-permute-done.refs_1_), channel_id=1, source_target_pairs={{0,16},{1,9},{2,18},{3,11},{4,20},{5,13},{6,22},{7,15},{8,24},{9,1... | collective-permute-start | bytes 307208 | tf_op jit(solution)/shard_map/ppermute | solution.py:250
  10.7 6.6 %collective-permute-start.7 = (f32[200,128]{1,0:T(8,128)S(1)}, f32[200,128]{1,0:T(8,128)S(1)}, u32[]{:S(2)}, u32[]{:S(2)}) collective-permute-start(f32[200,128]{1,0:T(8,128)S(1)} %collective-permute-done.3.refs_0_), channel_id=1, source_target_pairs={{0,6},{1,7},{2,4},{3,5},{4,2},{5,3},{6,0},{7,1},{8,14},{9,15},{10,... | collective-permute-start | bytes 307208 | tf_op jit(solution)/shard_map/ppermute | solution.py:250
  14.9 8.6 %collective-permute-start.6 = (f32[400,128]{1,0:T(8,128)S(1)}, f32[400,128]{1,0:T(8,128)S(1)}, u32[]{:S(2)}, u32[]{:S(2)}) collective-permute-start(f32[400,128]{1,0:T(8,128)S(1)} %shard_map.69.refs_4_), channel_id=1, source_target_pairs={{0,16},{1,9},{2,18},{3,11},{4,20},{5,13},{6,22},{7,15},{8,24},{9,1... | collective-permute-start | bytes 614408 | tf_op jit(solution)/shard_map/ppermute | solution.py:250
  16.1 7.5 %collective-permute-start.5 = (f32[400,128]{1,0:T(8,128)S(1)}, f32[400,128]{1,0:T(8,128)S(1)}, u32[]{:S(2)}, u32[]{:S(2)}) collective-permute-start(f32[400,128]{1,0:T(8,128)S(1)} %shard_map.69.refs_4_), channel_id=1, source_target_pairs={{0,8},{1,17},{2,10},{3,19},{4,12},{5,21},{6,14},{7,23},{8,0},{9,25... | collective-permute-start | bytes 614408 | tf_op jit(solution)/shard_map/ppermute | solution.py:250
  17.3 6.2 %collective-permute-start.9 = (f32[200,128]{1,0:T(8,128)S(1)}, f32[200,128]{1,0:T(8,128)S(1)}, u32[]{:S(2)}, u32[]{:S(2)}) collective-permute-start(f32[200,128]{1,0:T(8,128)S(1)} %collective-permute-done.7.refs_5_), channel_id=1, source_target_pairs={{0,16},{1,9},{2,18},{3,11},{4,20},{5,13},{6,22},{7,15},{8,24},{9,1... | collective-permute-start | bytes 307208 | tf_op jit(solution)/shard_map/ppermute | solution.py:250
  18.7 4.8 %collective-permute-start.8 = (f32[200,128]{1,0:T(8,128)S(1)}, f32[200,128]{1,0:T(8,128)S(1)}, u32[]{:S(2)}, u32[]{:S(2)}) collective-permute-start(f32[200,128]{1,0:T(8,128)S(1)} %collective-permute-done.7.refs_5_), channel_id=1, source_target_pairs={{0,8},{1,17},{2,10},{3,19},{4,12},{5,21},{6,14},{7,23},{8,0},{9,25... | collective-permute-start | bytes 307208 | tf_op jit(solution)/shard_map/ppermute | solution.py:250
  19.4 11.1 %collective-permute-start.13 = (f32[1400,128]{1,0:T(8,128)S(1)}, f32[1400,128]{1,0:T(8,128)S(1)}, u32[]{:S(2)}, u32[]{:S(2)}) collective-permute-start(f32[1400,128]{1,0:T(8,128)S(1)} %shard_map.72.refs_0_), channel_id=1, source_target_pairs={{0,1},{1,0},{2,3},{3,2},{4,5},{5,4},{6,7},{7,6},{8,9},{9,8},{10,11... | collective-permute-start | bytes 2150408 | tf_op jit(solution)/shard_map/ppermute | solution.py:250
  23.6 8.5 %copy-start = (f32[64,2,512]{2,1,0:T(2,128)S(1)}, f32[64,2,512]{2,1,0:T(2,128)}, u32[]{:S(2)}) copy-start(f32[64,2,512]{2,1,0:T(2,128)} %param.9) | copy-start | bytes 786436
  23.6 6.9 %collective-permute-start.14 = (f32[1200,128]{1,0:T(8,128)S(1)}, f32[1200,128]{1,0:T(8,128)S(1)}, u32[]{:S(2)}, u32[]{:S(2)}) collective-permute-start(f32[1200,128]{1,0:T(8,128)S(1)} %shard_map.73.refs_1_), channel_id=1, source_target_pairs={{0,1},{1,0},{2,3},{3,2},{4,5},{5,4},{6,7},{7,6},{8,9},{9,8},{10,11... | collective-permute-start | bytes 1843208 | tf_op jit(solution)/shard_map/ppermute | solution.py:250
  23.7 6.6 %collective-permute-start.10 = (f32[304,128]{1,0:T(8,128)S(1)}, f32[304,128]{1,0:T(8,128)S(1)}, u32[]{:S(2)}, u32[]{:S(2)}) collective-permute-start(f32[304,128]{1,0:T(8,128)S(1)} %get-tuple-element.26), channel_id=1, source_target_pairs={{0,16},{1,9},{2,18},{3,11},{4,20},{5,13},{6,22},{7,15},{8,24},{9,1... | collective-permute-start | bytes 466952 | tf_op jit(solution)/shard_map/ppermute | solution.py:250
  24.2 5.9 %collective-permute-start.11 = (f32[296,128]{1,0:T(8,128)S(1)}, f32[296,128]{1,0:T(8,128)S(1)}, u32[]{:S(2)}, u32[]{:S(2)}) collective-permute-start(f32[296,128]{1,0:T(8,128)S(1)} %get-tuple-element.27), channel_id=1, source_target_pairs={{0,8},{1,17},{2,10},{3,19},{4,12},{5,21},{6,14},{7,23},{8,0},{9,25... | collective-permute-start | bytes 454664 | tf_op jit(solution)/shard_map/ppermute | solution.py:250
  30.4 1.7 %collective-permute-start.12 = (f32[600,128]{1,0:T(8,128)S(1)}, f32[600,128]{1,0:T(8,128)S(1)}, u32[]{:S(2)}, u32[]{:S(2)}) collective-permute-start(f32[600,128]{1,0:T(8,128)S(1)} %shard_map.71.mine), channel_id=1, source_target_pairs={{0,1},{1,0},{2,3},{3,2},{4,5},{5,4},{6,7},{7,6},{8,9},{9,8},{10,11... | collective-permute-start | bytes 921608 | tf_op jit(solution)/shard_map/ppermute | solution.py:250

commit v5 on v4

--- a/solution.py
+++ b/solution.py
@@ -29,13 +29,12 @@
     return high, (x - high.astype(jnp.float32)).astype(jnp.bfloat16)
 
 
-def product(a, b):
-    (ah, al), (bh, bl) = halves(a), halves(b)
-
+def product(a, high, low):
     def dot(x, y):
         return lax.dot_general(x, y, (((1,), (0,)), ((), ())), preferred_element_type=jnp.float32)
 
-    return dot(ah, bh) + (dot(ah, bl) + dot(al, bh))
+    a_high, a_low = halves(a)
+    return dot(a_high, high) + (dot(a_high, low) + dot(a_low, high))
 
 
 def supernode_pass(present, masked, listed_f, diag_part, ratio):
@@ -107,8 +106,8 @@
             and self.span == LANES
             and self.width % LANES == 0
             and self.slots % 8 == 0
-            and self.own % 8 == 0
-            and self.rows_c % 8 == 0
+            and self.own % 16 == 0
+            and self.rows_c % 16 == 0
             and self.nodes % CORES == 0
             and self.nodes <= 8
         )
@@ -166,25 +165,27 @@
     two[pl.ds(n.bulk - low, n.bulk), :] = s_outer[pl.ds(n.bulk, n.bulk), :]
 
 
-def put(n, ref, at, r2, c2, m_all, m_sel, p_t, mask):
+def put(n, ref, at, r2, c2, m_high, m_low, m_sel, p_high, p_low, mask):
     _, z, core = spot()
     first = core == 0
     left = lax.broadcasted_iota(jnp.int32, (n.own, LANES), 1) < n.wide
-    row = r2 * n.span + c2 * n.own
-    m_all[pl.ds(row * n.slots, n.m_rows), :] = ref[pl.ds(at, n.m_rows), :]
-    p_t[r2, pl.ds(c2 * n.rows_c, n.rows_c), :] = ref[pl.ds(at + n.m_rows, n.rows_c), :]
+    rows = pl.ds(pl.multiple_of(r2 * n.span + c2 * n.own, n.own), n.own)
+    cols = pl.ds(pl.multiple_of(c2 * n.rows_c, n.rows_c), n.rows_c)
+    p_high[r2, cols, :], p_low[r2, cols, :] = halves(ref[pl.ds(at + n.m_rows, n.rows_c), :])
     mask[r2, c2] = ref[pl.ds(at + n.m_rows + n.rows_c, 8), :]
+    chosen = []
+    for k in range(n.nodes):
+        piece = None
+        for t in range(n.tiles):
+            load = ref[pl.ds(at + t * n.nodes + k, n.own, stride=n.slots), :]
+            lanes = pl.ds(t * LANES, LANES)
+            m_high[k, rows, lanes], m_low[k, rows, lanes] = halves(load)
+            piece = load if piece is None else jnp.where(z == t, load, piece)
+        chosen.append(piece)
     for k in range(0, n.nodes, CORES):
-        pair = []
-        for i in range(CORES):
-            piece = None
-            for t in range(n.tiles):
-                load = ref[pl.ds(at + t * n.nodes + k + i, n.own, stride=n.slots), :]
-                piece = load if piece is None else jnp.where(z == t, load, piece)
-            pair.append(piece)
-        one, two = pair
+        one, two = chosen[k], chosen[k + 1]
         turned = pltpu.roll(jnp.where(first, two, one), n.wide, 1)
-        m_sel[k // CORES, pl.ds(row, n.own), :] = jnp.where(left == first, jnp.where(first, one, two), turned)
+        m_sel[k // CORES, rows, :] = jnp.where(left == first, jnp.where(first, one, two), turned)
 
 
 def fill(n, pieces, mine, theirs, *refs):
@@ -204,9 +205,9 @@
 
 
 def work_kernel(n, pieces, mine, theirs, *refs):
-    diag, columns, schur, *store = refs[4:]
+    diag, columns, schur, *store = refs[6:]
     fill(n, pieces, mine, theirs, *store)
-    m_all, m_sel, p_t, masks = store
+    m_high, m_low, m_sel, p_high, p_low, masks = store
     r, _, _ = spot()
     mask = []
     for i in range(n.n_row):
@@ -214,10 +215,10 @@
         for c in range(1, n.n_col):
             total += masks[i, c]
         mask.append(total)
-    p_all = jnp.concatenate([p_t[i] for i in range(n.n_row)], axis=1)
+    p_all = [jnp.concatenate([p[i] for i in range(n.n_row)], axis=1) for p in (p_high, p_low)]
     for k in range(n.nodes):
         if k % CORES == 0:
-            x_t = product(m_sel[k // CORES].T, p_all)
+            x_t = product(m_sel[k // CORES].T, *p_all)
         at = k % CORES * n.wide
         spread = jnp.concatenate([m[k : k + 1, :] for m in mask], axis=1)
         part = -x_t[at : at + n.wide, :] * spread
@@ -225,8 +226,7 @@
         for i in range(1, n.n_row):
             own = jnp.where(r == i, part[:, i * LANES : (i + 1) * LANES], own)
         columns[pl.ds(k, n.wide, stride=n.nodes), :] = own
-        sides = [m_all[pl.ds(t * n.nodes + k, n.total, stride=n.slots), :] for t in range(n.tiles)]
-        wide = product(part, jnp.concatenate(sides, axis=1))
+        wide = product(part, m_high[k], m_low[k])
         for t in range(n.tiles):
             line = pl.ds(t * n.nodes + k, n.wide, stride=n.slots)
             schur[line, :] = diag[line, :] - wide[:, t * LANES : (t + 1) * LANES]
@@ -292,9 +292,9 @@
     near, across = 1, n.n_z - 1
     z1, z3 = over_z(bulk, near), over_z(bulk, across)
     z2 = over_z(z1, across)
-    early = [bulk, over_pair(bulk, 0), over_pair(bulk, 1)]
+    mid, z1 = lax.optimization_barrier((bulk, z1))
+    early = [bulk, over_pair(mid, 0), over_pair(mid, 1)]
     early.append(over_pair(early[1], 1))
-    early, z1, z3 = lax.optimization_barrier((early, z1, z3))
     outer = join(z1, z3)
     trip = [over_pair(outer, 0), over_pair(outer, 1), over_pair(z2, 0), over_pair(z2, 1)]
     trip = lax.optimization_barrier(trip)
@@ -314,17 +314,20 @@
     shell, beyond = (near, across), (near ^ across,)
     pieces = [(here, (0,)), (side, (0,)), (turn, (0,)), (both, (0,)), (here, shell), (here, beyond)]
     pieces = [pieces, [(side, shell), (turn, shell), (side, beyond), (turn, beyond)]]
+    def short(*dims):
+        return [jax.ShapeDtypeStruct(dims, jnp.bfloat16)] * 2
+
     store = [
-        shape(n.total * n.slots, LANES),
+        *short(n.nodes, n.total, n.width),
         shape(n.nodes // CORES, n.total, LANES),
-        shape(n.n_row, n.n_col * n.rows_c, LANES),
+        *short(n.n_row, n.n_col * n.rows_c, LANES),
         shape(n.n_row, n.n_col, 8, LANES),
     ]
     taken = [*part, *[over_core(p) for p in part]]
     placed = pl.pallas_call(
         functools.partial(fill_kernel, n, pieces),
         in_specs=[VMEM] * len(taken),
-        out_specs=[VMEM] * 4,
+        out_specs=[VMEM] * len(store),
         out_shape=store,
         compiler_params=room(*taken, *store),
     )(*taken)
@@ -336,7 +339,7 @@
         in_specs=[VMEM] * len(taken),
         out_specs=[VMEM] * len(out),
         out_shape=out,
-        input_output_aliases={2 + i: 2 + i for i in range(4)},
+        input_output_aliases={2 + i: 2 + i for i in range(len(store))},
         compiler_params=room(*taken, *out),
     )(*taken)
     schur = jnp.transpose(schur.reshape(n.wide, n.tiles, n.nodes, LANES), (0, 2, 1, 3))

time: 34.4 us -> 34.1 us (level)
  waiting for transfers between devices: 11 us -> 8.06 us
  starting transfers between devices: 18.6 us -> 21.3 us
    ppermute x15, waiting for transfers between devices: 11 us -> 8.06 us  [route(): return lax.ppermute(array, AXES, pairs)]
    ppermute x15, starting transfers between devices: 18.6 us -> 21.3 us  [route(): return lax.ppermute(array, AXES, pairs)]
  transfers between devices with their start and end apart: 15 -> 15, of which waited for: 6 -> 5; matrix products, arithmetic and copies ran while one was open for 0% -> 0% of each run, Pallas kernels for 2% -> 3%
where the time goes in v5:
time: 34.1 us; the launch traced here: 33.9 us
  starting transfers between devices  21.3 us (62%)
  waiting for transfers between devices  8.06 us (24%)
  Pallas kernels  3.87 us (11%)
  between operations  0.71 us (2%)
    ppermute x15, starting transfers between devices, route(): return lax.ppermute(array, AXES, pairs)  21.3 us
    ppermute x15, waiting for transfers between devices, route(): return lax.ppermute(array, AXES, pairs)  8.06 us
    pallas_call x1, Pallas kernels, fast(): pl.pallas_call(functools.partial(work_kernel, n, pieces), in_specs=[VMEM]...  1.92 us
    pallas_call x1, Pallas kernels, fast(): pl.pallas_call(functools.partial(pack_kernel, n), in_specs=[pl.BlockSpec(...  1 us
    pallas_call x1, Pallas kernels, fast(): pl.pallas_call(functools.partial(fill_kernel, n, pieces), in_specs=[VMEM]...  0.8 us
  transfers between devices with their start and end apart: 15, of which 5 were waited for; matrix products, arithmetic and copies ran while one was open for 0% of the time, Pallas kernels for 3%

profile of v5, /device:TPU:0, one launch (start us, length us, event | category | flops | bytes accessed | tf_op | source)
XLA Modules:
  0.0 33.9 jit_solution(6485794997235918862)
XLA Ops:
  0.6 1.0 %shard_map.68.refs_0_ = f32[200,128]{1,0:T(8,128)S(1)} custom-call(f32[128,128]{1,0:T(8,128)} %bitcast.20, s32[2,16]{1,0:T(2,128)} %bitcast.22, f32[64,128]{1,0:T(8,128)} %bitcast.21, s32[1,2]{1,0:T(1,128)} %bitcast.23), custom_call_target="tpu_custom_call" | custom-call | tf_op jit(solution)/shard_map/pallas_call | solution.py:270
  1.6 3.1 %collective-permute-start = (f32[200,128]{1,0:T(8,128)S(1)}, f32[200,128]{1,0:T(8,128)S(1)}, u32[]{:S(2)}, u32[]{:S(2)}) collective-permute-start(f32[200,128]{1,0:T(8,128)S(1)} %shard_map.68.refs_0_), channel_id=1, source_target_pairs={{0,2},{1,3},{2,0},{3,1},{4,6},{5,7},{6,4},{7,5},{8,10},{9,11},{10,... | collective-permute-start | bytes 307208 | tf_op jit(solution)/shard_map/ppermute | solution.py:250
  4.7 2.5 %collective-permute-start.1 = (f32[200,128]{1,0:T(8,128)S(1)}, f32[200,128]{1,0:T(8,128)S(1)}, u32[]{:S(2)}, u32[]{:S(2)}) collective-permute-start(f32[200,128]{1,0:T(8,128)S(1)} %shard_map.68.refs_0_), channel_id=1, source_target_pairs={{0,6},{1,7},{2,4},{3,5},{4,2},{5,3},{6,0},{7,1},{8,14},{9,15},{10,... | collective-permute-start | bytes 307208 | tf_op jit(solution)/shard_map/ppermute | solution.py:250
  7.2 0.4 %collective-permute-done.refs_0_ = f32[200,128]{1,0:T(8,128)S(1)} collective-permute-done((f32[200,128]{1,0:T(8,128)S(1)}, f32[200,128]{1,0:T(8,128)S(1)}, u32[]{:S(2)}, u32[]{:S(2)}) %collective-permute-start) | collective-permute-done | bytes 102432 | tf_op jit(solution)/shard_map/ppermute | solution.py:250
  7.6 1.7 %collective-permute-start.10 = (f32[200,128]{1,0:T(8,128)S(1)}, f32[200,128]{1,0:T(8,128)S(1)}, u32[]{:S(2)}, u32[]{:S(2)}) collective-permute-start(f32[200,128]{1,0:T(8,128)S(1)} %shard_map.68.refs_0_), channel_id=1, source_target_pairs={{0,8},{1,17},{2,10},{3,19},{4,12},{5,21},{6,14},{7,23},{8,0},{9,25... | collective-permute-start | bytes 307208 | tf_op jit(solution)/shard_map/ppermute | solution.py:250
  9.3 1.5 %collective-permute-start.11 = (f32[200,128]{1,0:T(8,128)S(1)}, f32[200,128]{1,0:T(8,128)S(1)}, u32[]{:S(2)}, u32[]{:S(2)}) collective-permute-start(f32[200,128]{1,0:T(8,128)S(1)} %shard_map.68.refs_0_), channel_id=1, source_target_pairs={{0,16},{1,9},{2,18},{3,11},{4,20},{5,13},{6,22},{7,15},{8,24},{9,1... | collective-permute-start | bytes 307208 | tf_op jit(solution)/shard_map/ppermute | solution.py:250
  10.8 4.7 %collective-permute-start.4 = (f32[200,128]{1,0:T(8,128)S(1)}, f32[200,128]{1,0:T(8,128)S(1)}, u32[]{:S(2)}, u32[]{:S(2)}) collective-permute-start(f32[200,128]{1,0:T(8,128)S(1)} %collective-permute-done.refs_0_), channel_id=1, source_target_pairs={{0,6},{1,7},{2,4},{3,5},{4,2},{5,3},{6,0},{7,1},{8,14},{9,15},{10,... | collective-permute-start | bytes 307208 | tf_op jit(solution)/shard_map/ppermute | solution.py:250
  15.5 0.0 collective-permute-done.1.refs_1_
  15.5 0.6 %collective-permute-start.3 = (f32[400,128]{1,0:T(8,128)S(1)}, f32[400,128]{1,0:T(8,128)S(1)}, u32[]{:S(2)}, u32[]{:S(2)}) collective-permute-start(f32[400,128]{1,0:T(8,128)S(1)} %shard_map.69.refs_4_), channel_id=1, source_target_pairs={{0,16},{1,9},{2,18},{3,11},{4,20},{5,13},{6,22},{7,15},{8,24},{9,1... | collective-permute-start | bytes 614408 | tf_op jit(solution)/shard_map/ppermute | solution.py:250
  16.1 0.5 %collective-permute-start.2 = (f32[400,128]{1,0:T(8,128)S(1)}, f32[400,128]{1,0:T(8,128)S(1)}, u32[]{:S(2)}, u32[]{:S(2)}) collective-permute-start(f32[400,128]{1,0:T(8,128)S(1)} %shard_map.69.refs_4_), channel_id=1, source_target_pairs={{0,8},{1,17},{2,10},{3,19},{4,12},{5,21},{6,14},{7,23},{8,0},{9,25... | collective-permute-start | bytes 614408 | tf_op jit(solution)/shard_map/ppermute | solution.py:250
  16.6 0.0 collective-permute-done.10.refs_1_
  16.7 1.5 %collective-permute-start.12 = (f32[200,128]{1,0:T(8,128)S(1)}, f32[200,128]{1,0:T(8,128)S(1)}, u32[]{:S(2)}, u32[]{:S(2)}) collective-permute-start(f32[200,128]{1,0:T(8,128)S(1)} %collective-permute-done.10.refs_1_), channel_id=1, source_target_pairs={{0,16},{1,9},{2,18},{3,11},{4,20},{5,13},{6,22},{7,15},{8,24},{9,1... | collective-permute-start | bytes 307208 | tf_op jit(solution)/shard_map/ppermute | solution.py:250
  18.2 0.0 collective-permute-done.4.refs_5_
  18.2 0.5 %collective-permute-start.6 = (f32[200,128]{1,0:T(8,128)S(1)}, f32[200,128]{1,0:T(8,128)S(1)}, u32[]{:S(2)}, u32[]{:S(2)}) collective-permute-start(f32[200,128]{1,0:T(8,128)S(1)} %collective-permute-done.4.refs_5_), channel_id=1, source_target_pairs={{0,16},{1,9},{2,18},{3,11},{4,20},{5,13},{6,22},{7,15},{8,24},{9,1... | collective-permute-start | bytes 307208 | tf_op jit(solution)/shard_map/ppermute | solution.py:250
  18.7 0.0 collective-permute-done.11.refs_2_
  18.7 1.5 %collective-permute-start.5 = (f32[200,128]{1,0:T(8,128)S(1)}, f32[200,128]{1,0:T(8,128)S(1)}, u32[]{:S(2)}, u32[]{:S(2)}) collective-permute-start(f32[200,128]{1,0:T(8,128)S(1)} %collective-permute-done.4.refs_5_), channel_id=1, source_target_pairs={{0,8},{1,17},{2,10},{3,19},{4,12},{5,21},{6,14},{7,23},{8,0},{9,25... | collective-permute-start | bytes 307208 | tf_op jit(solution)/shard_map/ppermute | solution.py:250
  20.2 2.3 %collective-permute-done.12.refs_3_ = f32[200,128]{1,0:T(8,128)S(1)} collective-permute-done((f32[200,128]{1,0:T(8,128)S(1)}, f32[200,128]{1,0:T(8,128)S(1)}, u32[]{:S(2)}, u32[]{:S(2)}) %collective-permute-start.12) | collective-permute-done | bytes 102432 | tf_op jit(solution)/shard_map/ppermute | solution.py:250
  22.5 0.1 collective-permute-start.13
  22.6 1.0 %collective-permute-done.6.s_far.refs_3_ = f32[200,128]{1,0:T(8,128)S(1)} collective-permute-done((f32[200,128]{1,0:T(8,128)S(1)}, f32[200,128]{1,0:T(8,128)S(1)}, u32[]{:S(2)}, u32[]{:S(2)}) %collective-permute-start.6) | collective-permute-done | bytes 102432 | tf_op jit(solution)/shard_map/ppermute | solution.py:250
  23.6 0.0 collective-permute-done.5.f_far.refs_2_
  23.6 0.0 collective-permute-done.3.s_outer.refs_1_
  23.6 0.0 collective-permute-done.2.f_outer.refs_0_
  23.6 0.1 collective-permute-start.14
  23.7 1.4 %collective-permute-start.7 = (f32[304,128]{1,0:T(8,128)S(1)}, f32[304,128]{1,0:T(8,128)S(1)}, u32[]{:S(2)}, u32[]{:S(2)}) collective-permute-start(f32[304,128]{1,0:T(8,128)S(1)} %get-tuple-element.23), channel_id=1, source_target_pairs={{0,16},{1,9},{2,18},{3,11},{4,20},{5,13},{6,22},{7,15},{8,24},{9,1... | collective-permute-start | bytes 466952 | tf_op jit(solution)/shard_map/ppermute | solution.py:250
  25.1 1.5 %collective-permute-start.8 = (f32[296,128]{1,0:T(8,128)S(1)}, f32[296,128]{1,0:T(8,128)S(1)}, u32[]{:S(2)}, u32[]{:S(2)}) collective-permute-start(f32[296,128]{1,0:T(8,128)S(1)} %get-tuple-element.24), channel_id=1, source_target_pairs={{0,8},{1,17},{2,10},{3,19},{4,12},{5,21},{6,14},{7,23},{8,0},{9,25... | collective-permute-start | bytes 454664 | tf_op jit(solution)/shard_map/ppermute | solution.py:250
  26.6 3.7 %collective-permute-done.8.refs_1_ = f32[296,128]{1,0:T(8,128)S(1)} collective-permute-done((f32[296,128]{1,0:T(8,128)S(1)}, f32[296,128]{1,0:T(8,128)S(1)}, u32[]{:S(2)}, u32[]{:S(2)}) %collective-permute-start.8) | collective-permute-done | bytes 151584 | tf_op jit(solution)/shard_map/ppermute | solution.py:250
  30.3 0.0 collective-permute-done.7.refs_0_
  30.3 0.0 copy-start
  30.4 0.2 collective-permute-start.9
  30.6 0.0 collective-permute-done.14.refs_3_
  30.6 0.0 collective-permute-done.13.refs_2_
  30.6 0.8 %shard_map.74 = (bf16[2,512,512]{2,1,0:T(8,128)(2,1)S(1)}, bf16[2,512,512]{2,1,0:T(8,128)(2,1)S(1)}, f32[1,512,128]{2,1,0:T(8,128)S(1)}, bf16[4,512,128]{2,1,0:T...) custom-call(f32[1400,128]{1,0:T(8,128)S(1)} %shard_map.72.refs_0_, ...), custom_call_target="tpu_custom_call" | custom-call | tf_op jit(solution)/shard_map/pallas_call | solution.py:327
  31.4 0.6 %collective-permute-done.9.theirs = f32[600,128]{1,0:T(8,128)S(1)} collective-permute-done((f32[600,128]{1,0:T(8,128)S(1)}, f32[600,128]{1,0:T(8,128)S(1)}, u32[]{:S(2)}, u32[]{:S(2)}) %collective-permute-start.9) | collective-permute-done | bytes 307232 | tf_op jit(solution)/shard_map/ppermute | solution.py:250
  32.0 0.0 copy-done
  32.0 1.9 %shard_map.75 = (f32[128,128]{1,0:T(8,128)}, f32[512,128]{1,0:T(8,128)}, bf16[2,512,512]{2,1,0:T(8,128)(2,1)S(1)}, bf16[2,512,512]{2,1,0:T(8,128)(2,1)S(1)}, f32...) custom-call(f32[600,128]{1,0:T(8,128)S(1)} %shard_map.71.mine, ...), custom_call_target="tpu_custom_call", output_to_operand_aliasing={{2}: (2, {}), {3}: (3, {}), {4}: (4, {}), {5}: (5, {}), {6}... | custom-call | tf_op jit(solution)/shard_map/pallas_call | solution.py:337
  (5 shorter events, 0.1 us)
Async XLA Ops:
  1.6 6.0 %collective-permute-start = (f32[200,128]{1,0:T(8,128)S(1)}, f32[200,128]{1,0:T(8,128)S(1)}, u32[]{:S(2)}, u32[]{:S(2)}) collective-permute-start(f32[200,128]{1,0:T(8,128)S(1)} %shard_map.68.refs_0_), channel_id=1, source_target_pairs={{0,2},{1,3},{2,0},{3,1},{4,6},{5,7},{6,4},{7,5},{8,10},{9,11},{10,... | collective-permute-start | bytes 307208 | tf_op jit(solution)/shard_map/ppermute | solution.py:250
  4.7 10.8 %collective-permute-start.1 = (f32[200,128]{1,0:T(8,128)S(1)}, f32[200,128]{1,0:T(8,128)S(1)}, u32[]{:S(2)}, u32[]{:S(2)}) collective-permute-start(f32[200,128]{1,0:T(8,128)S(1)} %shard_map.68.refs_0_), channel_id=1, source_target_pairs={{0,6},{1,7},{2,4},{3,5},{4,2},{5,3},{6,0},{7,1},{8,14},{9,15},{10,... | collective-permute-start | bytes 307208 | tf_op jit(solution)/shard_map/ppermute | solution.py:250
  7.6 9.0 %collective-permute-start.10 = (f32[200,128]{1,0:T(8,128)S(1)}, f32[200,128]{1,0:T(8,128)S(1)}, u32[]{:S(2)}, u32[]{:S(2)}) collective-permute-start(f32[200,128]{1,0:T(8,128)S(1)} %shard_map.68.refs_0_), channel_id=1, source_target_pairs={{0,8},{1,17},{2,10},{3,19},{4,12},{5,21},{6,14},{7,23},{8,0},{9,25... | collective-permute-start | bytes 307208 | tf_op jit(solution)/shard_map/ppermute | solution.py:250
  9.3 9.4 %collective-permute-start.11 = (f32[200,128]{1,0:T(8,128)S(1)}, f32[200,128]{1,0:T(8,128)S(1)}, u32[]{:S(2)}, u32[]{:S(2)}) collective-permute-start(f32[200,128]{1,0:T(8,128)S(1)} %shard_map.68.refs_0_), channel_id=1, source_target_pairs={{0,16},{1,9},{2,18},{3,11},{4,20},{5,13},{6,22},{7,15},{8,24},{9,1... | collective-permute-start | bytes 307208 | tf_op jit(solution)/shard_map/ppermute | solution.py:250
  10.8 7.4 %collective-permute-start.4 = (f32[200,128]{1,0:T(8,128)S(1)}, f32[200,128]{1,0:T(8,128)S(1)}, u32[]{:S(2)}, u32[]{:S(2)}) collective-permute-start(f32[200,128]{1,0:T(8,128)S(1)} %collective-permute-done.refs_0_), channel_id=1, source_target_pairs={{0,6},{1,7},{2,4},{3,5},{4,2},{5,3},{6,0},{7,1},{8,14},{9,15},{10,... | collective-permute-start | bytes 307208 | tf_op jit(solution)/shard_map/ppermute | solution.py:250
  15.5 8.0 %collective-permute-start.3 = (f32[400,128]{1,0:T(8,128)S(1)}, f32[400,128]{1,0:T(8,128)S(1)}, u32[]{:S(2)}, u32[]{:S(2)}) collective-permute-start(f32[400,128]{1,0:T(8,128)S(1)} %shard_map.69.refs_4_), channel_id=1, source_target_pairs={{0,16},{1,9},{2,18},{3,11},{4,20},{5,13},{6,22},{7,15},{8,24},{9,1... | collective-permute-start | bytes 614408 | tf_op jit(solution)/shard_map/ppermute | solution.py:250
  16.1 7.5 %collective-permute-start.2 = (f32[400,128]{1,0:T(8,128)S(1)}, f32[400,128]{1,0:T(8,128)S(1)}, u32[]{:S(2)}, u32[]{:S(2)}) collective-permute-start(f32[400,128]{1,0:T(8,128)S(1)} %shard_map.69.refs_4_), channel_id=1, source_target_pairs={{0,8},{1,17},{2,10},{3,19},{4,12},{5,21},{6,14},{7,23},{8,0},{9,25... | collective-permute-start | bytes 614408 | tf_op jit(solution)/shard_map/ppermute | solution.py:250
  16.7 5.8 %collective-permute-start.12 = (f32[200,128]{1,0:T(8,128)S(1)}, f32[200,128]{1,0:T(8,128)S(1)}, u32[]{:S(2)}, u32[]{:S(2)}) collective-permute-start(f32[200,128]{1,0:T(8,128)S(1)} %collective-permute-done.10.refs_1_), channel_id=1, source_target_pairs={{0,16},{1,9},{2,18},{3,11},{4,20},{5,13},{6,22},{7,15},{8,24},{9,1... | collective-permute-start | bytes 307208 | tf_op jit(solution)/shard_map/ppermute | solution.py:250
  18.2 5.4 %collective-permute-start.6 = (f32[200,128]{1,0:T(8,128)S(1)}, f32[200,128]{1,0:T(8,128)S(1)}, u32[]{:S(2)}, u32[]{:S(2)}) collective-permute-start(f32[200,128]{1,0:T(8,128)S(1)} %collective-permute-done.4.refs_5_), channel_id=1, source_target_pairs={{0,16},{1,9},{2,18},{3,11},{4,20},{5,13},{6,22},{7,15},{8,24},{9,1... | collective-permute-start | bytes 307208 | tf_op jit(solution)/shard_map/ppermute | solution.py:250
  18.7 4.8 %collective-permute-start.5 = (f32[200,128]{1,0:T(8,128)S(1)}, f32[200,128]{1,0:T(8,128)S(1)}, u32[]{:S(2)}, u32[]{:S(2)}) collective-permute-start(f32[200,128]{1,0:T(8,128)S(1)} %collective-permute-done.4.refs_5_), channel_id=1, source_target_pairs={{0,8},{1,17},{2,10},{3,19},{4,12},{5,21},{6,14},{7,23},{8,0},{9,25... | collective-permute-start | bytes 307208 | tf_op jit(solution)/shard_map/ppermute | solution.py:250
  22.5 8.1 %collective-permute-start.13 = (f32[1400,128]{1,0:T(8,128)S(1)}, f32[1400,128]{1,0:T(8,128)S(1)}, u32[]{:S(2)}, u32[]{:S(2)}) collective-permute-start(f32[1400,128]{1,0:T(8,128)S(1)} %shard_map.72.refs_0_), channel_id=1, source_target_pairs={{0,1},{1,0},{2,3},{3,2},{4,5},{5,4},{6,7},{7,6},{8,9},{9,8},{10,11... | collective-permute-start | bytes 2150408 | tf_op jit(solution)/shard_map/ppermute | solution.py:250
  23.6 7.0 %collective-permute-start.14 = (f32[1200,128]{1,0:T(8,128)S(1)}, f32[1200,128]{1,0:T(8,128)S(1)}, u32[]{:S(2)}, u32[]{:S(2)}) collective-permute-start(f32[1200,128]{1,0:T(8,128)S(1)} %shard_map.73.refs_1_), channel_id=1, source_target_pairs={{0,1},{1,0},{2,3},{3,2},{4,5},{5,4},{6,7},{7,6},{8,9},{9,8},{10,11... | collective-permute-start | bytes 1843208 | tf_op jit(solution)/shard_map/ppermute | solution.py:250
  23.7 6.6 %collective-permute-start.7 = (f32[304,128]{1,0:T(8,128)S(1)}, f32[304,128]{1,0:T(8,128)S(1)}, u32[]{:S(2)}, u32[]{:S(2)}) collective-permute-start(f32[304,128]{1,0:T(8,128)S(1)} %get-tuple-element.23), channel_id=1, source_target_pairs={{0,16},{1,9},{2,18},{3,11},{4,20},{5,13},{6,22},{7,15},{8,24},{9,1... | collective-permute-start | bytes 466952 | tf_op jit(solution)/shard_map/ppermute | solution.py:250
  25.1 5.2 %collective-permute-start.8 = (f32[296,128]{1,0:T(8,128)S(1)}, f32[296,128]{1,0:T(8,128)S(1)}, u32[]{:S(2)}, u32[]{:S(2)}) collective-permute-start(f32[296,128]{1,0:T(8,128)S(1)} %get-tuple-element.24), channel_id=1, source_target_pairs={{0,8},{1,17},{2,10},{3,19},{4,12},{5,21},{6,14},{7,23},{8,0},{9,25... | collective-permute-start | bytes 454664 | tf_op jit(solution)/shard_map/ppermute | solution.py:250
  30.3 1.7 %copy-start = (f32[64,2,512]{2,1,0:T(2,128)S(1)}, f32[64,2,512]{2,1,0:T(2,128)}, u32[]{:S(2)}) copy-start(f32[64,2,512]{2,1,0:T(2,128)} %param.9) | copy-start | bytes 786436
  30.4 1.7 %collective-permute-start.9 = (f32[600,128]{1,0:T(8,128)S(1)}, f32[600,128]{1,0:T(8,128)S(1)}, u32[]{:S(2)}, u32[]{:S(2)}) collective-permute-start(f32[600,128]{1,0:T(8,128)S(1)} %shard_map.71.mine), channel_id=1, source_target_pairs={{0,1},{1,0},{2,3},{3,2},{4,5},{5,4},{6,7},{7,6},{8,9},{9,8},{10,11... | collective-permute-start | bytes 921608 | tf_op jit(solution)/shard_map/ppermute | solution.py:250

commit v6 on v5

--- a/solution.py
+++ b/solution.py
@@ -291,7 +291,7 @@
     side, turn, both = (one, two), (two, one), (one ^ two, one ^ two)
     near, across = 1, n.n_z - 1
     z1, z3 = over_z(bulk, near), over_z(bulk, across)
-    z2 = over_z(z1, across)
+    z2 = over_z(z3, near)
     mid, z1 = lax.optimization_barrier((bulk, z1))
     early = [bulk, over_pair(mid, 0), over_pair(mid, 1)]
     early.append(over_pair(early[1], 1))

time: 34.1 us -> 34.3 us (level)
  waiting for transfers between devices: 8.06 us -> 11 us
  starting transfers between devices: 21.3 us -> 18.6 us
    ppermute x15, waiting for transfers between devices: 8.06 us -> 11 us  [route(): return lax.ppermute(array, AXES, pairs)]
    ppermute x15, starting transfers between devices: 21.3 us -> 18.6 us  [route(): return lax.ppermute(array, AXES, pairs)]
  transfers between devices with their start and end apart: 15 -> 15, of which waited for: 5 -> 6; matrix products, arithmetic and copies ran while one was open for 0% -> 0% of each run, Pallas kernels for 3% -> 3%
where the time goes in v6:
time: 34.3 us; the launch traced here: 34.2 us
  starting transfers between devices  18.6 us (54%)
  waiting for transfers between devices  11 us (32%)
  Pallas kernels  3.87 us (11%)
  between operations  0.71 us (2%)
    ppermute x15, starting transfers between devices, route(): return lax.ppermute(array, AXES, pairs)  18.6 us
    ppermute x15, waiting for transfers between devices, route(): return lax.ppermute(array, AXES, pairs)  11 us
    pallas_call x1, Pallas kernels, fast(): pl.pallas_call(functools.partial(work_kernel, n, pieces), in_specs=[VMEM]...  1.92 us
    pallas_call x1, Pallas kernels, fast(): pl.pallas_call(functools.partial(pack_kernel, n), in_specs=[pl.BlockSpec(...  1 us
    pallas_call x1, Pallas kernels, fast(): pl.pallas_call(functools.partial(fill_kernel, n, pieces), in_specs=[VMEM]...  0.8 us
  transfers between devices with their start and end apart: 15, of which 6 were waited for; matrix products, arithmetic and copies ran while one was open for 0% of the time, Pallas kernels for 3%

profile of v6, /device:TPU:0, one launch (start us, length us, event | category | flops | bytes accessed | tf_op | source)
XLA Modules:
  0.0 34.2 jit_solution(16802623589768302447)
XLA Ops:
  0.6 1.0 %shard_map.68.refs_0_ = f32[200,128]{1,0:T(8,128)S(1)} custom-call(f32[128,128]{1,0:T(8,128)} %bitcast.20, s32[2,16]{1,0:T(2,128)} %bitcast.22, f32[64,128]{1,0:T(8,128)} %bitcast.21, s32[1,2]{1,0:T(1,128)} %bitcast.23), custom_call_target="tpu_custom_call" | custom-call | tf_op jit(solution)/shard_map/pallas_call | solution.py:270
  1.6 3.1 %collective-permute-start = (f32[200,128]{1,0:T(8,128)S(1)}, f32[200,128]{1,0:T(8,128)S(1)}, u32[]{:S(2)}, u32[]{:S(2)}) collective-permute-start(f32[200,128]{1,0:T(8,128)S(1)} %shard_map.68.refs_0_), channel_id=1, source_target_pairs={{0,2},{1,3},{2,0},{3,1},{4,6},{5,7},{6,4},{7,5},{8,10},{9,11},{10,... | collective-permute-start | bytes 307208 | tf_op jit(solution)/shard_map/ppermute | solution.py:250
  4.7 2.5 %collective-permute-start.1 = (f32[200,128]{1,0:T(8,128)S(1)}, f32[200,128]{1,0:T(8,128)S(1)}, u32[]{:S(2)}, u32[]{:S(2)}) collective-permute-start(f32[200,128]{1,0:T(8,128)S(1)} %shard_map.68.refs_0_), channel_id=1, source_target_pairs={{0,6},{1,7},{2,4},{3,5},{4,2},{5,3},{6,0},{7,1},{8,14},{9,15},{10,... | collective-permute-start | bytes 307208 | tf_op jit(solution)/shard_map/ppermute | solution.py:250
  7.2 0.4 %collective-permute-done.refs_0_ = f32[200,128]{1,0:T(8,128)S(1)} collective-permute-done((f32[200,128]{1,0:T(8,128)S(1)}, f32[200,128]{1,0:T(8,128)S(1)}, u32[]{:S(2)}, u32[]{:S(2)}) %collective-permute-start) | collective-permute-done | bytes 102432 | tf_op jit(solution)/shard_map/ppermute | solution.py:250
  7.6 1.7 %collective-permute-start.10 = (f32[200,128]{1,0:T(8,128)S(1)}, f32[200,128]{1,0:T(8,128)S(1)}, u32[]{:S(2)}, u32[]{:S(2)}) collective-permute-start(f32[200,128]{1,0:T(8,128)S(1)} %shard_map.68.refs_0_), channel_id=1, source_target_pairs={{0,8},{1,17},{2,10},{3,19},{4,12},{5,21},{6,14},{7,23},{8,0},{9,25... | collective-permute-start | bytes 307208 | tf_op jit(solution)/shard_map/ppermute | solution.py:250
  9.3 2.7 %collective-permute-done.1.refs_1_ = f32[200,128]{1,0:T(8,128)S(1)} collective-permute-done((f32[200,128]{1,0:T(8,128)S(1)}, f32[200,128]{1,0:T(8,128)S(1)}, u32[]{:S(2)}, u32[]{:S(2)}) %collective-permute-start.1) | collective-permute-done | bytes 102432 | tf_op jit(solution)/shard_map/ppermute | solution.py:250
  12.0 0.6 %collective-permute-start.4 = (f32[200,128]{1,0:T(8,128)S(1)}, f32[200,128]{1,0:T(8,128)S(1)}, u32[]{:S(2)}, u32[]{:S(2)}) collective-permute-start(f32[200,128]{1,0:T(8,128)S(1)} %collective-permute-done.1.refs_1_), channel_id=1, source_target_pairs={{0,2},{1,3},{2,0},{3,1},{4,6},{5,7},{6,4},{7,5},{8,10},{9,11},{10,... | collective-permute-start | bytes 307208 | tf_op jit(solution)/shard_map/ppermute | solution.py:250
  12.7 1.5 %collective-permute-start.11 = (f32[200,128]{1,0:T(8,128)S(1)}, f32[200,128]{1,0:T(8,128)S(1)}, u32[]{:S(2)}, u32[]{:S(2)}) collective-permute-start(f32[200,128]{1,0:T(8,128)S(1)} %shard_map.68.refs_0_), channel_id=1, source_target_pairs={{0,16},{1,9},{2,18},{3,11},{4,20},{5,13},{6,22},{7,15},{8,24},{9,1... | collective-permute-start | bytes 307208 | tf_op jit(solution)/shard_map/ppermute | solution.py:250
  14.2 0.6 %collective-permute-start.3 = (f32[400,128]{1,0:T(8,128)S(1)}, f32[400,128]{1,0:T(8,128)S(1)}, u32[]{:S(2)}, u32[]{:S(2)}) collective-permute-start(f32[400,128]{1,0:T(8,128)S(1)} %shard_map.69.refs_4_), channel_id=1, source_target_pairs={{0,16},{1,9},{2,18},{3,11},{4,20},{5,13},{6,22},{7,15},{8,24},{9,1... | collective-permute-start | bytes 614408 | tf_op jit(solution)/shard_map/ppermute | solution.py:250
  14.8 1.5 %collective-permute-start.2 = (f32[400,128]{1,0:T(8,128)S(1)}, f32[400,128]{1,0:T(8,128)S(1)}, u32[]{:S(2)}, u32[]{:S(2)}) collective-permute-start(f32[400,128]{1,0:T(8,128)S(1)} %shard_map.69.refs_4_), channel_id=1, source_target_pairs={{0,8},{1,17},{2,10},{3,19},{4,12},{5,21},{6,14},{7,23},{8,0},{9,25... | collective-permute-start | bytes 614408 | tf_op jit(solution)/shard_map/ppermute | solution.py:250
  16.3 0.0 collective-permute-done.10.refs_1_
  16.3 1.5 %collective-permute-start.12 = (f32[200,128]{1,0:T(8,128)S(1)}, f32[200,128]{1,0:T(8,128)S(1)}, u32[]{:S(2)}, u32[]{:S(2)}) collective-permute-start(f32[200,128]{1,0:T(8,128)S(1)} %collective-permute-done.10.refs_1_), channel_id=1, source_target_pairs={{0,16},{1,9},{2,18},{3,11},{4,20},{5,13},{6,22},{7,15},{8,24},{9,1... | collective-permute-start | bytes 307208 | tf_op jit(solution)/shard_map/ppermute | solution.py:250
  17.8 0.0 collective-permute-done.4.refs_5_
  17.8 0.5 %collective-permute-start.6 = (f32[200,128]{1,0:T(8,128)S(1)}, f32[200,128]{1,0:T(8,128)S(1)}, u32[]{:S(2)}, u32[]{:S(2)}) collective-permute-start(f32[200,128]{1,0:T(8,128)S(1)} %collective-permute-done.4.refs_5_), channel_id=1, source_target_pairs={{0,16},{1,9},{2,18},{3,11},{4,20},{5,13},{6,22},{7,15},{8,24},{9,1... | collective-permute-start | bytes 307208 | tf_op jit(solution)/shard_map/ppermute | solution.py:250
  18.3 0.0 collective-permute-done.11.refs_2_
  18.3 1.7 %collective-permute-start.5 = (f32[200,128]{1,0:T(8,128)S(1)}, f32[200,128]{1,0:T(8,128)S(1)}, u32[]{:S(2)}, u32[]{:S(2)}) collective-permute-start(f32[200,128]{1,0:T(8,128)S(1)} %collective-permute-done.4.refs_5_), channel_id=1, source_target_pairs={{0,8},{1,17},{2,10},{3,19},{4,12},{5,21},{6,14},{7,23},{8,0},{9,25... | collective-permute-start | bytes 307208 | tf_op jit(solution)/shard_map/ppermute | solution.py:250
  20.0 2.5 %collective-permute-done.12.refs_3_ = f32[200,128]{1,0:T(8,128)S(1)} collective-permute-done((f32[200,128]{1,0:T(8,128)S(1)}, f32[200,128]{1,0:T(8,128)S(1)}, u32[]{:S(2)}, u32[]{:S(2)}) %collective-permute-start.12) | collective-permute-done | bytes 102432 | tf_op jit(solution)/shard_map/ppermute | solution.py:250
  22.5 0.1 collective-permute-start.13
  22.6 1.0 %collective-permute-done.6.s_far.refs_3_ = f32[200,128]{1,0:T(8,128)S(1)} collective-permute-done((f32[200,128]{1,0:T(8,128)S(1)}, f32[200,128]{1,0:T(8,128)S(1)}, u32[]{:S(2)}, u32[]{:S(2)}) %collective-permute-start.6) | collective-permute-done | bytes 102432 | tf_op jit(solution)/shard_map/ppermute | solution.py:250
  23.6 0.0 collective-permute-done.5.f_far.refs_2_
  23.6 0.0 collective-permute-done.3.s_outer.refs_1_
  23.6 0.0 collective-permute-done.2.f_outer.refs_0_
  23.6 0.1 collective-permute-start.14
  23.8 1.6 %collective-permute-start.7 = (f32[304,128]{1,0:T(8,128)S(1)}, f32[304,128]{1,0:T(8,128)S(1)}, u32[]{:S(2)}, u32[]{:S(2)}) collective-permute-start(f32[304,128]{1,0:T(8,128)S(1)} %get-tuple-element.23), channel_id=1, source_target_pairs={{0,16},{1,9},{2,18},{3,11},{4,20},{5,13},{6,22},{7,15},{8,24},{9,1... | collective-permute-start | bytes 466952 | tf_op jit(solution)/shard_map/ppermute | solution.py:250
  25.3 1.5 %collective-permute-start.8 = (f32[296,128]{1,0:T(8,128)S(1)}, f32[296,128]{1,0:T(8,128)S(1)}, u32[]{:S(2)}, u32[]{:S(2)}) collective-permute-start(f32[296,128]{1,0:T(8,128)S(1)} %get-tuple-element.24), channel_id=1, source_target_pairs={{0,8},{1,17},{2,10},{3,19},{4,12},{5,21},{6,14},{7,23},{8,0},{9,25... | collective-permute-start | bytes 454664 | tf_op jit(solution)/shard_map/ppermute | solution.py:250
  26.8 3.7 %collective-permute-done.8.refs_1_ = f32[296,128]{1,0:T(8,128)S(1)} collective-permute-done((f32[296,128]{1,0:T(8,128)S(1)}, f32[296,128]{1,0:T(8,128)S(1)}, u32[]{:S(2)}, u32[]{:S(2)}) %collective-permute-start.8) | collective-permute-done | bytes 151584 | tf_op jit(solution)/shard_map/ppermute | solution.py:250
  30.5 0.0 collective-permute-done.7.refs_0_
  30.6 0.0 copy-start
  30.6 0.2 collective-permute-start.9
  30.8 0.0 collective-permute-done.14.refs_3_
  30.8 0.0 collective-permute-done.13.refs_2_
  30.8 0.8 %shard_map.74 = (bf16[2,512,512]{2,1,0:T(8,128)(2,1)S(1)}, bf16[2,512,512]{2,1,0:T(8,128)(2,1)S(1)}, f32[1,512,128]{2,1,0:T(8,128)S(1)}, bf16[4,512,128]{2,1,0:T...) custom-call(f32[1400,128]{1,0:T(8,128)S(1)} %shard_map.72.refs_0_, ...), custom_call_target="tpu_custom_call" | custom-call | tf_op jit(solution)/shard_map/pallas_call | solution.py:327
  31.6 0.7 %collective-permute-done.9.theirs = f32[600,128]{1,0:T(8,128)S(1)} collective-permute-done((f32[600,128]{1,0:T(8,128)S(1)}, f32[600,128]{1,0:T(8,128)S(1)}, u32[]{:S(2)}, u32[]{:S(2)}) %collective-permute-start.9) | collective-permute-done | bytes 307232 | tf_op jit(solution)/shard_map/ppermute | solution.py:250
  32.2 0.0 copy-done
  32.2 1.9 %shard_map.75 = (f32[128,128]{1,0:T(8,128)}, f32[512,128]{1,0:T(8,128)}, bf16[2,512,512]{2,1,0:T(8,128)(2,1)S(1)}, bf16[2,512,512]{2,1,0:T(8,128)(2,1)S(1)}, f32...) custom-call(f32[600,128]{1,0:T(8,128)S(1)} %shard_map.71.mine, ...), custom_call_target="tpu_custom_call", output_to_operand_aliasing={{2}: (2, {}), {3}: (3, {}), {4}: (4, {}), {5}: (5, {}), {6}... | custom-call | tf_op jit(solution)/shard_map/pallas_call | solution.py:337
  (5 shorter events, 0.1 us)
Async XLA Ops:
  1.6 6.0 %collective-permute-start = (f32[200,128]{1,0:T(8,128)S(1)}, f32[200,128]{1,0:T(8,128)S(1)}, u32[]{:S(2)}, u32[]{:S(2)}) collective-permute-start(f32[200,128]{1,0:T(8,128)S(1)} %shard_map.68.refs_0_), channel_id=1, source_target_pairs={{0,2},{1,3},{2,0},{3,1},{4,6},{5,7},{6,4},{7,5},{8,10},{9,11},{10,... | collective-permute-start | bytes 307208 | tf_op jit(solution)/shard_map/ppermute | solution.py:250
  4.7 7.3 %collective-permute-start.1 = (f32[200,128]{1,0:T(8,128)S(1)}, f32[200,128]{1,0:T(8,128)S(1)}, u32[]{:S(2)}, u32[]{:S(2)}) collective-permute-start(f32[200,128]{1,0:T(8,128)S(1)} %shard_map.68.refs_0_), channel_id=1, source_target_pairs={{0,6},{1,7},{2,4},{3,5},{4,2},{5,3},{6,0},{7,1},{8,14},{9,15},{10,... | collective-permute-start | bytes 307208 | tf_op jit(solution)/shard_map/ppermute | solution.py:250
  7.6 8.7 %collective-permute-start.10 = (f32[200,128]{1,0:T(8,128)S(1)}, f32[200,128]{1,0:T(8,128)S(1)}, u32[]{:S(2)}, u32[]{:S(2)}) collective-permute-start(f32[200,128]{1,0:T(8,128)S(1)} %shard_map.68.refs_0_), channel_id=1, source_target_pairs={{0,8},{1,17},{2,10},{3,19},{4,12},{5,21},{6,14},{7,23},{8,0},{9,25... | collective-permute-start | bytes 307208 | tf_op jit(solution)/shard_map/ppermute | solution.py:250
  12.0 5.8 %collective-permute-start.4 = (f32[200,128]{1,0:T(8,128)S(1)}, f32[200,128]{1,0:T(8,128)S(1)}, u32[]{:S(2)}, u32[]{:S(2)}) collective-permute-start(f32[200,128]{1,0:T(8,128)S(1)} %collective-permute-done.1.refs_1_), channel_id=1, source_target_pairs={{0,2},{1,3},{2,0},{3,1},{4,6},{5,7},{6,4},{7,5},{8,10},{9,11},{10,... | collective-permute-start | bytes 307208 | tf_op jit(solution)/shard_map/ppermute | solution.py:250
  12.7 5.6 %collective-permute-start.11 = (f32[200,128]{1,0:T(8,128)S(1)}, f32[200,128]{1,0:T(8,128)S(1)}, u32[]{:S(2)}, u32[]{:S(2)}) collective-permute-start(f32[200,128]{1,0:T(8,128)S(1)} %shard_map.68.refs_0_), channel_id=1, source_target_pairs={{0,16},{1,9},{2,18},{3,11},{4,20},{5,13},{6,22},{7,15},{8,24},{9,1... | collective-permute-start | bytes 307208 | tf_op jit(solution)/shard_map/ppermute | solution.py:250
  14.2 9.4 %collective-permute-start.3 = (f32[400,128]{1,0:T(8,128)S(1)}, f32[400,128]{1,0:T(8,128)S(1)}, u32[]{:S(2)}, u32[]{:S(2)}) collective-permute-start(f32[400,128]{1,0:T(8,128)S(1)} %shard_map.69.refs_4_), channel_id=1, source_target_pairs={{0,16},{1,9},{2,18},{3,11},{4,20},{5,13},{6,22},{7,15},{8,24},{9,1... | collective-permute-start | bytes 614408 | tf_op jit(solution)/shard_map/ppermute | solution.py:250
  14.8 8.8 %collective-permute-start.2 = (f32[400,128]{1,0:T(8,128)S(1)}, f32[400,128]{1,0:T(8,128)S(1)}, u32[]{:S(2)}, u32[]{:S(2)}) collective-permute-start(f32[400,128]{1,0:T(8,128)S(1)} %shard_map.69.refs_4_), channel_id=1, source_target_pairs={{0,8},{1,17},{2,10},{3,19},{4,12},{5,21},{6,14},{7,23},{8,0},{9,25... | collective-permute-start | bytes 614408 | tf_op jit(solution)/shard_map/ppermute | solution.py:250
  16.3 6.2 %collective-permute-start.12 = (f32[200,128]{1,0:T(8,128)S(1)}, f32[200,128]{1,0:T(8,128)S(1)}, u32[]{:S(2)}, u32[]{:S(2)}) collective-permute-start(f32[200,128]{1,0:T(8,128)S(1)} %collective-permute-done.10.refs_1_), channel_id=1, source_target_pairs={{0,16},{1,9},{2,18},{3,11},{4,20},{5,13},{6,22},{7,15},{8,24},{9,1... | collective-permute-start | bytes 307208 | tf_op jit(solution)/shard_map/ppermute | solution.py:250
  17.8 5.8 %collective-permute-start.6 = (f32[200,128]{1,0:T(8,128)S(1)}, f32[200,128]{1,0:T(8,128)S(1)}, u32[]{:S(2)}, u32[]{:S(2)}) collective-permute-start(f32[200,128]{1,0:T(8,128)S(1)} %collective-permute-done.4.refs_5_), channel_id=1, source_target_pairs={{0,16},{1,9},{2,18},{3,11},{4,20},{5,13},{6,22},{7,15},{8,24},{9,1... | collective-permute-start | bytes 307208 | tf_op jit(solution)/shard_map/ppermute | solution.py:250
  18.3 5.3 %collective-permute-start.5 = (f32[200,128]{1,0:T(8,128)S(1)}, f32[200,128]{1,0:T(8,128)S(1)}, u32[]{:S(2)}, u32[]{:S(2)}) collective-permute-start(f32[200,128]{1,0:T(8,128)S(1)} %collective-permute-done.4.refs_5_), channel_id=1, source_target_pairs={{0,8},{1,17},{2,10},{3,19},{4,12},{5,21},{6,14},{7,23},{8,0},{9,25... | collective-permute-start | bytes 307208 | tf_op jit(solution)/shard_map/ppermute | solution.py:250
  22.5 8.2 %collective-permute-start.13 = (f32[1400,128]{1,0:T(8,128)S(1)}, f32[1400,128]{1,0:T(8,128)S(1)}, u32[]{:S(2)}, u32[]{:S(2)}) collective-permute-start(f32[1400,128]{1,0:T(8,128)S(1)} %shard_map.72.refs_0_), channel_id=1, source_target_pairs={{0,1},{1,0},{2,3},{3,2},{4,5},{5,4},{6,7},{7,6},{8,9},{9,8},{10,11... | collective-permute-start | bytes 2150408 | tf_op jit(solution)/shard_map/ppermute | solution.py:250
  23.6 7.1 %collective-permute-start.14 = (f32[1200,128]{1,0:T(8,128)S(1)}, f32[1200,128]{1,0:T(8,128)S(1)}, u32[]{:S(2)}, u32[]{:S(2)}) collective-permute-start(f32[1200,128]{1,0:T(8,128)S(1)} %shard_map.73.refs_1_), channel_id=1, source_target_pairs={{0,1},{1,0},{2,3},{3,2},{4,5},{5,4},{6,7},{7,6},{8,9},{9,8},{10,11... | collective-permute-start | bytes 1843208 | tf_op jit(solution)/shard_map/ppermute | solution.py:250
  23.8 6.8 %collective-permute-start.7 = (f32[304,128]{1,0:T(8,128)S(1)}, f32[304,128]{1,0:T(8,128)S(1)}, u32[]{:S(2)}, u32[]{:S(2)}) collective-permute-start(f32[304,128]{1,0:T(8,128)S(1)} %get-tuple-element.23), channel_id=1, source_target_pairs={{0,16},{1,9},{2,18},{3,11},{4,20},{5,13},{6,22},{7,15},{8,24},{9,1... | collective-permute-start | bytes 466952 | tf_op jit(solution)/shard_map/ppermute | solution.py:250
  25.3 5.2 %collective-permute-start.8 = (f32[296,128]{1,0:T(8,128)S(1)}, f32[296,128]{1,0:T(8,128)S(1)}, u32[]{:S(2)}, u32[]{:S(2)}) collective-permute-start(f32[296,128]{1,0:T(8,128)S(1)} %get-tuple-element.24), channel_id=1, source_target_pairs={{0,8},{1,17},{2,10},{3,19},{4,12},{5,21},{6,14},{7,23},{8,0},{9,25... | collective-permute-start | bytes 454664 | tf_op jit(solution)/shard_map/ppermute | solution.py:250
  30.6 1.7 %copy-start = (f32[64,2,512]{2,1,0:T(2,128)S(1)}, f32[64,2,512]{2,1,0:T(2,128)}, u32[]{:S(2)}) copy-start(f32[64,2,512]{2,1,0:T(2,128)} %param.9) | copy-start | bytes 786436
  30.6 1.7 %collective-permute-start.9 = (f32[600,128]{1,0:T(8,128)S(1)}, f32[600,128]{1,0:T(8,128)S(1)}, u32[]{:S(2)}, u32[]{:S(2)}) collective-permute-start(f32[600,128]{1,0:T(8,128)S(1)} %shard_map.71.mine), channel_id=1, source_target_pairs={{0,1},{1,0},{2,3},{3,2},{4,5},{5,4},{6,7},{7,6},{8,9},{9,8},{10,11... | collective-permute-start | bytes 921608 | tf_op jit(solution)/shard_map/ppermute | solution.py:250

commit v7 on v5

--- a/solution.py
+++ b/solution.py
@@ -298,7 +298,7 @@
     outer = join(z1, z3)
     trip = [over_pair(outer, 0), over_pair(outer, 1), over_pair(z2, 0), over_pair(z2, 1)]
     trip = lax.optimization_barrier(trip)
-    low = (n.bulk // 2 + 7) // 8 * 8
+    low = n.bulk * 5 // 6 // 8 * 8
     out = [shape(n.bulk + low, LANES), shape(2 * n.bulk - low, LANES)]
     ends = pl.pallas_call(
         functools.partial(cut_kernel, n, low),

time: 34.1 us -> 34.4 us (level)
  waiting for transfers between devices: 8.06 us -> 8.53 us
    ppermute x15, waiting for transfers between devices: 8.06 us -> 8.53 us  [route(): return lax.ppermute(array, AXES, pairs)]
  transfers between devices with their start and end apart: 15 -> 15, of which waited for: 5 -> 6; matrix products, arithmetic and copies ran while one was open for 0% -> 0% of each run, Pallas kernels for 3% -> 3%
where the time goes in v7:
time: 34.4 us; the launch traced here: 34.3 us
  starting transfers between devices  21.1 us (61%)
  waiting for transfers between devices  8.53 us (25%)
  Pallas kernels  3.87 us (11%)
  between operations  0.73 us (2%)
    ppermute x15, starting transfers between devices, route(): return lax.ppermute(array, AXES, pairs)  21.1 us
    ppermute x15, waiting for transfers between devices, route(): return lax.ppermute(array, AXES, pairs)  8.53 us
    pallas_call x1, Pallas kernels, fast(): pl.pallas_call(functools.partial(work_kernel, n, pieces), in_specs=[VMEM]...  1.92 us
    pallas_call x1, Pallas kernels, fast(): pl.pallas_call(functools.partial(pack_kernel, n), in_specs=[pl.BlockSpec(...  1 us
    pallas_call x1, Pallas kernels, fast(): pl.pallas_call(functools.partial(fill_kernel, n, pieces), in_specs=[VMEM]...  0.8 us
  transfers between devices with their start and end apart: 15, of which 6 were waited for; matrix products, arithmetic and copies ran while one was open for 0% of the time, Pallas kernels for 3%

profile of v7, /device:TPU:0, one launch (start us, length us, event | category | flops | bytes accessed | tf_op | source)
XLA Modules:
  0.0 34.3 jit_solution(917366691228164192)
XLA Ops:
  0.6 1.0 %shard_map.68.refs_0_ = f32[200,128]{1,0:T(8,128)S(1)} custom-call(f32[128,128]{1,0:T(8,128)} %bitcast.20, s32[2,16]{1,0:T(2,128)} %bitcast.22, f32[64,128]{1,0:T(8,128)} %bitcast.21, s32[1,2]{1,0:T(1,128)} %bitcast.23), custom_call_target="tpu_custom_call" | custom-call | tf_op jit(solution)/shard_map/pallas_call | solution.py:270
  1.6 3.1 %collective-permute-start = (f32[200,128]{1,0:T(8,128)S(1)}, f32[200,128]{1,0:T(8,128)S(1)}, u32[]{:S(2)}, u32[]{:S(2)}) collective-permute-start(f32[200,128]{1,0:T(8,128)S(1)} %shard_map.68.refs_0_), channel_id=1, source_target_pairs={{0,2},{1,3},{2,0},{3,1},{4,6},{5,7},{6,4},{7,5},{8,10},{9,11},{10,... | collective-permute-start | bytes 307208 | tf_op jit(solution)/shard_map/ppermute | solution.py:250
  4.7 2.5 %collective-permute-start.1 = (f32[200,128]{1,0:T(8,128)S(1)}, f32[200,128]{1,0:T(8,128)S(1)}, u32[]{:S(2)}, u32[]{:S(2)}) collective-permute-start(f32[200,128]{1,0:T(8,128)S(1)} %shard_map.68.refs_0_), channel_id=1, source_target_pairs={{0,6},{1,7},{2,4},{3,5},{4,2},{5,3},{6,0},{7,1},{8,14},{9,15},{10,... | collective-permute-start | bytes 307208 | tf_op jit(solution)/shard_map/ppermute | solution.py:250
  7.2 0.4 %collective-permute-done.refs_0_ = f32[200,128]{1,0:T(8,128)S(1)} collective-permute-done((f32[200,128]{1,0:T(8,128)S(1)}, f32[200,128]{1,0:T(8,128)S(1)}, u32[]{:S(2)}, u32[]{:S(2)}) %collective-permute-start) | collective-permute-done | bytes 102432 | tf_op jit(solution)/shard_map/ppermute | solution.py:250
  7.6 1.7 %collective-permute-start.10 = (f32[200,128]{1,0:T(8,128)S(1)}, f32[200,128]{1,0:T(8,128)S(1)}, u32[]{:S(2)}, u32[]{:S(2)}) collective-permute-start(f32[200,128]{1,0:T(8,128)S(1)} %shard_map.68.refs_0_), channel_id=1, source_target_pairs={{0,8},{1,17},{2,10},{3,19},{4,12},{5,21},{6,14},{7,23},{8,0},{9,25... | collective-permute-start | bytes 307208 | tf_op jit(solution)/shard_map/ppermute | solution.py:250
  9.3 1.5 %collective-permute-start.11 = (f32[200,128]{1,0:T(8,128)S(1)}, f32[200,128]{1,0:T(8,128)S(1)}, u32[]{:S(2)}, u32[]{:S(2)}) collective-permute-start(f32[200,128]{1,0:T(8,128)S(1)} %shard_map.68.refs_0_), channel_id=1, source_target_pairs={{0,16},{1,9},{2,18},{3,11},{4,20},{5,13},{6,22},{7,15},{8,24},{9,1... | collective-permute-start | bytes 307208 | tf_op jit(solution)/shard_map/ppermute | solution.py:250
  10.8 4.7 %collective-permute-start.4 = (f32[200,128]{1,0:T(8,128)S(1)}, f32[200,128]{1,0:T(8,128)S(1)}, u32[]{:S(2)}, u32[]{:S(2)}) collective-permute-start(f32[200,128]{1,0:T(8,128)S(1)} %collective-permute-done.refs_0_), channel_id=1, source_target_pairs={{0,6},{1,7},{2,4},{3,5},{4,2},{5,3},{6,0},{7,1},{8,14},{9,15},{10,... | collective-permute-start | bytes 307208 | tf_op jit(solution)/shard_map/ppermute | solution.py:250
  15.5 0.0 collective-permute-done.1.refs_1_
  15.5 0.6 %collective-permute-start.3 = (f32[400,128]{1,0:T(8,128)S(1)}, f32[400,128]{1,0:T(8,128)S(1)}, u32[]{:S(2)}, u32[]{:S(2)}) collective-permute-start(f32[400,128]{1,0:T(8,128)S(1)} %shard_map.69.refs_4_), channel_id=1, source_target_pairs={{0,16},{1,9},{2,18},{3,11},{4,20},{5,13},{6,22},{7,15},{8,24},{9,1... | collective-permute-start | bytes 614408 | tf_op jit(solution)/shard_map/ppermute | solution.py:250
  16.1 0.5 %collective-permute-start.2 = (f32[400,128]{1,0:T(8,128)S(1)}, f32[400,128]{1,0:T(8,128)S(1)}, u32[]{:S(2)}, u32[]{:S(2)}) collective-permute-start(f32[400,128]{1,0:T(8,128)S(1)} %shard_map.69.refs_4_), channel_id=1, source_target_pairs={{0,8},{1,17},{2,10},{3,19},{4,12},{5,21},{6,14},{7,23},{8,0},{9,25... | collective-permute-start | bytes 614408 | tf_op jit(solution)/shard_map/ppermute | solution.py:250
  16.6 0.0 collective-permute-done.10.refs_1_
  16.7 1.5 %collective-permute-start.12 = (f32[200,128]{1,0:T(8,128)S(1)}, f32[200,128]{1,0:T(8,128)S(1)}, u32[]{:S(2)}, u32[]{:S(2)}) collective-permute-start(f32[200,128]{1,0:T(8,128)S(1)} %collective-permute-done.10.refs_1_), channel_id=1, source_target_pairs={{0,16},{1,9},{2,18},{3,11},{4,20},{5,13},{6,22},{7,15},{8,24},{9,1... | collective-permute-start | bytes 307208 | tf_op jit(solution)/shard_map/ppermute | solution.py:250
  18.2 0.0 collective-permute-done.4.refs_5_
  18.2 0.5 %collective-permute-start.6 = (f32[200,128]{1,0:T(8,128)S(1)}, f32[200,128]{1,0:T(8,128)S(1)}, u32[]{:S(2)}, u32[]{:S(2)}) collective-permute-start(f32[200,128]{1,0:T(8,128)S(1)} %collective-permute-done.4.refs_5_), channel_id=1, source_target_pairs={{0,16},{1,9},{2,18},{3,11},{4,20},{5,13},{6,22},{7,15},{8,24},{9,1... | collective-permute-start | bytes 307208 | tf_op jit(solution)/shard_map/ppermute | solution.py:250
  18.7 0.0 collective-permute-done.11.refs_2_
  18.7 1.5 %collective-permute-start.5 = (f32[200,128]{1,0:T(8,128)S(1)}, f32[200,128]{1,0:T(8,128)S(1)}, u32[]{:S(2)}, u32[]{:S(2)}) collective-permute-start(f32[200,128]{1,0:T(8,128)S(1)} %collective-permute-done.4.refs_5_), channel_id=1, source_target_pairs={{0,8},{1,17},{2,10},{3,19},{4,12},{5,21},{6,14},{7,23},{8,0},{9,25... | collective-permute-start | bytes 307208 | tf_op jit(solution)/shard_map/ppermute | solution.py:250
  20.2 2.3 %collective-permute-done.12.refs_3_ = f32[200,128]{1,0:T(8,128)S(1)} collective-permute-done((f32[200,128]{1,0:T(8,128)S(1)}, f32[200,128]{1,0:T(8,128)S(1)}, u32[]{:S(2)}, u32[]{:S(2)}) %collective-permute-start.12) | collective-permute-done | bytes 102432 | tf_op jit(solution)/shard_map/ppermute | solution.py:250
  22.5 0.1 collective-permute-start.13
  22.6 1.0 %collective-permute-done.6.s_far.refs_3_ = f32[200,128]{1,0:T(8,128)S(1)} collective-permute-done((f32[200,128]{1,0:T(8,128)S(1)}, f32[200,128]{1,0:T(8,128)S(1)}, u32[]{:S(2)}, u32[]{:S(2)}) %collective-permute-start.6) | collective-permute-done | bytes 102432 | tf_op jit(solution)/shard_map/ppermute | solution.py:250
  23.6 0.0 collective-permute-done.5.f_far.refs_2_
  23.6 0.0 collective-permute-done.3.s_outer.refs_1_
  23.6 0.0 collective-permute-done.2.f_outer.refs_0_
  23.6 0.1 collective-permute-start.14
  23.7 1.4 %collective-permute-start.7 = (f32[360,128]{1,0:T(8,128)S(1)}, f32[360,128]{1,0:T(8,128)S(1)}, u32[]{:S(2)}, u32[]{:S(2)}) collective-permute-start(f32[360,128]{1,0:T(8,128)S(1)} %get-tuple-element.23), channel_id=1, source_target_pairs={{0,16},{1,9},{2,18},{3,11},{4,20},{5,13},{6,22},{7,15},{8,24},{9,1... | collective-permute-start | bytes 552968 | tf_op jit(solution)/shard_map/ppermute | solution.py:250
  25.1 1.5 %collective-permute-start.8 = (f32[240,128]{1,0:T(8,128)S(1)}, f32[240,128]{1,0:T(8,128)S(1)}, u32[]{:S(2)}, u32[]{:S(2)}) collective-permute-start(f32[240,128]{1,0:T(8,128)S(1)} %get-tuple-element.24), channel_id=1, source_target_pairs={{0,8},{1,17},{2,10},{3,19},{4,12},{5,21},{6,14},{7,23},{8,0},{9,25... | collective-permute-start | bytes 368648 | tf_op jit(solution)/shard_map/ppermute | solution.py:250
  26.6 3.6 %collective-permute-done.8.refs_1_ = f32[240,128]{1,0:T(8,128)S(1)} collective-permute-done((f32[240,128]{1,0:T(8,128)S(1)}, f32[240,128]{1,0:T(8,128)S(1)}, u32[]{:S(2)}, u32[]{:S(2)}) %collective-permute-start.8) | collective-permute-done | bytes 122912 | tf_op jit(solution)/shard_map/ppermute | solution.py:250
  30.2 0.5 %collective-permute-done.7.refs_0_ = f32[360,128]{1,0:T(8,128)S(1)} collective-permute-done((f32[360,128]{1,0:T(8,128)S(1)}, f32[360,128]{1,0:T(8,128)S(1)}, u32[]{:S(2)}, u32[]{:S(2)}) %collective-permute-start.7) | collective-permute-done | bytes 184352 | tf_op jit(solution)/shard_map/ppermute | solution.py:250
  30.7 0.0 copy-start
  30.7 0.1 collective-permute-start.9
  30.8 0.0 collective-permute-done.14.refs_3_
  30.8 0.0 collective-permute-done.13.refs_2_
  30.8 0.8 %shard_map.74 = (bf16[2,512,512]{2,1,0:T(8,128)(2,1)S(1)}, bf16[2,512,512]{2,1,0:T(8,128)(2,1)S(1)}, f32[1,512,128]{2,1,0:T(8,128)S(1)}, bf16[4,512,128]{2,1,0:T...) custom-call(f32[1400,128]{1,0:T(8,128)S(1)} %shard_map.72.refs_0_, ...), custom_call_target="tpu_custom_call" | custom-call | tf_op jit(solution)/shard_map/pallas_call | solution.py:327
  31.6 0.8 %collective-permute-done.9.theirs = f32[600,128]{1,0:T(8,128)S(1)} collective-permute-done((f32[600,128]{1,0:T(8,128)S(1)}, f32[600,128]{1,0:T(8,128)S(1)}, u32[]{:S(2)}, u32[]{:S(2)}) %collective-permute-start.9) | collective-permute-done | bytes 307232 | tf_op jit(solution)/shard_map/ppermute | solution.py:250
  32.4 0.0 copy-done
  32.4 1.9 %shard_map.75 = (f32[128,128]{1,0:T(8,128)}, f32[512,128]{1,0:T(8,128)}, bf16[2,512,512]{2,1,0:T(8,128)(2,1)S(1)}, bf16[2,512,512]{2,1,0:T(8,128)(2,1)S(1)}, f32...) custom-call(f32[600,128]{1,0:T(8,128)S(1)} %shard_map.71.mine, ...), custom_call_target="tpu_custom_call", output_to_operand_aliasing={{2}: (2, {}), {3}: (3, {}), {4}: (4, {}), {5}: (5, {}), {6}... | custom-call | tf_op jit(solution)/shard_map/pallas_call | solution.py:337
  (5 shorter events, 0.1 us)
Async XLA Ops:
  1.6 6.0 %collective-permute-start = (f32[200,128]{1,0:T(8,128)S(1)}, f32[200,128]{1,0:T(8,128)S(1)}, u32[]{:S(2)}, u32[]{:S(2)}) collective-permute-start(f32[200,128]{1,0:T(8,128)S(1)} %shard_map.68.refs_0_), channel_id=1, source_target_pairs={{0,2},{1,3},{2,0},{3,1},{4,6},{5,7},{6,4},{7,5},{8,10},{9,11},{10,... | collective-permute-start | bytes 307208 | tf_op jit(solution)/shard_map/ppermute | solution.py:250
  4.7 10.8 %collective-permute-start.1 = (f32[200,128]{1,0:T(8,128)S(1)}, f32[200,128]{1,0:T(8,128)S(1)}, u32[]{:S(2)}, u32[]{:S(2)}) collective-permute-start(f32[200,128]{1,0:T(8,128)S(1)} %shard_map.68.refs_0_), channel_id=1, source_target_pairs={{0,6},{1,7},{2,4},{3,5},{4,2},{5,3},{6,0},{7,1},{8,14},{9,15},{10,... | collective-permute-start | bytes 307208 | tf_op jit(solution)/shard_map/ppermute | solution.py:250
  7.6 9.0 %collective-permute-start.10 = (f32[200,128]{1,0:T(8,128)S(1)}, f32[200,128]{1,0:T(8,128)S(1)}, u32[]{:S(2)}, u32[]{:S(2)}) collective-permute-start(f32[200,128]{1,0:T(8,128)S(1)} %shard_map.68.refs_0_), channel_id=1, source_target_pairs={{0,8},{1,17},{2,10},{3,19},{4,12},{5,21},{6,14},{7,23},{8,0},{9,25... | collective-permute-start | bytes 307208 | tf_op jit(solution)/shard_map/ppermute | solution.py:250
  9.3 9.4 %collective-permute-start.11 = (f32[200,128]{1,0:T(8,128)S(1)}, f32[200,128]{1,0:T(8,128)S(1)}, u32[]{:S(2)}, u32[]{:S(2)}) collective-permute-start(f32[200,128]{1,0:T(8,128)S(1)} %shard_map.68.refs_0_), channel_id=1, source_target_pairs={{0,16},{1,9},{2,18},{3,11},{4,20},{5,13},{6,22},{7,15},{8,24},{9,1... | collective-permute-start | bytes 307208 | tf_op jit(solution)/shard_map/ppermute | solution.py:250
  10.8 7.4 %collective-permute-start.4 = (f32[200,128]{1,0:T(8,128)S(1)}, f32[200,128]{1,0:T(8,128)S(1)}, u32[]{:S(2)}, u32[]{:S(2)}) collective-permute-start(f32[200,128]{1,0:T(8,128)S(1)} %collective-permute-done.refs_0_), channel_id=1, source_target_pairs={{0,6},{1,7},{2,4},{3,5},{4,2},{5,3},{6,0},{7,1},{8,14},{9,15},{10,... | collective-permute-start | bytes 307208 | tf_op jit(solution)/shard_map/ppermute | solution.py:250
  15.5 8.0 %collective-permute-start.3 = (f32[400,128]{1,0:T(8,128)S(1)}, f32[400,128]{1,0:T(8,128)S(1)}, u32[]{:S(2)}, u32[]{:S(2)}) collective-permute-start(f32[400,128]{1,0:T(8,128)S(1)} %shard_map.69.refs_4_), channel_id=1, source_target_pairs={{0,16},{1,9},{2,18},{3,11},{4,20},{5,13},{6,22},{7,15},{8,24},{9,1... | collective-permute-start | bytes 614408 | tf_op jit(solution)/shard_map/ppermute | solution.py:250
  16.1 7.5 %collective-permute-start.2 = (f32[400,128]{1,0:T(8,128)S(1)}, f32[400,128]{1,0:T(8,128)S(1)}, u32[]{:S(2)}, u32[]{:S(2)}) collective-permute-start(f32[400,128]{1,0:T(8,128)S(1)} %shard_map.69.refs_4_), channel_id=1, source_target_pairs={{0,8},{1,17},{2,10},{3,19},{4,12},{5,21},{6,14},{7,23},{8,0},{9,25... | collective-permute-start | bytes 614408 | tf_op jit(solution)/shard_map/ppermute | solution.py:250
  16.7 5.8 %collective-permute-start.12 = (f32[200,128]{1,0:T(8,128)S(1)}, f32[200,128]{1,0:T(8,128)S(1)}, u32[]{:S(2)}, u32[]{:S(2)}) collective-permute-start(f32[200,128]{1,0:T(8,128)S(1)} %collective-permute-done.10.refs_1_), channel_id=1, source_target_pairs={{0,16},{1,9},{2,18},{3,11},{4,20},{5,13},{6,22},{7,15},{8,24},{9,1... | collective-permute-start | bytes 307208 | tf_op jit(solution)/shard_map/ppermute | solution.py:250
  18.2 5.4 %collective-permute-start.6 = (f32[200,128]{1,0:T(8,128)S(1)}, f32[200,128]{1,0:T(8,128)S(1)}, u32[]{:S(2)}, u32[]{:S(2)}) collective-permute-start(f32[200,128]{1,0:T(8,128)S(1)} %collective-permute-done.4.refs_5_), channel_id=1, source_target_pairs={{0,16},{1,9},{2,18},{3,11},{4,20},{5,13},{6,22},{7,15},{8,24},{9,1... | collective-permute-start | bytes 307208 | tf_op jit(solution)/shard_map/ppermute | solution.py:250
  18.7 4.8 %collective-permute-start.5 = (f32[200,128]{1,0:T(8,128)S(1)}, f32[200,128]{1,0:T(8,128)S(1)}, u32[]{:S(2)}, u32[]{:S(2)}) collective-permute-start(f32[200,128]{1,0:T(8,128)S(1)} %collective-permute-done.4.refs_5_), channel_id=1, source_target_pairs={{0,8},{1,17},{2,10},{3,19},{4,12},{5,21},{6,14},{7,23},{8,0},{9,25... | collective-permute-start | bytes 307208 | tf_op jit(solution)/shard_map/ppermute | solution.py:250
  22.5 8.3 %collective-permute-start.13 = (f32[1400,128]{1,0:T(8,128)S(1)}, f32[1400,128]{1,0:T(8,128)S(1)}, u32[]{:S(2)}, u32[]{:S(2)}) collective-permute-start(f32[1400,128]{1,0:T(8,128)S(1)} %shard_map.72.refs_0_), channel_id=1, source_target_pairs={{0,1},{1,0},{2,3},{3,2},{4,5},{5,4},{6,7},{7,6},{8,9},{9,8},{10,11... | collective-permute-start | bytes 2150408 | tf_op jit(solution)/shard_map/ppermute | solution.py:250
  23.6 7.1 %collective-permute-start.14 = (f32[1200,128]{1,0:T(8,128)S(1)}, f32[1200,128]{1,0:T(8,128)S(1)}, u32[]{:S(2)}, u32[]{:S(2)}) collective-permute-start(f32[1200,128]{1,0:T(8,128)S(1)} %shard_map.73.refs_1_), channel_id=1, source_target_pairs={{0,1},{1,0},{2,3},{3,2},{4,5},{5,4},{6,7},{7,6},{8,9},{9,8},{10,11... | collective-permute-start | bytes 1843208 | tf_op jit(solution)/shard_map/ppermute | solution.py:250
  23.7 6.9 %collective-permute-start.7 = (f32[360,128]{1,0:T(8,128)S(1)}, f32[360,128]{1,0:T(8,128)S(1)}, u32[]{:S(2)}, u32[]{:S(2)}) collective-permute-start(f32[360,128]{1,0:T(8,128)S(1)} %get-tuple-element.23), channel_id=1, source_target_pairs={{0,16},{1,9},{2,18},{3,11},{4,20},{5,13},{6,22},{7,15},{8,24},{9,1... | collective-permute-start | bytes 552968 | tf_op jit(solution)/shard_map/ppermute | solution.py:250
  25.1 5.0 %collective-permute-start.8 = (f32[240,128]{1,0:T(8,128)S(1)}, f32[240,128]{1,0:T(8,128)S(1)}, u32[]{:S(2)}, u32[]{:S(2)}) collective-permute-start(f32[240,128]{1,0:T(8,128)S(1)} %get-tuple-element.24), channel_id=1, source_target_pairs={{0,8},{1,17},{2,10},{3,19},{4,12},{5,21},{6,14},{7,23},{8,0},{9,25... | collective-permute-start | bytes 368648 | tf_op jit(solution)/shard_map/ppermute | solution.py:250
  30.7 1.7 %copy-start = (f32[64,2,512]{2,1,0:T(2,128)S(1)}, f32[64,2,512]{2,1,0:T(2,128)}, u32[]{:S(2)}) copy-start(f32[64,2,512]{2,1,0:T(2,128)} %param.9) | copy-start | bytes 786436
  30.7 1.7 %collective-permute-start.9 = (f32[600,128]{1,0:T(8,128)S(1)}, f32[600,128]{1,0:T(8,128)S(1)}, u32[]{:S(2)}, u32[]{:S(2)}) collective-permute-start(f32[600,128]{1,0:T(8,128)S(1)} %shard_map.71.mine), channel_id=1, source_target_pairs={{0,1},{1,0},{2,3},{3,2},{4,5},{5,4},{6,7},{7,6},{8,9},{9,8},{10,11... | collective-permute-start | bytes 921608 | tf_op jit(solution)/shard_map/ppermute | solution.py:250
